TPU v7x, 128 devices: a whole 4x4x4 slice. The times are simulated.
128 devices in a mesh: batch: 128 (over y, z, x, core).
Axes of the slice: x: 4, y: 4, z: 4, core: 2. Of those that a mesh axis runs over, the one named last changes fastest.
Arguments:
- encoder_output_matrix: bfloat16 [98304, 1024], P('batch'), may hold values from -24 to 24
- mapping_head_matrix: bfloat16 [1024, 1024], replicated, may hold values from -0.1875 to 0.1875
- duplicate_group_label: int32 [98304], P('batch'), may hold values from 0 to 49151, as said below
- score_scale_parameter: float32 [1], replicated, may hold values from 20 to 40
- score_shift_term: float32 [1], replicated, may hold values from -8 to -6
Outputs:
- loss: float32 [], replicated
- grad_rows: bfloat16 [98304, 1024], P('batch')
- grad_head: float32 [1024, 1024], P('batch')
Inputs may be any that keep to these rules, and one draw needn't show every extreme that they name: `duplicate_group_label`: rows with equal ids are near-duplicates; ids are more crowded in later blocks.
All inputs are finite; a program needn't handle non-finite values.
Results may differ from a plain program's by a relative error of at most 0.0052.
Values may be sent and summed in bfloat16 or wider, within the bound.
No kernel may reach another device: no remote copies, remote signals or barrier semaphores. Data moves between devices by JAX's collectives and lax.ppermute only.
A program may use at most 128 MiB of HBM per device.

v0:
```python
import jax
import jax.numpy as jnp
from jax import lax
from jax.sharding import PartitionSpec as P


def shifted(value, axis, steps):
    count = lax.axis_size(axis)
    pairs = [(source, (source + steps) % count) for source in range(count)]
    return lax.ppermute(value, axis, pairs)


def tile_terms(rows_emb, row_ids, column_embedding_vectors, col_ids, score_scaling_factor, offset):
    cosine = lax.dot_general(
        rows_emb,
        column_embedding_vectors,
        (((1,), (1,)), ((), ())),
        preferred_element_type=jnp.float32,
    )
    logits = score_scaling_factor * cosine + offset
    target = jnp.where(row_ids[:, None] == col_ids[None, :], 1.0, -1.0).astype(jnp.float32)
    logit_offset = target * logits
    running = jnp.sum(jax.nn.softplus(-logit_offset))
    slopes = (-target * jax.nn.sigmoid(-logit_offset)).astype(jnp.bfloat16)
    return (running, slopes)


def transposed(slopes, emb):
    return lax.dot_general(
        slopes, emb, (((0,), (0,)), ((), ())), preferred_element_type=jnp.float32
    )


def on_device(
    encoder_output_matrix,
    mapping_head_matrix,
    duplicate_group_label,
    score_scale_parameter,
    score_shift_term,
):
    score_scaling_factor = score_scale_parameter[0]
    offset = score_shift_term[0]
    projected_rows = jnp.dot(
        encoder_output_matrix, mapping_head_matrix, preferred_element_type=jnp.float32
    )
    inverse = lax.rsqrt(
        mapping_head_matrix.shape[1]
        * (jnp.mean(projected_rows * projected_rows, axis=1, keepdims=True) + 1e-06)
    )
    unit_rows = projected_rows * inverse
    unit_half = unit_rows.astype(jnp.bfloat16)
    nearer = shifted((unit_half, duplicate_group_label), "batch", 1)
    farther = shifted((unit_half, duplicate_group_label), "batch", 2)
    running, slopes = tile_terms(
        unit_half,
        duplicate_group_label,
        unit_half,
        duplicate_group_label,
        score_scaling_factor,
        offset,
    )
    summed = jnp.dot(slopes, unit_half, preferred_element_type=jnp.float32) + transposed(
        slopes, unit_half
    )
    returned = []
    for partner in (nearer, farther):
        piece, slopes = tile_terms(
            unit_half, duplicate_group_label, partner[0], partner[1], score_scaling_factor, offset
        )
        running = running + piece
        summed = summed + jnp.dot(slopes, partner[0], preferred_element_type=jnp.float32)
        returned.append(transposed(slopes, unit_half))
    relayed = shifted(returned[1], "batch", -1)
    summed = summed + shifted(returned[0] + relayed, "batch", -1)
    dunit = score_scaling_factor * summed
    radial = jnp.sum(dunit * unit_rows, axis=1, keepdims=True)
    dproj = ((dunit - unit_rows * radial) * inverse).astype(jnp.bfloat16)
    grad_rows = lax.dot_general(
        dproj, mapping_head_matrix, (((1,), (1,)), ((), ())), preferred_element_type=jnp.float32
    ).astype(jnp.bfloat16)
    grad_head = lax.psum_scatter(
        lax.dot_general(
            encoder_output_matrix,
            dproj,
            (((0,), (0,)), ((), ())),
            preferred_element_type=jnp.float32,
        ),
        "batch",
        scatter_dimension=0,
        tiled=True,
    )
    loss = lax.psum(running, "batch") / (encoder_output_matrix.shape[0] * lax.axis_size("batch"))
    return (loss, grad_rows, grad_head)


def solution(mesh):
    placed = (P("batch", None), P(), P("batch"), P(), P())
    return jax.shard_map(
        on_device,
        mesh=mesh,
        in_specs=placed,
        out_specs=(P(), P("batch", None), P("batch", None)),
        check_vma=False,
    )
```

profile of v0, /device:TPU:0, one launch (start us, length us, event | category | flops | bytes accessed | tf_op | source)
XLA Modules:
  0.0 813.8 jit_solution(9677232723825277835)
XLA Ops:
  7.2 0.0 copy-start
  7.2 0.0 reduce-scatter.4.cloned.1.call-start
  7.2 1.5 copy-done
  8.8 3.3 multiply_reduce_fusion.1
  12.0 0.0 copy-start.3
  12.1 0.2 multiply_convert_fusion.1
  12.3 1.6 collective-permute-start.3
  13.9 0.0 copy-done.3
  13.9 1.5 collective-permute-start.2
  16.7 1.4 select_multiply_fusion.2
  18.2 37.4 %collective-permute-done.2 = s32[768]{0:T(1024)S(1)} collective-permute-done((s32[768]{0:T(1024)S(1)}, s32[768]{0:T(1024)S(1)}, u32[]{:S(2)}, u32[]{:S(2)}) %collective-permute-start.2) | collective-permute-done | bytes 3104 | tf_op jit(solution)/shard_map/ppermute | solution.py:10
  55.6 0.0 collective-permute-done.3
  55.6 6.5 fusion.1
  62.1 1.4 fusion.15
  63.6 0.4 collective-permute-start.4
  63.9 0.2 collective-permute-start.1
  64.1 0.5 collective-permute-start
  64.7 24.6 %collective-permute-done = s32[768]{0:T(1024)S(1)} collective-permute-done((s32[768]{0:T(1024)S(1)}, s32[768]{0:T(1024)S(1)}, u32[]{:S(2)}, u32[]{:S(2)}) %collective-permute-start) | collective-permute-done | bytes 3104 | tf_op jit(solution)/shard_map/ppermute | solution.py:10
  89.3 0.0 collective-permute-done.1
  89.3 3.6 fusion.7
  92.8 5.9 collective-permute-done.4
  98.7 1.6 convolution_add_fusion
  100.4 7.4 collective-permute-start.5
  107.8 3.0 fusion.12
  110.8 3.1 fusion.13
  113.9 3.1 fusion.14
  117.0 3.2 fusion.10
  120.2 22.3 %collective-permute-done.5 = f32[768,1024]{1,0:T(8,128)} collective-permute-done((f32[768,1024]{1,0:T(8,128)S(1)}, f32[768,1024]{1,0:T(8,128)}, u32[]{:S(2)}, u32[]{:S(2)}) %collective-permute-start.5) | collective-permute-done | bytes 3145760 | tf_op jit(solution)/shard_map/ppermute | solution.py:10
  142.6 6.7 multiply_reduce_fusion
  149.3 0.0 copy-start.2
  149.3 0.5 multiply_convert_fusion
  149.8 0.0 copy-start.1
  149.8 1.2 copy-done.1
  151.1 0.0 copy-done.2
  151.1 3.8 convolution_bitcast_fusion
  154.9 5.3 copy.10
  160.2 0.0 reduce-scatter.4.cloned.1.call-update
  162.2 68.6 %psum.7 = f32[]{:T(128)} all-reduce(f32[]{:T(128)S(6)} %add.79), channel_id=1, replica_groups=mesh['batch'=128] {'batch'}, use_global_device_ids=true, to_apply=%region_4.5 | all-reduce | flops 1 | bytes 8 | tf_op jit(solution)/shard_map/psum | solution.py:92
  231.4 4.4 convolution_convert_fusion
  235.8 570.0 %reduce-scatter.4.cloned.1.call-done = f32[8,1024]{1,0:T(8,128)} async-done(((f32[1024,1024]{1,0:T(8,128)}), f32[8,1024]{1,0:T(8,128)}) %reduce-scatter.4.cloned.1.call-update) | async-done | bytes 32784
  (1 shorter events, 0.0 us)
Async XLA Ops:
  7.2 1.6 copy-start
  7.2 798.7 %reduce-scatter.4.cloned.1.call-start = ((), (), s32[]{:S(2)}) async-start(), calls=%async_computation.1 | async-start | bytes 4227072
  12.0 1.9 copy-start.3
  12.3 43.3 %collective-permute-start.3 = (bf16[768,1024]{1,0:T(8,128)(2,1)S(1)}, bf16[768,1024]{1,0:T(8,128)(2,1)S(1)}, u32[]{:S(2)}, u32[]{:S(2)}) collective-permute-start(bf16[768,1024]{1,0:T(8,128)(2,1)S(1)} %multiply_convert_fusion.1), channel_id=1, source_target_pairs={{0,2},{1,3},{2,4},{3,5},{4,6},{5,7},{6,8},{7,9},{8,10},{9,11},{10,... | collective-permute-start | bytes 4718600 | tf_op jit(solution)/shard_map/ppermute | solution.py:10
  13.9 41.7 %collective-permute-start.2 = (s32[768]{0:T(1024)S(1)}, s32[768]{0:T(1024)S(1)}, u32[]{:S(2)}, u32[]{:S(2)}) collective-permute-start(s32[768]{0:T(1024)S(1)} %copy-done.3), channel_id=1, source_target_pairs={{0,2},{1,3},{2,4},{3,5},{4,6},{5,7},{6,8},{7,9},{8,10},{9,11},{10,... | collective-permute-start | bytes 9224 | tf_op jit(solution)/shard_map/ppermute | solution.py:10
  63.6 35.2 %collective-permute-start.4 = (f32[768,1024]{1,0:T(8,128)S(1)}, f32[768,1024]{1,0:T(8,128)S(1)}, u32[]{:S(2)}, u32[]{:S(2)}) collective-permute-start(f32[768,1024]{1,0:T(8,128)S(1)} %fusion.15), channel_id=1, source_target_pairs={{0,127},{1,0},{2,1},{3,2},{4,3},{5,4},{6,5},{7,6},{8,7},{9,8},{10,... | collective-permute-start | bytes 9437192 | tf_op jit(solution)/shard_map/ppermute | solution.py:10
  63.9 25.3 %collective-permute-start.1 = (bf16[768,1024]{1,0:T(8,128)(2,1)S(1)}, bf16[768,1024]{1,0:T(8,128)(2,1)S(1)}, u32[]{:S(2)}, u32[]{:S(2)}) collective-permute-start(bf16[768,1024]{1,0:T(8,128)(2,1)S(1)} %multiply_convert_fusion.1), channel_id=1, source_target_pairs={{0,1},{1,2},{2,3},{3,4},{4,5},{5,6},{6,7},{7,8},{8,9},{9,10},{10,1... | collective-permute-start | bytes 4718600 | tf_op jit(solution)/shard_map/ppermute | solution.py:10
  64.1 25.1 %collective-permute-start = (s32[768]{0:T(1024)S(1)}, s32[768]{0:T(1024)S(1)}, u32[]{:S(2)}, u32[]{:S(2)}) collective-permute-start(s32[768]{0:T(1024)S(1)} %copy-done.3), channel_id=1, source_target_pairs={{0,1},{1,2},{2,3},{3,4},{4,5},{5,6},{6,7},{7,8},{8,9},{9,10},{10,1... | collective-permute-start | bytes 9224 | tf_op jit(solution)/shard_map/ppermute | solution.py:10
  100.4 42.2 %collective-permute-start.5 = (f32[768,1024]{1,0:T(8,128)S(1)}, f32[768,1024]{1,0:T(8,128)}, u32[]{:S(2)}, u32[]{:S(2)}) collective-permute-start(f32[768,1024]{1,0:T(8,128)S(1)} %convolution_add_fusion), channel_id=1, source_target_pairs={{0,127},{1,0},{2,1},{3,2},{4,3},{5,4},{6,5},{7,6},{8,7},{9,8},{10,... | collective-permute-start | bytes 9437192 | tf_op jit(solution)/shard_map/ppermute | solution.py:10
  149.3 1.8 copy-start.2
  149.8 1.2 copy-start.1
Sparse Core Ops, SparseCore 0:
  160.4 645.4 reduce-scatter.3
where the time goes:
time: 814 us
  waiting for transfers between devices  660 us (81%)
  blocking collectives  68.6 us (8%)
  matrix products  38.5 us (5%)
  between operations  19.1 us (2%)
  starting transfers between devices  11.7 us (1%)
    unnamed x2, waiting for transfers between devices  570 us
    ppermute x6, waiting for transfers between devices, shifted(): return lax.ppermute(value, axis, pairs)  90.3 us
    psum x1, blocking collectives, on_device(): lax.psum(running, 'batch')  68.6 us
  transfers between devices with their start and end apart: 7, of which 5 were waited for; matrix products, arithmetic and copies ran while one was open for 3% of the time, Pallas kernels for 0%

commit v1 on v0

v1 whole, which is shorter than its diff:
```python
import functools

import jax
import jax.numpy as jnp
from jax import lax
from jax.experimental import pallas as pl
from jax.experimental.pallas import tpu as pltpu
from jax.sharding import PartitionSpec as P

ROWS = 768
DIM = 1024
STEP = 256
HEAD_PART = 512
TAIL_PART = ROWS - HEAD_PART
MIB = 1 << 20

NT = (((1,), (1,)), ((), ()))


def params(mib, steps=1):
    return pltpu.CompilerParams(
        dimension_semantics=("arbitrary",) * steps, vmem_limit_bytes=mib * MIB
    )


def cost(flops, moved):
    return pl.CostEstimate(flops=flops, bytes_accessed=moved, transcendentals=0)


def rows_block(width=DIM, rows=STEP):
    return pl.BlockSpec((rows, width), lambda i: (i, 0))


def whole(*shape):
    return pl.BlockSpec(shape, lambda i: (0,) * len(shape))


SCALARS = pl.BlockSpec(memory_space=pltpu.SMEM)


def normalised(x, w):
    projected = jnp.dot(x, w, preferred_element_type=jnp.float32)
    inverse = lax.rsqrt(DIM * (jnp.mean(projected * projected, axis=1, keepdims=True) + 1e-06))
    return projected * inverse, inverse


def own_projection_kernel(x_ref, w_ref, half_ref, unit_ref, inverse_ref, turned_ref):
    x = x_ref[...]
    unit, inverse = normalised(x, w_ref[...])
    unit_ref[...] = unit
    half_ref[...] = unit.astype(jnp.bfloat16)
    inverse_ref[...] = inverse
    turned_ref[...] = x.T


def own_projection(x, w):
    return pl.pallas_call(
        own_projection_kernel,
        grid=(ROWS // STEP,),
        in_specs=[rows_block(), whole(DIM, DIM)],
        out_specs=[
            rows_block(),
            rows_block(),
            rows_block(1),
            pl.BlockSpec((DIM, STEP), lambda i: (0, i)),
        ],
        out_shape=[
            jax.ShapeDtypeStruct((ROWS, DIM), jnp.bfloat16),
            jax.ShapeDtypeStruct((ROWS, DIM), jnp.float32),
            jax.ShapeDtypeStruct((ROWS, 1), jnp.float32),
            jax.ShapeDtypeStruct((DIM, ROWS), jnp.bfloat16),
        ],
        compiler_params=params(32),
        cost_estimate=cost(2 * ROWS * DIM * DIM, 10 * MIB),
    )(x, w)


def partner_projection_kernel(x_ref, w_ref, tail_ref, half_ref, sent_ref):
    unit, _ = normalised(x_ref[...], w_ref[...])
    half_ref[...] = unit.astype(jnp.bfloat16)
    sent_ref[...] = tail_ref[...]


def partner_projection(x, w, half):
    return pl.pallas_call(
        partner_projection_kernel,
        grid=(ROWS // STEP,),
        in_specs=[
            rows_block(),
            whole(DIM, DIM),
            pl.BlockSpec((TAIL_PART, DIM), lambda i: (HEAD_PART // TAIL_PART, 0)),
        ],
        out_specs=[rows_block(), whole(TAIL_PART, DIM)],
        out_shape=[
            jax.ShapeDtypeStruct((ROWS, DIM), jnp.bfloat16),
            jax.ShapeDtypeStruct((TAIL_PART, DIM), jnp.bfloat16),
        ],
        compiler_params=params(32),
        cost_estimate=cost(2 * ROWS * DIM * DIM, 6 * MIB),
    )(x, w, half)


def slopes_of(cosine, row_ids, col_ids, scale, shift, with_loss):
    logits = scale * cosine + shift
    same = row_ids == col_ids
    signed = jnp.where(same, -logits, logits)
    if not with_loss:
        gate = 1.0 / (1.0 + jnp.exp(-signed))
        return jnp.where(same, -gate, gate).astype(jnp.bfloat16), None
    decay = jnp.exp(-jnp.abs(signed))
    share = 1.0 / (1.0 + decay)
    gate = jnp.where(signed >= 0, share, decay * share)
    losses = jnp.maximum(signed, 0.0) + jnp.log1p(decay)
    return jnp.where(same, -gate, gate).astype(jnp.bfloat16), losses


def lane_sums(losses):
    rows, cols = losses.shape
    by_tile = losses.reshape(rows // 8, 8, cols).sum(axis=0)
    total = by_tile[:, :128]
    for start in range(128, cols, 128):
        total = total + by_tile[:, start : start + 128]
    return total


def tile_body(scalars, rows, partner_ref, row_ids, col_ids_ref, with_loss):
    scale, shift = scalars[0], scalars[1]
    total = loss = None
    for start in range(0, partner_ref.shape[0], STEP):
        cols = partner_ref[start : start + STEP, :]
        cosine = lax.dot_general(rows, cols, NT, preferred_element_type=jnp.float32)
        slopes, losses = slopes_of(
            cosine, row_ids, col_ids_ref[:, start : start + STEP], scale, shift, with_loss
        )
        piece = jnp.dot(slopes, cols, preferred_element_type=jnp.float32)
        total = piece if total is None else total + piece
        if with_loss:
            part = lane_sums(losses)
            loss = part if loss is None else loss + part
    return total, loss


def own_tile_kernel(scalars, rows_ref, all_ref, row_ids, col_ids, sum_ref, loss_ref, sent_ref):
    step = pl.program_id(0)
    rows = rows_ref[...]
    total, loss = tile_body(scalars, rows, all_ref, row_ids[...], col_ids, True)
    sum_ref[...] = 2.0 * total

    @pl.when(step == 0)
    def _():
        loss_ref[...] = jnp.zeros_like(loss_ref)

    loss_ref[...] += loss

    @pl.when(step < HEAD_PART // STEP)
    def _():
        sent_ref[...] = rows


def own_tile(scalars, half, row_ids, col_ids):
    return pl.pallas_call(
        own_tile_kernel,
        grid=(ROWS // STEP,),
        in_specs=[SCALARS, rows_block(), whole(ROWS, DIM), rows_block(1), whole(1, ROWS)],
        out_specs=[
            rows_block(),
            whole(8, 128),
            pl.BlockSpec((STEP, DIM), lambda i: (jnp.minimum(i, HEAD_PART // STEP - 1), 0)),
        ],
        out_shape=[
            jax.ShapeDtypeStruct((ROWS, DIM), jnp.float32),
            jax.ShapeDtypeStruct((8, 128), jnp.float32),
            jax.ShapeDtypeStruct((HEAD_PART, DIM), jnp.bfloat16),
        ],
        compiler_params=params(32),
        cost_estimate=cost(4 * ROWS * ROWS * DIM, 8 * MIB),
    )(scalars, half, half, row_ids, col_ids)


def partner_tile_kernel(
    weight, scalars, rows_ref, partner_ref, row_ids, col_ids, sum_in, loss_in, sum_ref, loss_ref
):
    step = pl.program_id(0)
    total, loss = tile_body(
        scalars, rows_ref[...], partner_ref, row_ids[...], col_ids, weight is not None
    )
    sum_ref[...] = sum_in[...] + total

    @pl.when(step == 0)
    def _():
        loss_ref[...] = loss_in[...]

    if weight is not None:
        loss_ref[...] += weight * loss


def partner_tile(weight, scalars, half, partner, row_ids, col_ids, summed, loss):
    count = partner.shape[0]
    return pl.pallas_call(
        functools.partial(partner_tile_kernel, weight),
        grid=(ROWS // STEP,),
        in_specs=[
            SCALARS,
            rows_block(),
            whole(count, DIM),
            rows_block(1),
            whole(1, count),
            rows_block(),
            whole(8, 128),
        ],
        out_specs=[rows_block(), whole(8, 128)],
        out_shape=[
            jax.ShapeDtypeStruct((ROWS, DIM), jnp.float32),
            jax.ShapeDtypeStruct((8, 128), jnp.float32),
        ],
        input_output_aliases={5: 0},
        compiler_params=params(32),
        cost_estimate=cost(4 * ROWS * count * DIM, 10 * MIB),
    )(scalars, half, partner, row_ids, col_ids, summed, loss)


def last_kernel(
    scalars,
    parity,
    rows_ref,
    partner_ref,
    row_ids,
    col_ids,
    sum_in,
    unit_ref,
    inverse_ref,
    turned_ref,
    dproj_ref,
    kept_ref,
    sent_ref,
    held,
):
    step = pl.program_id(0)
    row_steps = ROWS // STEP

    @pl.when(step < row_steps)
    def _():
        total, _ = tile_body(scalars, rows_ref[...], partner_ref, row_ids[...], col_ids, False)
        unit = unit_ref[...]
        dunit = scalars[0] * (sum_in[...] + total)
        radial = jnp.sum(dunit * unit, axis=1, keepdims=True)
        dproj = ((dunit - unit * radial) * inverse_ref[...]).astype(jnp.bfloat16)
        dproj_ref[...] = dproj
        held[pl.ds(pl.multiple_of(step * STEP, STEP), STEP), :] = dproj

    @pl.when(step >= row_steps)
    def _():
        product = jnp.dot(turned_ref[...], held[...], preferred_element_type=jnp.float32)
        product = product.reshape(STEP // 16, 2, 8, DIM)
        even, odd = product[:, 0], product[:, 1]
        first = parity[0] == 0
        kept_ref[...] = jnp.where(first, even, odd).reshape(STEP // 2, DIM)
        sent_ref[...] = jnp.where(first, odd, even).reshape(STEP // 2, DIM).astype(jnp.bfloat16)


def last(scalars, parity, half, partner, row_ids, col_ids, summed, unit, inverse, turned):
    row_steps, head_steps = ROWS // STEP, DIM // STEP
    count = partner.shape[0]

    def early(i):
        return jnp.minimum(i, row_steps - 1), 0

    def late(i):
        return jnp.maximum(i - row_steps, 0), 0

    return pl.pallas_call(
        last_kernel,
        grid=(row_steps + head_steps,),
        in_specs=[
            SCALARS,
            SCALARS,
            pl.BlockSpec((STEP, DIM), early),
            whole(count, DIM),
            pl.BlockSpec((STEP, 1), early),
            whole(1, count),
            pl.BlockSpec((STEP, DIM), early),
            pl.BlockSpec((STEP, DIM), early),
            pl.BlockSpec((STEP, 1), early),
            pl.BlockSpec((STEP, ROWS), late),
        ],
        out_specs=[
            pl.BlockSpec((STEP, DIM), early),
            pl.BlockSpec((STEP // 2, DIM), late),
            pl.BlockSpec((STEP // 2, DIM), late),
        ],
        out_shape=[
            jax.ShapeDtypeStruct((ROWS, DIM), jnp.bfloat16),
            jax.ShapeDtypeStruct((DIM // 2, DIM), jnp.float32),
            jax.ShapeDtypeStruct((DIM // 2, DIM), jnp.bfloat16),
        ],
        scratch_shapes=[pltpu.VMEM((ROWS, DIM), jnp.bfloat16)],
        compiler_params=params(40),
        cost_estimate=cost(4 * ROWS * count * DIM + 2 * ROWS * DIM * DIM, 14 * MIB),
    )(scalars, parity, half, partner, row_ids, col_ids, summed, unit, inverse, turned)


def grad_rows_kernel(dproj_ref, w_ref, out_ref):
    out_ref[...] = lax.dot_general(
        dproj_ref[...], w_ref[...], NT, preferred_element_type=jnp.float32
    ).astype(jnp.bfloat16)


def grad_rows_of(dproj, w):
    return pl.pallas_call(
        grad_rows_kernel,
        grid=(ROWS // STEP,),
        in_specs=[rows_block(), whole(DIM, DIM)],
        out_specs=rows_block(),
        out_shape=jax.ShapeDtypeStruct((ROWS, DIM), jnp.bfloat16),
        compiler_params=params(32),
        cost_estimate=cost(2 * ROWS * DIM * DIM, 5 * MIB),
    )(dproj, w)


def packed_kernel(kept_ref, received_ref, loss_ref, other_loss_ref, out_ref):
    out_ref[:, :DIM] = (kept_ref[...] + received_ref[...].astype(jnp.float32)).astype(jnp.bfloat16)
    lanes = jnp.sum(loss_ref[...] + other_loss_ref[...], axis=0, keepdims=True)
    high = lanes.astype(jnp.bfloat16).astype(jnp.float32)
    middle = (lanes - high).astype(jnp.bfloat16).astype(jnp.float32)
    low = lanes - high - middle
    place = lax.broadcasted_iota(jnp.int32, (16, 128), 0) % 8
    tile = jnp.where(
        place == 0, high, jnp.where(place == 1, middle, jnp.where(place == 2, low, 0.0))
    ).astype(jnp.bfloat16)
    for start in range(0, out_ref.shape[0], 16):
        out_ref[start : start + 16, DIM:] = tile


def packed(kept, received, loss, other_loss):
    rows = 128
    return pl.pallas_call(
        packed_kernel,
        grid=(DIM // 2 // rows,),
        in_specs=[rows_block(DIM, rows), rows_block(DIM, rows), whole(8, 128), whole(8, 128)],
        out_specs=rows_block(DIM + 128, rows),
        out_shape=jax.ShapeDtypeStruct((DIM // 2, DIM + 128), jnp.bfloat16),
        compiler_params=params(16),
        cost_estimate=cost(DIM * DIM, 5 * MIB),
    )(kept, received, loss, other_loss)


def finish_kernel(tokens, parts_ref, head_ref, loss_ref):
    total = parts_ref[0].astype(jnp.float32)
    for part in range(1, parts_ref.shape[0]):
        total = total + parts_ref[part].astype(jnp.float32)
    head_ref[...] = total[:, :DIM]
    loss_ref[...] = jnp.sum(total[:, DIM:]).reshape(1, 1) / tokens


def finish(parts, tokens):
    return pl.pallas_call(
        functools.partial(finish_kernel, tokens),
        out_shape=[
            jax.ShapeDtypeStruct((8, DIM), jnp.float32),
            jax.ShapeDtypeStruct((1, 1), jnp.float32),
        ],
        compiler_params=pltpu.CompilerParams(vmem_limit_bytes=16 * MIB),
        cost_estimate=cost(DIM * DIM, 2 * MIB),
    )(parts)


def on_device(x, w, label, score_scale, score_shift):
    count = lax.axis_size("batch")

    def move(value, target):
        return lax.ppermute(value, "batch", [(i, target(i) % count) for i in range(count)])

    def pair(i):
        return i ^ 1

    def near(i):
        return i + 1 if i & 1 else i - 1

    def far(i):
        return i - 2 if i & 1 else i + 2

    scalars = jnp.concatenate([score_scale, score_shift])
    parity = (lax.axis_index("batch") & 1).astype(jnp.int32).reshape(1)
    row_ids = label.reshape(ROWS, 1)
    own_ids = label.reshape(1, ROWS)

    near_x = move(x, near)
    near_ids = move(own_ids, near)
    far_ids = move(own_ids, far)
    pair_ids = move(own_ids, pair)
    third_ids = move(near_ids, pair)

    half, unit, inverse, turned = own_projection(x, w)
    pair_half = move(half, pair)
    summed, loss, far_sent = own_tile(scalars, half, row_ids, own_ids)
    far_head = move(far_sent, far)
    summed, loss = partner_tile(0.5, scalars, half, pair_half, row_ids, pair_ids, summed, loss)
    near_half, far_sent = partner_projection(near_x, w, half)
    far_tail = move(far_sent, far)
    third_half = move(near_half, pair)
    summed, loss = partner_tile(0.5, scalars, half, near_half, row_ids, near_ids, summed, loss)
    summed, loss = partner_tile(1.0, scalars, half, third_half, row_ids, third_ids, summed, loss)
    other_loss = move(loss, pair)
    summed, _ = partner_tile(
        None, scalars, half, far_head, row_ids, far_ids[:, :HEAD_PART], summed, loss
    )
    dproj, kept, sent = last(
        scalars,
        parity,
        half,
        far_tail,
        row_ids,
        far_ids[:, HEAD_PART:],
        summed,
        unit,
        inverse,
        turned,
    )
    received = move(sent, pair)
    grad_rows = grad_rows_of(dproj, w)
    chips = count // 2
    groups = [[2 * chip + core for chip in range(chips)] for core in range(2)]
    parts = packed(kept, received, loss, other_loss).reshape(chips, 8, DIM + 128)
    parts = lax.all_to_all(parts, "batch", 0, 0, tiled=True, axis_index_groups=groups)
    grad_head, total = finish(parts, float(ROWS * count))
    return (total.reshape(()), grad_rows, grad_head)


def solution(mesh):
    placed = (P("batch", None), P(), P("batch"), P(), P())
    return jax.shard_map(
        on_device,
        mesh=mesh,
        in_specs=placed,
        out_specs=(P(), P("batch", None), P("batch", None)),
        check_vma=False,
    )
```

time: 814 us -> 138 us (0.17)
  waiting for transfers between devices: 660 us -> 42.5 us
  blocking collectives: 68.6 us -> 0 us
  Pallas kernels: 0 us -> 56.1 us
  matrix products: 38.5 us -> 0 us
  between operations: 19.1 us -> 2.13 us
  starting transfers between devices: 11.7 us -> 26.9 us
    unnamed x2 -> x0, waiting for transfers between devices: 570 us -> none
    psum x1 -> x0, blocking collectives: 68.6 us -> none  [on_device(): lax.psum(running, 'batch')]
    ppermute x6 -> x11, waiting for transfers between devices: 90.3 us -> 25.9 us  [move(): lax.ppermute(value, 'batch', [(i, target(i) % count) for i in range(count)])]
    pallas_call x0 -> x11, Pallas kernels: none -> 56.1 us  [the longest x4 27 us: partner_tile(): pl.pallas_call(functools.partial(partner_tile_kernel, weight), grid=(ROWS...]
    dot_general x12 -> x0, matrix products: 38.5 us -> none  [the longest x3 11.5 us: tile_terms(): lax.dot_general(rows_emb, column_embedding_vectors, (((1,), (1,)), ((), (...]
    all_to_all x0 -> x1, waiting for transfers between devices: none -> 16.7 us  [on_device(): lax.all_to_all(parts, 'batch', 0, 0, tiled=True, axis_index_groups=groups)]
    ppermute x6 -> x11, starting transfers between devices: 11.6 us -> 22.1 us  [move(): lax.ppermute(value, 'batch', [(i, target(i) % count) for i in range(count)])]
  transfers between devices with their start and end apart: 7 -> 12, of which waited for: 5 -> 4; matrix products, arithmetic and copies ran while one was open for 3% -> 1% of each run, Pallas kernels for 0% -> 34%
where the time goes in v1:
time: 138 us; the launch traced here: 137 us
  Pallas kernels  56.1 us (41%)
  waiting for transfers between devices  42.5 us (31%)
  starting transfers between devices  26.9 us (19%)
  local copies, waits for them, and re-layouts  9.38 us (7%)
  between operations  2.13 us (2%)
    pallas_call x4, Pallas kernels, partner_tile(): pl.pallas_call(functools.partial(partner_tile_kernel, weight), grid=(ROWS...  27 us
    ppermute x11, waiting for transfers between devices, move(): lax.ppermute(value, 'batch', [(i, target(i) % count) for i in range(count)])  25.9 us
    ppermute x11, starting transfers between devices, move(): lax.ppermute(value, 'batch', [(i, target(i) % count) for i in range(count)])  22.1 us
    all_to_all x1, waiting for transfers between devices, on_device(): lax.all_to_all(parts, 'batch', 0, 0, tiled=True, axis_index_groups=groups)  16.7 us
    pallas_call x1, Pallas kernels, own_tile(): pl.pallas_call(own_tile_kernel, grid=(ROWS // STEP,), in_specs=[SCALARS,...  8.06 us
    unnamed x32, local copies, waits for them, and re-layouts  7.92 us
    pallas_call x1, Pallas kernels, last(): pl.pallas_call(last_kernel, grid=(row_steps + head_steps,), in_specs=[SCA...  7.56 us
    all_to_all x1, starting transfers between devices, on_device(): lax.all_to_all(parts, 'batch', 0, 0, tiled=True, axis_index_groups=groups)  4.79 us
  transfers between devices with their start and end apart: 12, of which 4 were waited for; matrix products, arithmetic and copies ran while one was open for 1% of the time, Pallas kernels for 34%

profile of v1, /device:TPU:0, one launch (start us, length us, event | category | flops | bytes accessed | tf_op | source)
XLA Modules:
  0.0 137.0 jit_solution(5156653793862485138)
XLA Ops:
  0.6 8.3 %collective-permute-start = (bf16[768,1024]{1,0:T(8,128)(2,1)}, bf16[768,1024]{1,0:T(8,128)(2,1)S(1)}, u32[]{:S(2)}, u32[]{:S(2)}) collective-permute-start(bf16[768,1024]{1,0:T(8,128)(2,1)} %x_ref.1), channel_id=1, source_target_pairs={{0,127},{1,2},{2,1},{3,4},{4,3},{5,6},{6,5},{7,8},{8,7},{9,10},{10... | collective-permute-start | bytes 4718600 | tf_op jit(solution)/shard_map/ppermute | solution.py:371
  8.9 1.6 %copy-done.5 = bf16[1024,1024]{1,0:T(8,128)(2,1)S(1)} copy-done((bf16[1024,1024]{1,0:T(8,128)(2,1)S(1)}, bf16[1024,1024]{1,0:T(8,128)(2,1)}, u32[]{:S(2)}) %copy-start.5) | copy-done | bytes 2097176
  10.5 1.4 %copy-done.8 = bf16[768,1024]{1,0:T(8,128)(2,1)S(1)} copy-done((bf16[768,1024]{1,0:T(8,128)(2,1)S(1)}, bf16[768,1024]{1,0:T(8,128)(2,1)}, u32[]{:S(2)}) %copy-start.8) | copy-done | bytes 1572888
  11.9 3.4 %shard_map.76 = (bf16[768,1024]{1,0:T(8,128)(2,1)}, f32[768,1024]{1,0:T(8,128)S(1)}, f32[768,1]{1,0:T(8,128)S(1)}, bf16[1024,768]{1,0:T(8,128)(2,1)S(1)}) custom-call(bf16[768,1024]{1,0:T(8,128)(2,1)S(1)} %copy-done.8, bf16[1024,1024]{1,0:T(8,128)(2,1)S(1)} %copy-done.5), custom_call_target="tpu_custom_call" | custom-call | flops 1610612736 | bytes 10485760 | tf_op jit(solution)/shard_map/pallas_call | solution.py:57
  15.4 1.6 %copy-done = f32[768,1024]{1,0:T(8,128)} copy-done((f32[768,1024]{1,0:T(8,128)}, f32[768,1024]{1,0:T(8,128)S(1)}, u32[]{:S(2)}) %copy-start) | copy-done | bytes 3145752
  17.0 0.0 collective-permute-start.7
  17.0 10.2 %collective-permute-done.x_ref = bf16[768,1024]{1,0:T(8,128)(2,1)S(1)} collective-permute-done((bf16[768,1024]{1,0:T(8,128)(2,1)}, bf16[768,1024]{1,0:T(8,128)(2,1)S(1)}, u32[]{:S(2)}, u32[]{:S(2)}) %collective-permute-start) | collective-permute-done | bytes 1572896 | tf_op jit(solution)/shard_map/ppermute | solution.py:371
  27.2 4.4 %shard_map.77 = (bf16[768,1024]{1,0:T(8,128)(2,1)}, bf16[256,1024]{1,0:T(8,128)(2,1)S(1)}) custom-call(bf16[768,1024]{1,0:T(8,128)(2,1)S(1)} %collective-permute-done.x_ref, bf16[1024,1024]{1,0:T(8,128)(2,1)S(1)} %copy-done.6, bf16[768,1024]{1,0:T(8,128)(2,1)} %get-tuple-element.24.tail_ref.rows_ref.all_ref), custom_call_target="tpu_custom_call" | custom-call | flops 1610612736 | bytes 6291456 | tf_op jit(solution)/shard_map/pallas_call | solution.py:85
  31.6 0.1 collective-permute-start.4
  31.7 0.2 reshape.26.row_ids
  33.2 0.1 pad_maximum_fusion.scalars
  33.3 8.1 %shard_map.78 = (f32[768,1024]{1,0:T(8,128)S(1)}, f32[8,128]{1,0:T(8,128)S(1)}, bf16[512,1024]{1,0:T(8,128)(2,1)}) custom-call(f32[2]{0:T(128)S(1)} %pad_maximum_fusion.scalars, bf16[768,1024]{1,0:T(8,128)(2,1)} %get-tuple-element.24.tail_ref.rows_ref.all_ref, bf16[768,1024]{1,0:T(8,128)(2,1)} %get-tuple-element.24.tail_ref.rows_ref.all_ref, ...), custom_call_target="tpu_custom_call" | custom-call | flops 2415919104 | bytes 8388608 | tf_op jit(solution)/shard_map/pallas_call | solution.py:161
  41.4 0.6 copy-done.12
  41.9 0.0 collective-permute-start.3
  41.9 0.0 collective-permute-start.2
  42.0 7.2 %collective-permute-start.5 = (s32[1,768]{1,0:T(1,128)S(1)}, s32[1,768]{1,0:T(1,128)S(1)}, u32[]{:S(2)}, u32[]{:S(2)}) collective-permute-start(s32[1,768]{1,0:T(1,128)S(1)} %reshape.23.col_ids), channel_id=1, source_target_pairs={{0,127},{1,2},{2,1},{3,4},{4,3},{5,6},{6,5},{7,8},{8,7},{9,10},{10... | collective-permute-start | bytes 9224 | tf_op jit(solution)/shard_map/ppermute | solution.py:371
  49.2 13.4 %collective-permute-done.2 = s32[1,768]{1,0:T(1,128)S(1)} collective-permute-done((s32[1,768]{1,0:T(1,128)S(1)}, s32[1,768]{1,0:T(1,128)S(1)}, u32[]{:S(2)}, u32[]{:S(2)}) %collective-permute-start.2) | collective-permute-done | bytes 3104 | tf_op jit(solution)/shard_map/ppermute | solution.py:371
  62.6 0.0 collective-permute-start.8
  62.6 0.6 copy-done.15
  63.2 0.6 slice.9.col_ids
  63.8 0.7 slice.8.col_ids
  64.5 0.0 collective-permute-done.5.col_ids
  64.5 0.0 collective-permute-start.6
  64.5 0.0 collective-permute-done.8.col_ids
  64.5 0.3 collective-permute-start.1
  64.7 0.0 collective-permute-done.7.partner_ref
  64.7 0.0 copy-start.13
  64.8 0.7 copy-done.13
  65.4 7.3 %shard_map.79 = (f32[768,1024]{1,0:T(8,128)S(1)}, f32[8,128]{1,0:T(8,128)S(1)}) custom-call(f32[2]{0:T(128)S(1)} %pad_maximum_fusion.scalars, bf16[768,1024]{1,0:T(8,128)(2,1)} %get-tuple-element.24.tail_ref.rows_ref.all_ref, bf16[768,1024]{1,0:T(8,128)(2,1)} %collective-permute-done.7.partner_ref, ...), custom_call_target="tpu_custom_call", output_to_operand_aliasing={{0}: (5, {})} | custom-call | flops 2415919104 | bytes 10485760 | tf_op jit(solution)/shard_map/pallas_call | solution.py:199
  72.7 7.3 %shard_map.80 = (f32[768,1024]{1,0:T(8,128)S(1)}, f32[8,128]{1,0:T(8,128)S(1)}) custom-call(f32[2]{0:T(128)S(1)} %pad_maximum_fusion.scalars, bf16[768,1024]{1,0:T(8,128)(2,1)} %get-tuple-element.24.tail_ref.rows_ref.all_ref, bf16[768,1024]{1,0:T(8,128)(2,1)} %get-tuple-element.27.partner_ref, ...), custom_call_target="tpu_custom_call", output_to_operand_aliasing={{0}: (5, {})} | custom-call | flops 2415919104 | bytes 10485760 | tf_op jit(solution)/shard_map/pallas_call | solution.py:199
  80.1 0.0 collective-permute-done.4.partner_ref
  80.1 7.3 %shard_map.81 = (f32[768,1024]{1,0:T(8,128)S(1)}, f32[8,128]{1,0:T(8,128)S(1)}) custom-call(f32[2]{0:T(128)S(1)} %pad_maximum_fusion.scalars, bf16[768,1024]{1,0:T(8,128)(2,1)} %get-tuple-element.24.tail_ref.rows_ref.all_ref, bf16[768,1024]{1,0:T(8,128)(2,1)} %collective-permute-done.4.partner_ref, ...), custom_call_target="tpu_custom_call", output_to_operand_aliasing={{0}: (5, {})} | custom-call | flops 2415919104 | bytes 10485760 | tf_op jit(solution)/shard_map/pallas_call | solution.py:199
  87.4 0.0 collective-permute-done.3.partner_ref
  87.4 5.1 %shard_map.82 = (f32[768,1024]{1,0:T(8,128)S(1)}, f32[8,128]{1,0:T(8,128)}) custom-call(f32[2]{0:T(128)S(1)} %pad_maximum_fusion.scalars, bf16[768,1024]{1,0:T(8,128)(2,1)} %get-tuple-element.24.tail_ref.rows_ref.all_ref, bf16[512,1024]{1,0:T(8,128)(2,1)} %collective-permute-done.3.partner_ref, ...), custom_call_target="tpu_custom_call", output_to_operand_aliasing={{0}: (5, {})} | custom-call | flops 1610612736 | bytes 10485760 | tf_op jit(solution)/shard_map/pallas_call | solution.py:199
  92.5 0.0 collective-permute-done.1.partner_ref
  92.5 7.6 %shard_map.83 = (bf16[768,1024]{1,0:T(8,128)(2,1)S(1)}, f32[512,1024]{1,0:T(8,128)S(1)}, bf16[512,1024]{1,0:T(8,128)(2,1)S(1)}) custom-call(f32[2]{0:T(128)S(1)} %pad_maximum_fusion.scalars, s32[1]{0:T(128)} %bitcast.parity, bf16[768,1024]{1,0:T(8,128)(2,1)} %get-tuple-element.24.tail_ref.rows_ref.all_ref, ...), custom_call_target="tpu_custom_call" | custom-call | flops 2415919104 | bytes 14680064 | tf_op jit(solution)/shard_map/pallas_call | solution.py:271
  100.1 0.0 copy-start.9
  100.1 6.1 %collective-permute-start.9 = (bf16[512,1024]{1,0:T(8,128)(2,1)S(1)}, bf16[512,1024]{1,0:T(8,128)(2,1)S(1)}, u32[]{:S(2)}, u32[]{:S(2)}) collective-permute-start(bf16[512,1024]{1,0:T(8,128)(2,1)S(1)} %get-tuple-element.41), channel_id=1, source_target_pairs={{0,1},{1,0},{2,3},{3,2},{4,5},{5,4},{6,7},{7,6},{8,9},{9,8},{10,11... | collective-permute-start | bytes 3145736 | tf_op jit(solution)/shard_map/ppermute | solution.py:371
  106.3 0.1 collective-permute-start.10
  106.4 2.2 %collective-permute-done.10.other_loss_ref = f32[8,128]{1,0:T(8,128)S(1)} collective-permute-done((f32[8,128]{1,0:T(8,128)S(1)}, f32[8,128]{1,0:T(8,128)S(1)}, u32[]{:S(2)}, u32[]{:S(2)}) %collective-permute-start.10) | collective-permute-done | bytes 4128 | tf_op jit(solution)/shard_map/ppermute | solution.py:371
  108.6 0.0 collective-permute-done.9.received_ref
  108.6 1.7 %shard_map.84 = bf16[512,1152]{1,0:T(8,128)(2,1)} custom-call(f32[512,1024]{1,0:T(8,128)S(1)} %get-tuple-element.40.kept_ref, bf16[512,1024]{1,0:T(8,128)(2,1)S(1)} %collective-permute-done.9.received_ref, f32[8,128]{1,0:T(8,128)S(1)} %get-tuple-element.35.loss_in.loss_ref, f32[8,128]{1,0:T(8,128)S(1)} %collective-permute-done.10.other_loss_ref), custom_call_target="tpu_custom_call" | custom-call | flops 1048576 | bytes 5242880 | tf_op jit(solution)/shard_map/pallas_call | solution.py:336
  110.3 4.8 %all-to-all-start = ((bf16[64,8,1152]{2,1,0:T(8,128)(2,1)}), bf16[64,8,1152]{2,1,0:T(8,128)(2,1)S(1)}, u32[]{:S(2)}, u32[]{:S(2)}) async-start(bf16[64,8,1152]{2,1,0:T(8,128)(2,1)} %bitcast.1), calls=%async_computation | async-start | bytes 2359296 | tf_op jit(solution)/shard_map/all_to_all | solution.py:424
  115.1 0.0 copy-start.10
  115.1 1.4 %copy-done.10 = bf16[768,1024]{1,0:T(8,128)(2,1)S(1)} copy-done((bf16[768,1024]{1,0:T(8,128)(2,1)S(1)}, bf16[768,1024]{1,0:T(8,128)(2,1)}, u32[]{:S(2)}) %copy-start.10) | copy-done | bytes 1572888
  116.5 3.1 %shard_map.86 = bf16[768,1024]{1,0:T(8,128)(2,1)} custom-call(bf16[768,1024]{1,0:T(8,128)(2,1)S(1)} %copy-done.10, bf16[1024,1024]{1,0:T(8,128)(2,1)S(1)} %copy-done.7), custom_call_target="tpu_custom_call" | custom-call | flops 1610612736 | bytes 5242880 | tf_op jit(solution)/shard_map/pallas_call | solution.py:309
  119.6 16.7 %all-to-all-done.parts_ref = bf16[64,8,1152]{2,1,0:T(8,128)(2,1)S(1)} async-done(((bf16[64,8,1152]{2,1,0:T(8,128)(2,1)}), bf16[64,8,1152]{2,1,0:T(8,128)(2,1)S(1)}, u32[]{:S(2)}, u32[]{:S(2)}) %all-to-all-start) | async-done | bytes 1179680 | tf_op jit(solution)/shard_map/all_to_all | solution.py:424
  136.3 0.8 shard_map.85
  (24 shorter events, 0.0 us)
Async XLA Ops:
  0.6 26.6 %collective-permute-start = (bf16[768,1024]{1,0:T(8,128)(2,1)}, bf16[768,1024]{1,0:T(8,128)(2,1)S(1)}, u32[]{:S(2)}, u32[]{:S(2)}) collective-permute-start(bf16[768,1024]{1,0:T(8,128)(2,1)} %x_ref.1), channel_id=1, source_target_pairs={{0,127},{1,2},{2,1},{3,4},{4,3},{5,6},{6,5},{7,8},{8,7},{9,10},{10... | collective-permute-start | bytes 4718600 | tf_op jit(solution)/shard_map/ppermute | solution.py:371
  8.9 1.6 %copy-start.5 = (bf16[1024,1024]{1,0:T(8,128)(2,1)S(1)}, bf16[1024,1024]{1,0:T(8,128)(2,1)}, u32[]{:S(2)}) copy-start(bf16[1024,1024]{1,0:T(8,128)(2,1)} %w_ref.5) | copy-start | bytes 6291460
  10.5 1.4 %copy-start.8 = (bf16[768,1024]{1,0:T(8,128)(2,1)S(1)}, bf16[768,1024]{1,0:T(8,128)(2,1)}, u32[]{:S(2)}) copy-start(bf16[768,1024]{1,0:T(8,128)(2,1)} %x_ref.1) | copy-start | bytes 4718596
  11.9 15.3 %copy-start.6 = (bf16[1024,1024]{1,0:T(8,128)(2,1)S(1)}, bf16[1024,1024]{1,0:T(8,128)(2,1)}, u32[]{:S(2)}) copy-start(bf16[1024,1024]{1,0:T(8,128)(2,1)} %w_ref.5) | copy-start | bytes 6291460
  15.4 1.6 %copy-start = (f32[768,1024]{1,0:T(8,128)}, f32[768,1024]{1,0:T(8,128)S(1)}, u32[]{:S(2)}) copy-start(f32[768,1024]{1,0:T(8,128)S(1)} %get-tuple-element.37.unit_ref) | copy-start | bytes 9437188
  17.0 14.6 %copy-start.1 = (bf16[1024,768]{1,0:T(8,128)(2,1)}, bf16[1024,768]{1,0:T(8,128)(2,1)S(1)}, u32[]{:S(2)}) copy-start(bf16[1024,768]{1,0:T(8,128)(2,1)S(1)} %get-tuple-element.39.turned_ref) | copy-start | bytes 4718596
  17.0 14.6 %copy-start.3 = (f32[768,1]{1,0:T(8,128)}, f32[768,1]{1,0:T(8,128)S(1)}, u32[]{:S(2)}) copy-start(f32[768,1]{1,0:T(8,128)S(1)} %get-tuple-element.38.inverse_ref) | copy-start | bytes 9220
  17.0 14.7 %copy-start.14 = (s32[768]{0:T(1024)S(1)}, s32[768]{0:T(1024)}, u32[]{:S(2)}) copy-start(s32[768]{0:T(1024)} %param.7) | copy-start | bytes 9220
  17.0 47.7 %collective-permute-start.7 = (bf16[768,1024]{1,0:T(8,128)(2,1)}, bf16[768,1024]{1,0:T(8,128)(2,1)}, u32[]{:S(2)}, u32[]{:S(2)}) collective-permute-start(bf16[768,1024]{1,0:T(8,128)(2,1)} %get-tuple-element.24.tail_ref.rows_ref.all_ref), channel_id=1, source_target_pairs={{0,1},{1,0},{2,3},{3,2},{4,5},{5,4},{6,7},{7,6},{8,9},{9,8},{10,11... | collective-permute-start | bytes 4718600 | tf_op jit(solution)/shard_map/ppermute | solution.py:371
  31.6 9.7 %copy-start.11 = (bf16[256,1024]{1,0:T(8,128)(2,1)}, bf16[256,1024]{1,0:T(8,128)(2,1)S(1)}, u32[]{:S(2)}) copy-start(bf16[256,1024]{1,0:T(8,128)(2,1)S(1)} %get-tuple-element.25) | copy-start | bytes 1572868
  31.6 48.4 %collective-permute-start.4 = (bf16[768,1024]{1,0:T(8,128)(2,1)}, bf16[768,1024]{1,0:T(8,128)(2,1)}, u32[]{:S(2)}, u32[]{:S(2)}) collective-permute-start(bf16[768,1024]{1,0:T(8,128)(2,1)} %get-tuple-element.27.partner_ref), channel_id=1, source_target_pairs={{0,1},{1,0},{2,3},{3,2},{4,5},{5,4},{6,7},{7,6},{8,9},{9,8},{10,11... | collective-permute-start | bytes 4718600 | tf_op jit(solution)/shard_map/ppermute | solution.py:371
  41.4 0.6 copy-start.12
  41.9 45.4 %collective-permute-start.3 = (bf16[512,1024]{1,0:T(8,128)(2,1)}, bf16[512,1024]{1,0:T(8,128)(2,1)}, u32[]{:S(2)}, u32[]{:S(2)}) collective-permute-start(bf16[512,1024]{1,0:T(8,128)(2,1)} %get-tuple-element.26), channel_id=1, source_target_pairs={{0,2},{1,127},{2,4},{3,1},{4,6},{5,3},{6,8},{7,5},{8,10},{9,7},{10... | collective-permute-start | bytes 3145736 | tf_op jit(solution)/shard_map/ppermute | solution.py:371
  41.9 20.6 %collective-permute-start.2 = (s32[1,768]{1,0:T(1,128)S(1)}, s32[1,768]{1,0:T(1,128)S(1)}, u32[]{:S(2)}, u32[]{:S(2)}) collective-permute-start(s32[1,768]{1,0:T(1,128)S(1)} %reshape.23.col_ids), channel_id=1, source_target_pairs={{0,2},{1,127},{2,4},{3,1},{4,6},{5,3},{6,8},{7,5},{8,10},{9,7},{10... | collective-permute-start | bytes 9224 | tf_op jit(solution)/shard_map/ppermute | solution.py:371
  42.0 22.5 %collective-permute-start.5 = (s32[1,768]{1,0:T(1,128)S(1)}, s32[1,768]{1,0:T(1,128)S(1)}, u32[]{:S(2)}, u32[]{:S(2)}) collective-permute-start(s32[1,768]{1,0:T(1,128)S(1)} %reshape.23.col_ids), channel_id=1, source_target_pairs={{0,127},{1,2},{2,1},{3,4},{4,3},{5,6},{6,5},{7,8},{8,7},{9,10},{10... | collective-permute-start | bytes 9224 | tf_op jit(solution)/shard_map/ppermute | solution.py:371
  62.6 0.6 copy-start.15
  62.6 1.9 %collective-permute-start.8 = (s32[1,768]{1,0:T(1,128)S(1)}, s32[1,768]{1,0:T(1,128)S(1)}, u32[]{:S(2)}, u32[]{:S(2)}) collective-permute-start(s32[1,768]{1,0:T(1,128)S(1)} %reshape.23.col_ids), channel_id=1, source_target_pairs={{0,1},{1,0},{2,3},{3,2},{4,5},{5,4},{6,7},{7,6},{8,9},{9,8},{10,11... | collective-permute-start | bytes 9224 | tf_op jit(solution)/shard_map/ppermute | solution.py:371
  64.5 15.6 %collective-permute-start.6 = (s32[1,768]{1,0:T(1,128)S(1)}, s32[1,768]{1,0:T(1,128)S(1)}, u32[]{:S(2)}, u32[]{:S(2)}) collective-permute-start(s32[1,768]{1,0:T(1,128)S(1)} %collective-permute-done.5.col_ids), channel_id=1, source_target_pairs={{0,1},{1,0},{2,3},{3,2},{4,5},{5,4},{6,7},{7,6},{8,9},{9,8},{10,11... | collective-permute-start | bytes 9224 | tf_op jit(solution)/shard_map/ppermute | solution.py:371
  64.5 28.1 %collective-permute-start.1 = (bf16[256,1024]{1,0:T(8,128)(2,1)}, bf16[256,1024]{1,0:T(8,128)(2,1)S(1)}, u32[]{:S(2)}, u32[]{:S(2)}) collective-permute-start(bf16[256,1024]{1,0:T(8,128)(2,1)} %copy-done.11), channel_id=1, source_target_pairs={{0,2},{1,127},{2,4},{3,1},{4,6},{5,3},{6,8},{7,5},{8,10},{9,7},{10... | collective-permute-start | bytes 1572872 | tf_op jit(solution)/shard_map/ppermute | solution.py:371
  64.7 0.7 copy-start.13
  87.4 5.1 %copy-start.2 = (bf16[1024,768]{1,0:T(8,128)(2,1)S(1)}, bf16[1024,768]{1,0:T(8,128)(2,1)}, u32[]{:S(2)}) copy-start(bf16[1024,768]{1,0:T(8,128)(2,1)} %copy-done.1) | copy-start | bytes 4718596
  87.4 5.1 %copy-start.4 = (f32[768,1]{1,0:T(8,128)S(1)}, f32[768,1]{1,0:T(8,128)}, u32[]{:S(2)}) copy-start(f32[768,1]{1,0:T(8,128)} %copy-done.3) | copy-start | bytes 9220
  100.1 10.2 %copy-start.9 = (bf16[768,1024]{1,0:T(8,128)(2,1)}, bf16[768,1024]{1,0:T(8,128)(2,1)S(1)}, u32[]{:S(2)}) copy-start(bf16[768,1024]{1,0:T(8,128)(2,1)S(1)} %get-tuple-element.43.dproj_ref) | copy-start | bytes 4718596
  100.1 8.4 %collective-permute-start.9 = (bf16[512,1024]{1,0:T(8,128)(2,1)S(1)}, bf16[512,1024]{1,0:T(8,128)(2,1)S(1)}, u32[]{:S(2)}, u32[]{:S(2)}) collective-permute-start(bf16[512,1024]{1,0:T(8,128)(2,1)S(1)} %get-tuple-element.41), channel_id=1, source_target_pairs={{0,1},{1,0},{2,3},{3,2},{4,5},{5,4},{6,7},{7,6},{8,9},{9,8},{10,11... | collective-permute-start | bytes 3145736 | tf_op jit(solution)/shard_map/ppermute | solution.py:371
  106.3 2.3 %collective-permute-start.10 = (f32[8,128]{1,0:T(8,128)S(1)}, f32[8,128]{1,0:T(8,128)S(1)}, u32[]{:S(2)}, u32[]{:S(2)}) collective-permute-start(f32[8,128]{1,0:T(8,128)S(1)} %get-tuple-element.35.loss_in.loss_ref), channel_id=1, source_target_pairs={{0,1},{1,0},{2,3},{3,2},{4,5},{5,4},{6,7},{7,6},{8,9},{9,8},{10,11... | collective-permute-start | bytes 12296 | tf_op jit(solution)/shard_map/ppermute | solution.py:371
  110.3 4.8 %copy-start.7 = (bf16[1024,1024]{1,0:T(8,128)(2,1)S(1)}, bf16[1024,1024]{1,0:T(8,128)(2,1)}, u32[]{:S(2)}) copy-start(bf16[1024,1024]{1,0:T(8,128)(2,1)} %w_ref.5) | copy-start | bytes 6291460
  110.3 26.0 %all-to-all-start = ((bf16[64,8,1152]{2,1,0:T(8,128)(2,1)}), bf16[64,8,1152]{2,1,0:T(8,128)(2,1)S(1)}, u32[]{:S(2)}, u32[]{:S(2)}) async-start(bf16[64,8,1152]{2,1,0:T(8,128)(2,1)} %bitcast.1), calls=%async_computation | async-start | bytes 2359296 | tf_op jit(solution)/shard_map/all_to_all | solution.py:424
  115.1 1.4 %copy-start.10 = (bf16[768,1024]{1,0:T(8,128)(2,1)S(1)}, bf16[768,1024]{1,0:T(8,128)(2,1)}, u32[]{:S(2)}) copy-start(bf16[768,1024]{1,0:T(8,128)(2,1)} %copy-done.9) | copy-start | bytes 4718596

commit v2 on v0

v2 whole, which is shorter than its diff:
```python
import functools

import jax
import jax.numpy as jnp
from jax import lax
from jax.experimental import pallas as pl
from jax.experimental.pallas import tpu as pltpu
from jax.sharding import PartitionSpec as P

ROWS = 768
DIM = 1024
STEP = 256
GROUP = 256
FIRST = 256
SECOND = ROWS - FIRST
LABELS = 16
PIECE = 128
LANES = 128
MIB = 1 << 20

NT = (((1,), (1,)), ((), ()))
TN = (((0,), (0,)), ((), ()))

VMEM = pl.BlockSpec(memory_space=pltpu.VMEM)
SCALARS = pl.BlockSpec(memory_space=pltpu.SMEM)
ANY = pl.BlockSpec(memory_space=pl.ANY)
HBM = pl.BlockSpec(memory_space=pltpu.HBM)


def params(mib):
    return pltpu.CompilerParams(vmem_limit_bytes=mib * MIB)


def cost(flops, moved):
    return pl.CostEstimate(flops=flops, bytes_accessed=moved, transcendentals=0)


def shape(rows, cols, kind=jnp.float32):
    return jax.ShapeDtypeStruct((rows, cols), kind)


BLOCK_SHAPE = [shape(FIRST + LABELS, DIM, jnp.bfloat16), shape(SECOND, DIM, jnp.bfloat16)]


def normalised(x, w):
    projected = jnp.dot(x, w, preferred_element_type=jnp.float32)
    inverse = lax.rsqrt(DIM * (jnp.mean(projected * projected, axis=1, keepdims=True) + 1e-06))
    return projected * inverse, inverse


def id_row(label_ref):
    return jnp.concatenate([label_ref[i : i + 1, :] for i in range(ROWS // LANES)], axis=1)


def label_rows(label_ref):
    ids = id_row(label_ref)
    ids = jnp.concatenate([ids, jnp.zeros((1, DIM - ROWS), jnp.int32)], axis=1)
    high = (ids >> 8).astype(jnp.float32)
    low = (ids & 255).astype(jnp.float32)
    place = lax.broadcasted_iota(jnp.int32, (LABELS, DIM), 0)
    return jnp.where(place == 0, high, jnp.where(place == 1, low, 0.0)).astype(jnp.bfloat16)


def ids_of(first_ref):
    rows = first_ref[first_ref.shape[0] - LABELS :, :ROWS].astype(jnp.float32)
    return 256.0 * rows[:1] + rows[1:2]


def project_kernel(x_hbm, w_hbm, label_ref, first_ref, second_ref, x_ref, w_ref, x_sems, w_sems):
    heads, groups = [], []
    for number, start in enumerate(range(0, DIM, STEP)):
        rows = pl.ds(start, STEP)
        heads.append(
            pltpu.make_async_copy(w_hbm.at[rows], w_ref.at[rows], w_sems.at[number])
        )
        heads[-1].start()
    for number, start in enumerate(range(0, ROWS, GROUP)):
        rows = pl.ds(start, GROUP)
        groups.append(
            pltpu.make_async_copy(x_hbm.at[rows], x_ref.at[rows], x_sems.at[number])
        )
        groups[-1].start()
    first_ref[FIRST:, :] = label_rows(label_ref)
    for head in heads:
        head.wait()
    for number, start in enumerate(range(0, ROWS, GROUP)):
        groups[number].wait()
        unit, _ = normalised(x_ref[start : start + GROUP, :], w_ref[...])
        ref, at = (first_ref, start) if start < FIRST else (second_ref, start - FIRST)
        ref[at : at + GROUP, :] = unit.astype(jnp.bfloat16)


def project(x, w, label):
    return pl.pallas_call(
        project_kernel,
        in_specs=[HBM, HBM, VMEM],
        out_specs=[VMEM] * 2,
        out_shape=BLOCK_SHAPE,
        scratch_shapes=[
            pltpu.VMEM((ROWS, DIM), jnp.bfloat16),
            pltpu.VMEM((DIM, DIM), jnp.bfloat16),
            pltpu.SemaphoreType.DMA((ROWS // GROUP,)),
            pltpu.SemaphoreType.DMA((DIM // STEP,)),
        ],
        compiler_params=params(62),
        cost_estimate=cost(2 * ROWS * DIM * DIM, 5 * MIB),
    )(x, w, label)


def slopes_of(cosine, row_ids, col_ids, scale, shift, with_loss):
    logits = scale * cosine + shift
    same = row_ids == col_ids
    signed = jnp.where(same, -logits, logits)
    if not with_loss:
        gate = 1.0 / (1.0 + jnp.exp(-signed))
        return jnp.where(same, -gate, gate).astype(jnp.bfloat16), None
    decay = jnp.exp(-jnp.abs(signed))
    share = 1.0 / (1.0 + decay)
    gate = jnp.where(signed >= 0, share, decay * share)
    slopes = jnp.where(same, -gate, gate).astype(jnp.bfloat16)
    while decay.shape[0] > STEP // 8:
        half = decay.shape[0] // 2
        above, below = decay[:half], decay[half:]
        decay = above + below + above * below
    return slopes, lane_sums(jnp.maximum(signed, 0.0)) + lane_sums(jnp.log1p(decay))


def lane_sums(losses):
    rows, cols = losses.shape
    by_tile = losses.reshape(rows // 8, 8, cols).sum(axis=0)
    total = by_tile[:, :LANES]
    for start in range(LANES, cols, LANES):
        total = total + by_tile[:, start : start + LANES]
    return total


def own_rows(own, start):
    first_ref, second_ref = own
    if start + STEP <= FIRST:
        return first_ref[start : start + STEP, :]
    if start >= FIRST:
        return second_ref[start - FIRST : start - FIRST + STEP, :]
    return jnp.concatenate([first_ref[start:FIRST, :], second_ref[: start + STEP - FIRST, :]], axis=0)


def tile_pieces(scalars, own, partner, row_ids, col_ids, with_loss):
    scale, shift = scalars[0], scalars[1]
    count = sum(part.shape[0] for part in partner)

    def cosine_of(start):
        rows = own_rows(own, start)
        parts = [
            lax.dot_general(rows, part, NT, preferred_element_type=jnp.float32) for part in partner
        ]
        return parts[0] if len(parts) == 1 else jnp.concatenate(parts, axis=1)

    cosine = cosine_of(0)
    for start in range(0, ROWS, STEP):
        ahead = cosine_of(start + STEP) if start + STEP < ROWS else None
        ids = jnp.concatenate([row_ids[start : start + STEP, :]] * (count // LANES), axis=1)
        slopes, loss = slopes_of(cosine, ids, col_ids, scale, shift, with_loss)
        piece, at = None, 0
        for part in partner:
            term = jnp.dot(
                slopes[:, at : at + part.shape[0]], part, preferred_element_type=jnp.float32
            )
            piece = term if piece is None else piece + term
            at += part.shape[0]
        yield pl.ds(start, STEP), piece, loss
        cosine = ahead


def both(first_ref, second_ref):
    return [first_ref[:FIRST, :], second_ref[...]]


def own_tile_kernel(
    scalars, first_ref, second_ref, ids_ref, sum_ref, loss_ref, first_out, second_out
):
    first_out[...] = first_ref[...]
    second_out[...] = second_ref[...]
    ids = ids_of(first_ref)
    ids_ref[...] = jnp.broadcast_to(ids, (LANES, ROWS)).T
    own = (first_ref, second_ref)
    total = jnp.zeros((8, LANES), jnp.float32)
    for rows, piece, loss in tile_pieces(scalars, own, both(*own), ids_ref, ids, True):
        sum_ref[rows, :] = 2.0 * piece
        total = total + loss
    loss_ref[...] = total


def own_tile(scalars, own):
    return pl.pallas_call(
        own_tile_kernel,
        in_specs=[SCALARS] + [VMEM] * 2,
        out_specs=[VMEM] * 5,
        out_shape=[shape(ROWS, LANES), shape(ROWS, DIM), shape(8, LANES)] + BLOCK_SHAPE,
        compiler_params=params(12),
        cost_estimate=cost(4 * ROWS * ROWS * DIM, 5 * MIB),
    )(scalars, *own)


def partner_tile_kernel(
    weight, forward, cols, scalars, first_ref, second_ref, ids, sum_in, loss_in, labels, *rest
):
    first, last, takes = cols
    parts = rest[: len(takes)]
    outs = rest[len(rest) - 2 - forward :]
    sum_ref, loss_ref = outs[:2]
    for number in range(forward):
        held = outs[2 + number]
        held[...] = parts[0][PIECE * number : PIECE * number + held.shape[0], :]
    col_ids = ids_of(labels)[:, first:last]
    partner = [part[:take, :] for part, take in zip(parts, takes)]
    if len(parts) > 1:
        partner = [jnp.concatenate(partner, axis=0)]
    total = loss_in[...]
    for rows, piece, loss in tile_pieces(
        scalars, (first_ref, second_ref), partner, ids, col_ids, weight is not None
    ):
        sum_ref[rows, :] = sum_in[rows, :] + piece
        if weight is not None:
            total = total + weight * loss
    loss_ref[...] = total


def pieces_of(part):
    count = part.shape[0] // PIECE
    sizes = [PIECE] * (count - 1) + [part.shape[0] - PIECE * (count - 1)]
    return [shape(size, DIM, jnp.bfloat16) for size in sizes]


def partner_tile(weight, forward, scalars, own, partner, cols, ids, summed, loss, labels, after=()):
    passed = pieces_of(partner[0]) if forward else []
    takes = tuple(part.shape[0] // PIECE * PIECE for part in partner)
    return pl.pallas_call(
        functools.partial(partner_tile_kernel, weight, len(passed), (*cols, takes)),
        in_specs=[SCALARS] + [VMEM] * (6 + len(partner)) + [ANY] * len(after),
        out_specs=[VMEM] * (2 + len(passed)),
        out_shape=[shape(ROWS, DIM), shape(8, LANES)] + passed,
        compiler_params=params(12),
        cost_estimate=cost(4 * ROWS * (cols[1] - cols[0]) * DIM, 10 * MIB),
    )(scalars, *own, ids, summed, loss, labels, *partner, *after)


def unit_kernel(x_ref, w_ref, after, unit_ref, inverse_ref):
    for start in range(0, ROWS, STEP):
        rows = pl.ds(start, STEP)
        unit, inverse = normalised(x_ref[rows, :], w_ref[...])
        unit_ref[rows, :] = unit
        inverse_ref[rows, :] = jnp.broadcast_to(inverse, (STEP, LANES))


def unit_rows(x, w, after):
    return pl.pallas_call(
        unit_kernel,
        in_specs=[VMEM] * 2 + [ANY],
        out_specs=[VMEM] * 2,
        out_shape=[shape(ROWS, DIM), shape(ROWS, LANES)],
        compiler_params=params(12),
        cost_estimate=cost(2 * ROWS * DIM * DIM, 7 * MIB),
    )(x, w, after)


def last_kernel(
    scalars,
    first_ref,
    second_ref,
    far_first,
    far_ref,
    ids,
    sum_in,
    unit_ref,
    inverse_ref,
    x_ref,
    dproj_ref,
    kept_ref,
    sent_ref,
):
    col_ids = ids_of(far_first)[:, FIRST:]
    for rows, piece, _ in tile_pieces(
        scalars, (first_ref, second_ref), [far_ref[...]], ids, col_ids, False
    ):
        unit = unit_ref[rows, :]
        dunit = scalars[0] * (sum_in[rows, :] + piece)
        radial = jnp.sum(dunit * unit, axis=1, keepdims=True)
        inverse = inverse_ref[rows, :][:, :1]
        dproj_ref[rows, :] = ((dunit - unit * radial) * inverse).astype(jnp.bfloat16)
    first = lax.axis_index("batch") % 2 == 0
    for start in range(0, DIM, STEP):
        product = lax.dot_general(
            x_ref[:, start : start + STEP], dproj_ref[...], TN, preferred_element_type=jnp.float32
        ).reshape(STEP // 16, 2, 8, DIM)
        even, odd = product[:, 0], product[:, 1]
        rows = pl.ds(start // 2, STEP // 2)
        kept_ref[rows, :] = jnp.where(first, even, odd).reshape(STEP // 2, DIM)
        sent_ref[rows, :] = (
            jnp.where(first, odd, even).reshape(STEP // 2, DIM).astype(jnp.bfloat16)
        )


def last(scalars, own, far, ids, summed, unit, inverse, x):
    return pl.pallas_call(
        last_kernel,
        in_specs=[SCALARS] + [VMEM] * 9,
        out_specs=[VMEM] * 3,
        out_shape=[
            shape(ROWS, DIM, jnp.bfloat16),
            shape(DIM // 2, DIM),
            shape(DIM // 2, DIM, jnp.bfloat16),
        ],
        compiler_params=params(12),
        cost_estimate=cost(4 * ROWS * SECOND * DIM + 2 * ROWS * DIM * DIM, 14 * MIB),
    )(scalars, *own, *far, ids, summed, unit, inverse, x)


def grad_rows_kernel(dproj_ref, w_ref, out_ref):
    for start in range(0, ROWS, STEP):
        rows = pl.ds(start, STEP)
        out_ref[rows, :] = lax.dot_general(
            dproj_ref[rows, :], w_ref[...], NT, preferred_element_type=jnp.float32
        ).astype(jnp.bfloat16)


def grad_rows_of(dproj, w):
    return pl.pallas_call(
        grad_rows_kernel,
        in_specs=[VMEM] * 2,
        out_specs=VMEM,
        out_shape=shape(ROWS, DIM, jnp.bfloat16),
        compiler_params=params(12),
        cost_estimate=cost(2 * ROWS * DIM * DIM, 5 * MIB),
    )(dproj, w)


def packed_kernel(kept_ref, received_ref, loss_ref, other_loss_ref, out_ref):
    out_ref[:, :DIM] = (kept_ref[...] + received_ref[...].astype(jnp.float32)).astype(jnp.bfloat16)
    lanes = jnp.sum(loss_ref[...] + other_loss_ref[...], axis=0, keepdims=True)
    high = lanes.astype(jnp.bfloat16).astype(jnp.float32)
    middle = (lanes - high).astype(jnp.bfloat16).astype(jnp.float32)
    low = lanes - high - middle
    place = lax.broadcasted_iota(jnp.int32, (16, LANES), 0) % 8
    tile = jnp.where(
        place == 0, high, jnp.where(place == 1, middle, jnp.where(place == 2, low, 0.0))
    ).astype(jnp.bfloat16)
    for start in range(0, out_ref.shape[0], 16):
        out_ref[start : start + 16, DIM:] = tile


def packed(kept, received, loss, other_loss):
    return pl.pallas_call(
        packed_kernel,
        in_specs=[VMEM] * 4,
        out_specs=VMEM,
        out_shape=shape(DIM // 2, DIM + LANES, jnp.bfloat16),
        compiler_params=params(12),
        cost_estimate=cost(DIM * DIM, 5 * MIB),
    )(kept, received, loss, other_loss)


def finish_kernel(tokens, parts_ref, head_ref, loss_ref):
    total = parts_ref[0].astype(jnp.float32)
    for part in range(1, parts_ref.shape[0]):
        total = total + parts_ref[part].astype(jnp.float32)
    head_ref[...] = total[:, :DIM]
    loss_ref[...] = jnp.sum(total[:, DIM:]).reshape(1, 1) / tokens


def finish(parts, tokens):
    return pl.pallas_call(
        functools.partial(finish_kernel, tokens),
        in_specs=[VMEM],
        out_specs=[VMEM] * 2,
        out_shape=[shape(8, DIM), shape(1, 1)],
        compiler_params=params(12),
        cost_estimate=cost(DIM * DIM, 2 * MIB),
    )(parts)


def on_device(x, w, label, score_scale, score_shift):
    count = lax.axis_size("batch")

    def move(value, target):
        return lax.ppermute(value, "batch", [(i, target(i) % count) for i in range(count)])

    def pair(i):
        return i ^ 1

    def near(i):
        return i + 1 if i & 1 else i - 1

    def far(i):
        return i - 2 if i & 1 else i + 2

    own = project(x, w, label.reshape(ROWS // LANES, LANES))
    near_first = move(own[0], near)
    near_second = move(own[1], near)
    paired = [move(part, pair) for part in own]

    scalars = jnp.concatenate([score_scale, score_shift])
    ids, summed, loss, *again = own_tile(scalars, own)
    far_first = move(again[0], far)
    far_second = move(again[1], far)
    own = again
    tile = functools.partial(partner_tile, scalars=scalars, own=own, ids=ids)
    whole, early, late = (0, ROWS), (0, FIRST), (FIRST, ROWS)
    summed, loss = tile(
        0.5, False, partner=paired, cols=whole, summed=summed, loss=loss, labels=paired[0]
    )
    unit, inverse = unit_rows(x, w, loss)
    summed, loss, *passed = tile(
        0.5,
        True,
        partner=[near_first],
        cols=early,
        summed=summed,
        loss=loss,
        labels=near_first,
        after=(inverse,),
    )
    third_first = [move(piece, pair) for piece in passed]
    summed, loss = tile(
        1.0,
        False,
        partner=third_first,
        cols=early,
        summed=summed,
        loss=loss,
        labels=third_first[-1],
    )
    summed, loss = tile(
        None, False, partner=[far_first], cols=early, summed=summed, loss=loss, labels=far_first
    )
    summed, loss, *passed = tile(
        0.5, True, partner=[near_second], cols=late, summed=summed, loss=loss, labels=near_first
    )
    third_second = [move(piece, pair) for piece in passed]
    summed, loss = tile(
        1.0,
        False,
        partner=third_second,
        cols=late,
        summed=summed,
        loss=loss,
        labels=third_first[-1],
    )
    other_loss = move(loss, pair)
    dproj, kept, sent = last(
        scalars, own, [far_first, far_second], ids, summed, unit, inverse, x
    )
    received = move(sent, pair)
    grad_rows = grad_rows_of(dproj, w)
    chips = count // 2
    groups = [[2 * chip + core for chip in range(chips)] for core in range(2)]
    parts = packed(kept, received, loss, other_loss).reshape(chips, 8, DIM + LANES)
    parts = lax.all_to_all(parts, "batch", 0, 0, tiled=True, axis_index_groups=groups)
    grad_head, total = finish(parts, float(ROWS * count))
    return (total.reshape(()), grad_rows, grad_head)


def solution(mesh):
    placed = (P("batch", None), P(), P("batch"), P(), P())
    return jax.shard_map(
        on_device,
        mesh=mesh,
        in_specs=placed,
        out_specs=(P(), P("batch", None), P("batch", None)),
        check_vma=False,
    )
```

time: 814 us -> 93 us (0.11)
  waiting for transfers between devices: 660 us -> 21.8 us
  blocking collectives: 68.6 us -> 0 us
  matrix products: 38.5 us -> 0 us
  Pallas kernels: 0 us -> 37.7 us
  between operations: 19.1 us -> 2.15 us
  starting transfers between devices: 11.7 us -> 26.1 us
    unnamed x2 -> x0, waiting for transfers between devices: 570 us -> none
    ppermute x6 -> x14, waiting for transfers between devices: 90.3 us -> 5.3 us  [move(): lax.ppermute(value, 'batch', [(i, target(i) % count) for i in range(count)])]
    psum x1 -> x0, blocking collectives: 68.6 us -> none  [on_device(): lax.psum(running, 'batch')]
    dot_general x12 -> x0, matrix products: 38.5 us -> none  [the longest x3 11.5 us: tile_terms(): lax.dot_general(rows_emb, column_embedding_vectors, (((1,), (1,)), ((), (...]
    pallas_call x0 -> x13, Pallas kernels: none -> 37.7 us  [the longest x6 16 us: partner_tile(): pl.pallas_call(functools.partial(partner_tile_kernel, weight, len(passed)...]
    all_to_all x0 -> x1, waiting for transfers between devices: none -> 16.5 us  [on_device(): lax.all_to_all(parts, 'batch', 0, 0, tiled=True, axis_index_groups=groups)]
    ppermute x6 -> x14, starting transfers between devices: 11.6 us -> 18.4 us  [move(): lax.ppermute(value, 'batch', [(i, target(i) % count) for i in range(count)])]
  transfers between devices with their start and end apart: 7 -> 15, of which waited for: 5 -> 7; matrix products, arithmetic and copies ran while one was open for 3% -> 0% of each run, Pallas kernels for 0% -> 27%
where the time goes in v2:
time: 93 us; the launch traced here: 92.6 us
  Pallas kernels  37.7 us (41%)
  starting transfers between devices  26.1 us (28%)
  waiting for transfers between devices  21.8 us (23%)
  local copies, waits for them, and re-layouts  4.83 us (5%)
  between operations  2.15 us (2%)
    ppermute x14, starting transfers between devices, move(): lax.ppermute(value, 'batch', [(i, target(i) % count) for i in range(count)])  18.4 us
    all_to_all x1, waiting for transfers between devices, on_device(): lax.all_to_all(parts, 'batch', 0, 0, tiled=True, axis_index_groups=groups)  16.5 us
    pallas_call x6, Pallas kernels, partner_tile(): pl.pallas_call(functools.partial(partner_tile_kernel, weight, len(passed)...  16 us
    all_to_all x1, starting transfers between devices, on_device(): lax.all_to_all(parts, 'batch', 0, 0, tiled=True, axis_index_groups=groups)  7.67 us
    pallas_call x1, Pallas kernels, project(): pl.pallas_call(project_kernel, in_specs=[HBM, HBM, VMEM], out_specs=[VMEM...  5.98 us
    ppermute x14, waiting for transfers between devices, move(): lax.ppermute(value, 'batch', [(i, target(i) % count) for i in range(count)])  5.3 us
    pallas_call x1, Pallas kernels, last(): pl.pallas_call(last_kernel, in_specs=[SCALARS] + [VMEM] * 9, out_specs=[V...  4.84 us
    unnamed x12, local copies, waits for them, and re-layouts  4.83 us
  transfers between devices with their start and end apart: 15, of which 7 were waited for; matrix products, arithmetic and copies ran while one was open for 0% of the time, Pallas kernels for 27%

profile of v2, /device:TPU:0, one launch (start us, length us, event | category | flops | bytes accessed | tf_op | source)
XLA Modules:
  0.0 92.6 jit_solution(15695687761239428527)
XLA Ops:
  0.6 6.0 %shard_map.76 = (bf16[272,1024]{1,0:T(8,128)(2,1)}, bf16[512,1024]{1,0:T(8,128)(2,1)}) custom-call(bf16[768,1024]{1,0:T(8,128)(2,1)} %x_ref.3, bf16[1024,1024]{1,0:T(8,128)(2,1)} %w_ref.3, s32[6,128]{1,0:T(8,128)} %bitcast.3), custom_call_target="tpu_custom_call" | custom-call | flops 1610612736 | bytes 5242880 | tf_op jit(solution)/shard_map/pallas_call | solution.py:94
  6.6 0.1 collective-permute-start.3
  6.7 0.5 collective-permute-start.2
  7.2 8.5 %collective-permute-start.4 = (bf16[272,1024]{1,0:T(8,128)(2,1)}, bf16[272,1024]{1,0:T(8,128)(2,1)S(1)}, u32[]{:S(2)}, u32[]{:S(2)}) collective-permute-start(bf16[272,1024]{1,0:T(8,128)(2,1)} %get-tuple-element.35.first_ref), channel_id=1, source_target_pairs={{0,127},{1,2},{2,1},{3,4},{4,3},{5,6},{6,5},{7,8},{8,7},{9,10},{10... | collective-permute-start | bytes 1671176 | tf_op jit(solution)/shard_map/ppermute | solution.py:384
  15.7 0.0 collective-permute-start.7
  17.0 0.1 pad_maximum_fusion.scalars
  17.1 1.2 %copy-done.2 = bf16[512,1024]{1,0:T(8,128)(2,1)S(1)} copy-done((bf16[512,1024]{1,0:T(8,128)(2,1)S(1)}, bf16[512,1024]{1,0:T(8,128)(2,1)}, u32[]{:S(2)}) %copy-start.2) | copy-done | bytes 1048600
  18.3 1.1 %copy-done.3 = bf16[272,1024]{1,0:T(8,128)(2,1)S(1)} copy-done((bf16[272,1024]{1,0:T(8,128)(2,1)S(1)}, bf16[272,1024]{1,0:T(8,128)(2,1)}, u32[]{:S(2)}) %copy-start.3) | copy-done | bytes 557080
  19.4 3.9 %shard_map.77 = (f32[768,128]{1,0:T(8,128)S(1)}, f32[768,1024]{1,0:T(8,128)S(1)}, f32[8,128]{1,0:T(8,128)S(1)}, bf16[272,1024]{1,0:T(8,128)(2,1)S(1)}, bf16[512,1024]{1,0:T(8,128)(2,1)S(1)}) custom-call(f32[2]{0:T(128)S(1)} %pad_maximum_fusion.scalars, bf16[272,1024]{1,0:T(8,128)(2,1)S(1)} %copy-done.3, bf16[512,1024]{1,0:T(8,128)(2,1)S(1)} %copy-done.2), custom_call_target="tpu_custom_call" | custom-call | flops 2415919104 | bytes 5242880 | tf_op jit(solution)/shard_map/pallas_call | solution.py:193
  23.3 0.1 collective-permute-start
  23.4 0.0 collective-permute-done.2.labels.rest_0_
  23.4 0.3 collective-permute-start.1
  23.7 0.0 collective-permute-done.3.rest_1_
  23.7 0.0 copy-start
  23.7 0.0 copy-start.1
  23.7 3.8 %shard_map.78 = (f32[768,1024]{1,0:T(8,128)S(1)}, f32[8,128]{1,0:T(8,128)S(1)}) custom-call(f32[2]{0:T(128)S(1)} %pad_maximum_fusion.scalars, bf16[272,1024]{1,0:T(8,128)(2,1)S(1)} %get-tuple-element.37.first_ref, bf16[512,1024]{1,0:T(8,128)(2,1)S(1)} %get-tuple-element.38.second_ref, f32[768,128]{1,0:T(8,128)S(1)} %get-tuple-element.39.ids, ...), custom_call_target="tpu_custom_call" | custom-call | flops 2415919104 | bytes 10485760 | tf_op jit(solution)/shard_map/pallas_call | solution.py:236
  27.5 2.0 %shard_map.79 = (f32[768,1024]{1,0:T(8,128)S(1)}, f32[768,128]{1,0:T(8,128)S(1)}) custom-call(bf16[768,1024]{1,0:T(8,128)(2,1)S(1)} %copy-done.1, bf16[1024,1024]{1,0:T(8,128)(2,1)S(1)} %copy-done, f32[8,128]{1,0:T(8,128)S(1)} %get-tuple-element.43.after.loss_in), custom_call_target="tpu_custom_call" | custom-call | flops 1610612736 | bytes 7340032 | tf_op jit(solution)/shard_map/pallas_call | solution.py:255
  29.5 0.0 collective-permute-done.4.labels.rest_0_
  29.5 2.2 %shard_map.80 = (f32[768,1024]{1,0:T(8,128)S(1)}, f32[8,128]{1,0:T(8,128)S(1)}, bf16[128,1024]{1,0:T(8,128)(2,1)S(1)}, bf16[144,1024]{1,0:T(8,128)(2,1)S(1)}) custom-call(f32[2]{0:T(128)S(1)} %pad_maximum_fusion.scalars, bf16[272,1024]{1,0:T(8,128)(2,1)S(1)} %get-tuple-element.37.first_ref, bf16[512,1024]{1,0:T(8,128)(2,1)S(1)} %get-tuple-element.38.second_ref, ...), custom_call_target="tpu_custom_call" | custom-call | flops 805306368 | bytes 10485760 | tf_op jit(solution)/shard_map/pallas_call | solution.py:236
  31.8 7.3 %collective-permute-start.5 = (bf16[144,1024]{1,0:T(8,128)(2,1)S(1)}, bf16[144,1024]{1,0:T(8,128)(2,1)S(1)}, u32[]{:S(2)}, u32[]{:S(2)}) collective-permute-start(bf16[144,1024]{1,0:T(8,128)(2,1)S(1)} %get-tuple-element.47), channel_id=1, source_target_pairs={{0,1},{1,0},{2,3},{3,2},{4,5},{5,4},{6,7},{7,6},{8,9},{9,8},{10,11... | collective-permute-start | bytes 884744 | tf_op jit(solution)/shard_map/ppermute | solution.py:384
  39.0 0.1 collective-permute-start.6
  39.1 1.5 %collective-permute-done.6.rest_0_ = bf16[128,1024]{1,0:T(8,128)(2,1)S(1)} collective-permute-done((bf16[128,1024]{1,0:T(8,128)(2,1)S(1)}, bf16[128,1024]{1,0:T(8,128)(2,1)S(1)}, u32[]{:S(2)}, u32[]{:S(2)}) %collective-permute-start.6) | collective-permute-done | bytes 262176 | tf_op jit(solution)/shard_map/ppermute | solution.py:384
  40.6 0.0 collective-permute-done.5.labels.rest_1_
  40.6 2.2 %shard_map.81 = (f32[768,1024]{1,0:T(8,128)S(1)}, f32[8,128]{1,0:T(8,128)S(1)}) custom-call(f32[2]{0:T(128)S(1)} %pad_maximum_fusion.scalars, bf16[272,1024]{1,0:T(8,128)(2,1)S(1)} %get-tuple-element.37.first_ref, bf16[512,1024]{1,0:T(8,128)(2,1)S(1)} %get-tuple-element.38.second_ref, f32[768,128]{1,0:T(8,128)S(1)} %get-tuple-element.39.ids, ...), custom_call_target="tpu_custom_call" | custom-call | flops 805306368 | bytes 10485760 | tf_op jit(solution)/shard_map/pallas_call | solution.py:236
  42.8 1.9 %shard_map.82 = (f32[768,1024]{1,0:T(8,128)S(1)}, f32[8,128]{1,0:T(8,128)S(1)}) custom-call(f32[2]{0:T(128)S(1)} %pad_maximum_fusion.scalars, bf16[272,1024]{1,0:T(8,128)(2,1)S(1)} %get-tuple-element.37.first_ref, bf16[512,1024]{1,0:T(8,128)(2,1)S(1)} %get-tuple-element.38.second_ref, f32[768,128]{1,0:T(8,128)S(1)} %get-tuple-element.39.ids, ...), custom_call_target="tpu_custom_call" | custom-call | flops 805306368 | bytes 10485760 | tf_op jit(solution)/shard_map/pallas_call | solution.py:236
  44.8 2.9 %shard_map.83 = (f32[768,1024]{1,0:T(8,128)S(1)}, f32[8,128]{1,0:T(8,128)S(1)}, bf16[128,1024]{1,0:T(8,128)(2,1)S(1)}, bf16[128,1024]{1,0:T(8,128)(2,1)S(1)}, bf...) custom-call(f32[2]{0:T(128)S(1)} %pad_maximum_fusion.scalars, ...), custom_call_target="tpu_custom_call" | custom-call | flops 1610612736 | bytes 10485760 | tf_op jit(solution)/shard_map/pallas_call | solution.py:236
  47.7 0.5 collective-permute-start.10
  48.2 0.1 collective-permute-start.11
  48.3 0.4 collective-permute-start.8
  48.7 0.1 collective-permute-start.9
  48.8 0.5 collective-permute-done.10.rest_2_
  49.3 0.4 collective-permute-done.11.rest_3_
  49.7 0.4 collective-permute-done.8.rest_0_
  50.1 0.4 collective-permute-done.9.rest_1_
  50.4 2.9 %shard_map.84 = (f32[768,1024]{1,0:T(8,128)S(1)}, f32[8,128]{1,0:T(8,128)S(1)}) custom-call(f32[2]{0:T(128)S(1)} %pad_maximum_fusion.scalars, bf16[272,1024]{1,0:T(8,128)(2,1)S(1)} %get-tuple-element.37.first_ref, bf16[512,1024]{1,0:T(8,128)(2,1)S(1)} %get-tuple-element.38.second_ref, f32[768,128]{1,0:T(8,128)S(1)} %get-tuple-element.39.ids, ...), custom_call_target="tpu_custom_call" | custom-call | flops 1610612736 | bytes 10485760 | tf_op jit(solution)/shard_map/pallas_call | solution.py:236
  53.4 4.8 %shard_map.85 = (bf16[768,1024]{1,0:T(8,128)(2,1)S(1)}, f32[512,1024]{1,0:T(8,128)S(1)}, bf16[512,1024]{1,0:T(8,128)(2,1)S(1)}) custom-call(f32[2]{0:T(128)S(1)} %pad_maximum_fusion.scalars, bf16[272,1024]{1,0:T(8,128)(2,1)S(1)} %get-tuple-element.37.first_ref, bf16[512,1024]{1,0:T(8,128)(2,1)S(1)} %get-tuple-element.38.second_ref, ...), custom_call_target="tpu_custom_call" | custom-call | flops 3221225472 | bytes 14680064 | tf_op jit(solution)/shard_map/pallas_call | solution.py:303
  58.2 0.0 copy-start.4
  58.2 1.1 %copy-done.4 = bf16[768,1024]{1,0:T(8,128)(2,1)} copy-done((bf16[768,1024]{1,0:T(8,128)(2,1)}, bf16[768,1024]{1,0:T(8,128)(2,1)S(1)}, u32[]{:S(2)}) %copy-start.4) | copy-done | bytes 1572888
  59.4 0.4 collective-permute-start.12
  59.7 0.2 collective-permute-start.13
  59.9 2.2 %collective-permute-done.13.other_loss_ref = f32[8,128]{1,0:T(8,128)S(1)} collective-permute-done((f32[8,128]{1,0:T(8,128)S(1)}, f32[8,128]{1,0:T(8,128)S(1)}, u32[]{:S(2)}, u32[]{:S(2)}) %collective-permute-start.13) | collective-permute-done | bytes 4128 | tf_op jit(solution)/shard_map/ppermute | solution.py:384
  62.0 1.2 %shard_map.86 = bf16[512,1152]{1,0:T(8,128)(2,1)} custom-call(f32[512,1024]{1,0:T(8,128)S(1)} %get-tuple-element.61.kept_ref, bf16[512,1024]{1,0:T(8,128)(2,1)S(1)} %collective-permute-done.12.received_ref, f32[8,128]{1,0:T(8,128)S(1)} %get-tuple-element.63.loss_ref, f32[8,128]{1,0:T(8,128)S(1)} %collective-permute-done.13.other_loss_ref), custom_call_target="tpu_custom_call" | custom-call | flops 1048576 | bytes 5242880 | tf_op jit(solution)/shard_map/pallas_call | solution.py:351
  63.2 7.7 %all-to-all-start = ((bf16[64,8,1152]{2,1,0:T(8,128)(2,1)}), bf16[64,8,1152]{2,1,0:T(8,128)(2,1)S(1)}, u32[]{:S(2)}, u32[]{:S(2)}) async-start(bf16[64,8,1152]{2,1,0:T(8,128)(2,1)} %bitcast.1), calls=%async_computation | async-start | bytes 2359296 | tf_op jit(solution)/shard_map/all_to_all | solution.py:456
  70.9 0.0 copy-start.5
  70.9 1.4 %copy-done.5 = bf16[768,1024]{1,0:T(8,128)(2,1)S(1)} copy-done((bf16[768,1024]{1,0:T(8,128)(2,1)S(1)}, bf16[768,1024]{1,0:T(8,128)(2,1)}, u32[]{:S(2)}) %copy-start.5) | copy-done | bytes 1572888
  72.3 3.0 %shard_map.88 = bf16[768,1024]{1,0:T(8,128)(2,1)} custom-call(bf16[768,1024]{1,0:T(8,128)(2,1)S(1)} %copy-done.5, bf16[1024,1024]{1,0:T(8,128)(2,1)S(1)} %copy-done), custom_call_target="tpu_custom_call" | custom-call | flops 1610612736 | bytes 5242880 | tf_op jit(solution)/shard_map/pallas_call | solution.py:326
  75.3 16.5 %all-to-all-done.parts_ref = bf16[64,8,1152]{2,1,0:T(8,128)(2,1)S(1)} async-done(((bf16[64,8,1152]{2,1,0:T(8,128)(2,1)}), bf16[64,8,1152]{2,1,0:T(8,128)(2,1)S(1)}, u32[]{:S(2)}, u32[]{:S(2)}) %all-to-all-start) | async-done | bytes 1179680 | tf_op jit(solution)/shard_map/all_to_all | solution.py:456
  91.8 0.8 shard_map.87
  (8 shorter events, 0.0 us)
Async XLA Ops:
  6.6 17.1 %collective-permute-start.3 = (bf16[512,1024]{1,0:T(8,128)(2,1)}, bf16[512,1024]{1,0:T(8,128)(2,1)S(1)}, u32[]{:S(2)}, u32[]{:S(2)}) collective-permute-start(bf16[512,1024]{1,0:T(8,128)(2,1)} %get-tuple-element.36.second_ref), channel_id=1, source_target_pairs={{0,1},{1,0},{2,3},{3,2},{4,5},{5,4},{6,7},{7,6},{8,9},{9,8},{10,11... | collective-permute-start | bytes 3145736 | tf_op jit(solution)/shard_map/ppermute | solution.py:384
  6.7 16.7 %collective-permute-start.2 = (bf16[272,1024]{1,0:T(8,128)(2,1)}, bf16[272,1024]{1,0:T(8,128)(2,1)S(1)}, u32[]{:S(2)}, u32[]{:S(2)}) collective-permute-start(bf16[272,1024]{1,0:T(8,128)(2,1)} %get-tuple-element.35.first_ref), channel_id=1, source_target_pairs={{0,1},{1,0},{2,3},{3,2},{4,5},{5,4},{6,7},{7,6},{8,9},{9,8},{10,11... | collective-permute-start | bytes 1671176 | tf_op jit(solution)/shard_map/ppermute | solution.py:384
  7.2 22.3 %collective-permute-start.4 = (bf16[272,1024]{1,0:T(8,128)(2,1)}, bf16[272,1024]{1,0:T(8,128)(2,1)S(1)}, u32[]{:S(2)}, u32[]{:S(2)}) collective-permute-start(bf16[272,1024]{1,0:T(8,128)(2,1)} %get-tuple-element.35.first_ref), channel_id=1, source_target_pairs={{0,127},{1,2},{2,1},{3,4},{4,3},{5,6},{6,5},{7,8},{8,7},{9,10},{10... | collective-permute-start | bytes 1671176 | tf_op jit(solution)/shard_map/ppermute | solution.py:384
  15.7 29.1 %collective-permute-start.7 = (bf16[512,1024]{1,0:T(8,128)(2,1)}, bf16[512,1024]{1,0:T(8,128)(2,1)S(1)}, u32[]{:S(2)}, u32[]{:S(2)}) collective-permute-start(bf16[512,1024]{1,0:T(8,128)(2,1)} %get-tuple-element.36.second_ref), channel_id=1, source_target_pairs={{0,127},{1,2},{2,1},{3,4},{4,3},{5,6},{6,5},{7,8},{8,7},{9,10},{10... | collective-permute-start | bytes 3145736 | tf_op jit(solution)/shard_map/ppermute | solution.py:384
  17.1 1.2 %copy-start.2 = (bf16[512,1024]{1,0:T(8,128)(2,1)S(1)}, bf16[512,1024]{1,0:T(8,128)(2,1)}, u32[]{:S(2)}) copy-start(bf16[512,1024]{1,0:T(8,128)(2,1)} %get-tuple-element.36.second_ref) | copy-start | bytes 3145732
  18.3 1.1 %copy-start.3 = (bf16[272,1024]{1,0:T(8,128)(2,1)S(1)}, bf16[272,1024]{1,0:T(8,128)(2,1)}, u32[]{:S(2)}) copy-start(bf16[272,1024]{1,0:T(8,128)(2,1)} %get-tuple-element.35.first_ref) | copy-start | bytes 1671172
  23.3 19.5 %collective-permute-start = (bf16[272,1024]{1,0:T(8,128)(2,1)S(1)}, bf16[272,1024]{1,0:T(8,128)(2,1)S(1)}, u32[]{:S(2)}, u32[]{:S(2)}) collective-permute-start(bf16[272,1024]{1,0:T(8,128)(2,1)S(1)} %get-tuple-element.37.first_ref), channel_id=1, source_target_pairs={{0,2},{1,127},{2,4},{3,1},{4,6},{5,3},{6,8},{7,5},{8,10},{9,7},{10... | collective-permute-start | bytes 1671176 | tf_op jit(solution)/shard_map/ppermute | solution.py:384
  23.4 29.9 %collective-permute-start.1 = (bf16[512,1024]{1,0:T(8,128)(2,1)S(1)}, bf16[512,1024]{1,0:T(8,128)(2,1)S(1)}, u32[]{:S(2)}, u32[]{:S(2)}) collective-permute-start(bf16[512,1024]{1,0:T(8,128)(2,1)S(1)} %get-tuple-element.38.second_ref), channel_id=1, source_target_pairs={{0,2},{1,127},{2,4},{3,1},{4,6},{5,3},{6,8},{7,5},{8,10},{9,7},{10... | collective-permute-start | bytes 3145736 | tf_op jit(solution)/shard_map/ppermute | solution.py:384
  23.7 3.8 %copy-start = (bf16[1024,1024]{1,0:T(8,128)(2,1)S(1)}, bf16[1024,1024]{1,0:T(8,128)(2,1)}, u32[]{:S(2)}) copy-start(bf16[1024,1024]{1,0:T(8,128)(2,1)} %w_ref.3) | copy-start | bytes 6291460
  23.7 3.8 %copy-start.1 = (bf16[768,1024]{1,0:T(8,128)(2,1)S(1)}, bf16[768,1024]{1,0:T(8,128)(2,1)}, u32[]{:S(2)}) copy-start(bf16[768,1024]{1,0:T(8,128)(2,1)} %x_ref.3) | copy-start | bytes 4718596
  31.8 8.9 %collective-permute-start.5 = (bf16[144,1024]{1,0:T(8,128)(2,1)S(1)}, bf16[144,1024]{1,0:T(8,128)(2,1)S(1)}, u32[]{:S(2)}, u32[]{:S(2)}) collective-permute-start(bf16[144,1024]{1,0:T(8,128)(2,1)S(1)} %get-tuple-element.47), channel_id=1, source_target_pairs={{0,1},{1,0},{2,3},{3,2},{4,5},{5,4},{6,7},{7,6},{8,9},{9,8},{10,11... | collective-permute-start | bytes 884744 | tf_op jit(solution)/shard_map/ppermute | solution.py:384
  39.0 1.6 %collective-permute-start.6 = (bf16[128,1024]{1,0:T(8,128)(2,1)S(1)}, bf16[128,1024]{1,0:T(8,128)(2,1)S(1)}, u32[]{:S(2)}, u32[]{:S(2)}) collective-permute-start(bf16[128,1024]{1,0:T(8,128)(2,1)S(1)} %get-tuple-element.48), channel_id=1, source_target_pairs={{0,1},{1,0},{2,3},{3,2},{4,5},{5,4},{6,7},{7,6},{8,9},{9,8},{10,11... | collective-permute-start | bytes 786440 | tf_op jit(solution)/shard_map/ppermute | solution.py:384
  47.7 1.6 %collective-permute-start.10 = (bf16[128,1024]{1,0:T(8,128)(2,1)S(1)}, bf16[128,1024]{1,0:T(8,128)(2,1)S(1)}, u32[]{:S(2)}, u32[]{:S(2)}) collective-permute-start(bf16[128,1024]{1,0:T(8,128)(2,1)S(1)} %get-tuple-element.57), channel_id=1, source_target_pairs={{0,1},{1,0},{2,3},{3,2},{4,5},{5,4},{6,7},{7,6},{8,9},{9,8},{10,11... | collective-permute-start | bytes 786440 | tf_op jit(solution)/shard_map/ppermute | solution.py:384
  48.2 1.5 %collective-permute-start.11 = (bf16[128,1024]{1,0:T(8,128)(2,1)S(1)}, bf16[128,1024]{1,0:T(8,128)(2,1)S(1)}, u32[]{:S(2)}, u32[]{:S(2)}) collective-permute-start(bf16[128,1024]{1,0:T(8,128)(2,1)S(1)} %get-tuple-element.58), channel_id=1, source_target_pairs={{0,1},{1,0},{2,3},{3,2},{4,5},{5,4},{6,7},{7,6},{8,9},{9,8},{10,11... | collective-permute-start | bytes 786440 | tf_op jit(solution)/shard_map/ppermute | solution.py:384
  48.3 1.8 %collective-permute-start.8 = (bf16[128,1024]{1,0:T(8,128)(2,1)S(1)}, bf16[128,1024]{1,0:T(8,128)(2,1)S(1)}, u32[]{:S(2)}, u32[]{:S(2)}) collective-permute-start(bf16[128,1024]{1,0:T(8,128)(2,1)S(1)} %get-tuple-element.55), channel_id=1, source_target_pairs={{0,1},{1,0},{2,3},{3,2},{4,5},{5,4},{6,7},{7,6},{8,9},{9,8},{10,11... | collective-permute-start | bytes 786440 | tf_op jit(solution)/shard_map/ppermute | solution.py:384
  48.7 1.8 %collective-permute-start.9 = (bf16[128,1024]{1,0:T(8,128)(2,1)S(1)}, bf16[128,1024]{1,0:T(8,128)(2,1)S(1)}, u32[]{:S(2)}, u32[]{:S(2)}) collective-permute-start(bf16[128,1024]{1,0:T(8,128)(2,1)S(1)} %get-tuple-element.56), channel_id=1, source_target_pairs={{0,1},{1,0},{2,3},{3,2},{4,5},{5,4},{6,7},{7,6},{8,9},{9,8},{10,11... | collective-permute-start | bytes 786440 | tf_op jit(solution)/shard_map/ppermute | solution.py:384
  58.2 1.1 %copy-start.4 = (bf16[768,1024]{1,0:T(8,128)(2,1)}, bf16[768,1024]{1,0:T(8,128)(2,1)S(1)}, u32[]{:S(2)}) copy-start(bf16[768,1024]{1,0:T(8,128)(2,1)S(1)} %get-tuple-element.65.dproj_ref) | copy-start | bytes 4718596
  59.4 2.7 %collective-permute-start.12 = (bf16[512,1024]{1,0:T(8,128)(2,1)S(1)}, bf16[512,1024]{1,0:T(8,128)(2,1)S(1)}, u32[]{:S(2)}, u32[]{:S(2)}) collective-permute-start(bf16[512,1024]{1,0:T(8,128)(2,1)S(1)} %get-tuple-element.62), channel_id=1, source_target_pairs={{0,1},{1,0},{2,3},{3,2},{4,5},{5,4},{6,7},{7,6},{8,9},{9,8},{10,11... | collective-permute-start | bytes 3145736 | tf_op jit(solution)/shard_map/ppermute | solution.py:384
  59.7 2.3 %collective-permute-start.13 = (f32[8,128]{1,0:T(8,128)S(1)}, f32[8,128]{1,0:T(8,128)S(1)}, u32[]{:S(2)}, u32[]{:S(2)}) collective-permute-start(f32[8,128]{1,0:T(8,128)S(1)} %get-tuple-element.63.loss_ref), channel_id=1, source_target_pairs={{0,1},{1,0},{2,3},{3,2},{4,5},{5,4},{6,7},{7,6},{8,9},{9,8},{10,11... | collective-permute-start | bytes 12296 | tf_op jit(solution)/shard_map/ppermute | solution.py:384
  63.2 28.6 %all-to-all-start = ((bf16[64,8,1152]{2,1,0:T(8,128)(2,1)}), bf16[64,8,1152]{2,1,0:T(8,128)(2,1)S(1)}, u32[]{:S(2)}, u32[]{:S(2)}) async-start(bf16[64,8,1152]{2,1,0:T(8,128)(2,1)} %bitcast.1), calls=%async_computation | async-start | bytes 2359296 | tf_op jit(solution)/shard_map/all_to_all | solution.py:456
  70.9 1.4 %copy-start.5 = (bf16[768,1024]{1,0:T(8,128)(2,1)S(1)}, bf16[768,1024]{1,0:T(8,128)(2,1)}, u32[]{:S(2)}) copy-start(bf16[768,1024]{1,0:T(8,128)(2,1)} %copy-done.4) | copy-start | bytes 4718596

commit v3 on v2

--- a/solution.py
+++ b/solution.py
@@ -14,7 +14,7 @@
 FIRST = 256
 SECOND = ROWS - FIRST
 LABELS = 16
-PIECE = 128
+PIECE = 256
 LANES = 128
 MIB = 1 << 20
 
@@ -62,30 +62,45 @@
 
 
 def ids_of(first_ref):
+    if first_ref.dtype == jnp.int32:
+        return id_row(first_ref).astype(jnp.float32)
     rows = first_ref[first_ref.shape[0] - LABELS :, :ROWS].astype(jnp.float32)
     return 256.0 * rows[:1] + rows[1:2]
 
 
-def project_kernel(x_hbm, w_hbm, label_ref, first_ref, second_ref, x_ref, w_ref, x_sems, w_sems):
-    heads, groups = [], []
-    for number, start in enumerate(range(0, DIM, STEP)):
-        rows = pl.ds(start, STEP)
-        heads.append(
-            pltpu.make_async_copy(w_hbm.at[rows], w_ref.at[rows], w_sems.at[number])
-        )
-        heads[-1].start()
-    for number, start in enumerate(range(0, ROWS, GROUP)):
-        rows = pl.ds(start, GROUP)
-        groups.append(
-            pltpu.make_async_copy(x_hbm.at[rows], x_ref.at[rows], x_sems.at[number])
-        )
-        groups[-1].start()
+def project_kernel(
+    x_hbm,
+    w_hbm,
+    label_hbm,
+    first_ref,
+    second_ref,
+    unit_ref,
+    inverse_ref,
+    x_ref,
+    w_ref,
+    label_ref,
+    sems,
+):
+    copies = []
+
+    def fetch(source, target):
+        copies.append(pltpu.make_async_copy(source, target, sems.at[len(copies)]))
+        copies[-1].start()
+        return copies[-1]
+
+    needed = [fetch(w_hbm, w_ref)]
+    groups = [
+        fetch(x_hbm.at[pl.ds(start, GROUP)], x_ref.at[pl.ds(start, GROUP)])
+        for start in range(0, ROWS, GROUP)
+    ]
+    needed.append(fetch(label_hbm, label_ref))
+    for copy in needed + groups:
+        copy.wait()
     first_ref[FIRST:, :] = label_rows(label_ref)
-    for head in heads:
-        head.wait()
-    for number, start in enumerate(range(0, ROWS, GROUP)):
-        groups[number].wait()
-        unit, _ = normalised(x_ref[start : start + GROUP, :], w_ref[...])
+    for start in range(0, ROWS, GROUP):
+        unit, inverse = normalised(x_ref[start : start + GROUP, :], w_ref[...])
+        unit_ref[start : start + GROUP, :] = unit
+        inverse_ref[start : start + GROUP, :] = jnp.broadcast_to(inverse, (GROUP, LANES))
         ref, at = (first_ref, start) if start < FIRST else (second_ref, start - FIRST)
         ref[at : at + GROUP, :] = unit.astype(jnp.bfloat16)
 
@@ -93,18 +108,26 @@
 def project(x, w, label):
     return pl.pallas_call(
         project_kernel,
-        in_specs=[HBM, HBM, VMEM],
-        out_specs=[VMEM] * 2,
-        out_shape=BLOCK_SHAPE,
+        in_specs=[HBM] * 3,
+        out_specs=[VMEM] * 4,
+        out_shape=BLOCK_SHAPE + [shape(ROWS, DIM), shape(ROWS, LANES)],
         scratch_shapes=[
             pltpu.VMEM((ROWS, DIM), jnp.bfloat16),
             pltpu.VMEM((DIM, DIM), jnp.bfloat16),
-            pltpu.SemaphoreType.DMA((ROWS // GROUP,)),
-            pltpu.SemaphoreType.DMA((DIM // STEP,)),
+            pltpu.VMEM((ROWS // LANES, LANES), jnp.int32),
+            pltpu.SemaphoreType.DMA((2 + ROWS // GROUP,)),
         ],
-        compiler_params=params(62),
+        compiler_params=params(52),
         cost_estimate=cost(2 * ROWS * DIM * DIM, 5 * MIB),
     )(x, w, label)
+
+
+def scale_of(scalars):
+    return scalars[:1, :1]
+
+
+def shift_of(scalars):
+    return scalars[4:5, :1]
 
 
 def slopes_of(cosine, row_ids, col_ids, scale, shift, with_loss):
@@ -144,7 +167,7 @@
 
 
 def tile_pieces(scalars, own, partner, row_ids, col_ids, with_loss):
-    scale, shift = scalars[0], scalars[1]
+    scale, shift = scale_of(scalars), shift_of(scalars)
     count = sum(part.shape[0] for part in partner)
 
     def cosine_of(start):
@@ -175,44 +198,50 @@
 
 
 def own_tile_kernel(
-    scalars, first_ref, second_ref, ids_ref, sum_ref, loss_ref, first_out, second_out
+    scale_ref,
+    shift_ref,
+    first_ref,
+    second_ref,
+    scalars_ref,
+    ids_ref,
+    sum_ref,
+    loss_ref,
+    first_out,
+    second_out,
 ):
     first_out[...] = first_ref[...]
     second_out[...] = second_ref[...]
+    place = lax.broadcasted_iota(jnp.int32, (8, LANES), 0)
+    scalars_ref[...] = jnp.where(place < 4, scale_ref[0], shift_ref[0])
     ids = ids_of(first_ref)
     ids_ref[...] = jnp.broadcast_to(ids, (LANES, ROWS)).T
     own = (first_ref, second_ref)
     total = jnp.zeros((8, LANES), jnp.float32)
-    for rows, piece, loss in tile_pieces(scalars, own, both(*own), ids_ref, ids, True):
+    for rows, piece, loss in tile_pieces(scalars_ref, own, both(*own), ids_ref, ids, True):
         sum_ref[rows, :] = 2.0 * piece
         total = total + loss
     loss_ref[...] = total
 
 
-def own_tile(scalars, own):
+def own_tile(scale, shift, own):
     return pl.pallas_call(
         own_tile_kernel,
-        in_specs=[SCALARS] + [VMEM] * 2,
-        out_specs=[VMEM] * 5,
-        out_shape=[shape(ROWS, LANES), shape(ROWS, DIM), shape(8, LANES)] + BLOCK_SHAPE,
+        in_specs=[SCALARS] * 2 + [VMEM] * 2,
+        out_specs=[VMEM] * 6,
+        out_shape=[shape(8, LANES), shape(ROWS, LANES), shape(ROWS, DIM), shape(8, LANES)] + BLOCK_SHAPE,
         compiler_params=params(12),
         cost_estimate=cost(4 * ROWS * ROWS * DIM, 5 * MIB),
-    )(scalars, *own)
+    )(scale, shift, *own)
 
 
 def partner_tile_kernel(
-    weight, forward, cols, scalars, first_ref, second_ref, ids, sum_in, loss_in, labels, *rest
+    weight, cols, scalars, first_ref, second_ref, ids, sum_in, loss_in, labels, *rest
 ):
     first, last, takes = cols
-    parts = rest[: len(takes)]
-    outs = rest[len(rest) - 2 - forward :]
-    sum_ref, loss_ref = outs[:2]
-    for number in range(forward):
-        held = outs[2 + number]
-        held[...] = parts[0][PIECE * number : PIECE * number + held.shape[0], :]
+    sum_ref, loss_ref = rest[-2:]
     col_ids = ids_of(labels)[:, first:last]
-    partner = [part[:take, :] for part, take in zip(parts, takes)]
-    if len(parts) > 1:
+    partner = [part[:take, :] for part, take in zip(rest, takes)]
+    if len(partner) > 1:
         partner = [jnp.concatenate(partner, axis=0)]
     total = loss_in[...]
     for rows, piece, loss in tile_pieces(
@@ -224,42 +253,34 @@
     loss_ref[...] = total
 
 
-def pieces_of(part):
-    count = part.shape[0] // PIECE
-    sizes = [PIECE] * (count - 1) + [part.shape[0] - PIECE * (count - 1)]
-    return [shape(size, DIM, jnp.bfloat16) for size in sizes]
-
-
-def partner_tile(weight, forward, scalars, own, partner, cols, ids, summed, loss, labels, after=()):
-    passed = pieces_of(partner[0]) if forward else []
+def partner_tile(weight, partner, cols, labels, summed, loss, scalars, own, ids):
     takes = tuple(part.shape[0] // PIECE * PIECE for part in partner)
     return pl.pallas_call(
-        functools.partial(partner_tile_kernel, weight, len(passed), (*cols, takes)),
-        in_specs=[SCALARS] + [VMEM] * (6 + len(partner)) + [ANY] * len(after),
-        out_specs=[VMEM] * (2 + len(passed)),
-        out_shape=[shape(ROWS, DIM), shape(8, LANES)] + passed,
+        functools.partial(partner_tile_kernel, weight, (*cols, takes)),
+        in_specs=[VMEM] * (7 + len(partner)),
+        out_specs=[VMEM] * 2,
+        out_shape=[shape(ROWS, DIM), shape(8, LANES)],
         compiler_params=params(12),
         cost_estimate=cost(4 * ROWS * (cols[1] - cols[0]) * DIM, 10 * MIB),
-    )(scalars, *own, ids, summed, loss, labels, *partner, *after)
-
-
-def unit_kernel(x_ref, w_ref, after, unit_ref, inverse_ref):
+    )(scalars, *own, ids, summed, loss, labels, *partner)
+
+
+def partner_projection_kernel(x_ref, w_ref, after, also_after, *pieces):
     for start in range(0, ROWS, STEP):
-        rows = pl.ds(start, STEP)
-        unit, inverse = normalised(x_ref[rows, :], w_ref[...])
-        unit_ref[rows, :] = unit
-        inverse_ref[rows, :] = jnp.broadcast_to(inverse, (STEP, LANES))
-
-
-def unit_rows(x, w, after):
-    return pl.pallas_call(
-        unit_kernel,
-        in_specs=[VMEM] * 2 + [ANY],
-        out_specs=[VMEM] * 2,
-        out_shape=[shape(ROWS, DIM), shape(ROWS, LANES)],
-        compiler_params=params(12),
-        cost_estimate=cost(2 * ROWS * DIM * DIM, 7 * MIB),
-    )(x, w, after)
+        unit, _ = normalised(x_ref[start : start + STEP, :], w_ref[...])
+        for at in range(0, STEP, PIECE):
+            pieces[(start + at) // PIECE][...] = unit[at : at + PIECE, :].astype(jnp.bfloat16)
+
+
+def partner_projection(x, w, after, also_after):
+    return pl.pallas_call(
+        partner_projection_kernel,
+        in_specs=[VMEM] * 2 + [ANY] * 2,
+        out_specs=[VMEM] * (ROWS // PIECE),
+        out_shape=[shape(PIECE, DIM, jnp.bfloat16)] * (ROWS // PIECE),
+        compiler_params=params(12),
+        cost_estimate=cost(2 * ROWS * DIM * DIM, 5 * MIB),
+    )(x, w, after, also_after)
 
 
 def last_kernel(
@@ -282,7 +303,7 @@
         scalars, (first_ref, second_ref), [far_ref[...]], ids, col_ids, False
     ):
         unit = unit_ref[rows, :]
-        dunit = scalars[0] * (sum_in[rows, :] + piece)
+        dunit = scale_of(scalars) * (sum_in[rows, :] + piece)
         radial = jnp.sum(dunit * unit, axis=1, keepdims=True)
         inverse = inverse_ref[rows, :][:, :1]
         dproj_ref[rows, :] = ((dunit - unit * radial) * inverse).astype(jnp.bfloat16)
@@ -302,7 +323,7 @@
 def last(scalars, own, far, ids, summed, unit, inverse, x):
     return pl.pallas_call(
         last_kernel,
-        in_specs=[SCALARS] + [VMEM] * 9,
+        in_specs=[VMEM] * 10,
         out_specs=[VMEM] * 3,
         out_shape=[
             shape(ROWS, DIM, jnp.bfloat16),
@@ -392,58 +413,24 @@
     def far(i):
         return i - 2 if i & 1 else i + 2
 
-    own = project(x, w, label.reshape(ROWS // LANES, LANES))
-    near_first = move(own[0], near)
-    near_second = move(own[1], near)
+    labels = label.reshape(ROWS // LANES, LANES)
+    near_x = move(x, near)
+    near_labels = move(labels, near)
+    third_labels = move(near_labels, pair)
+
+    *own, unit, inverse = project(x, w, labels)
     paired = [move(part, pair) for part in own]
-
-    scalars = jnp.concatenate([score_scale, score_shift])
-    ids, summed, loss, *again = own_tile(scalars, own)
-    far_first = move(again[0], far)
-    far_second = move(again[1], far)
-    own = again
+    scalars, ids, summed, loss, *own = own_tile(score_scale, score_shift, own)
+    far_first = move(own[0], far)
+    far_second = move(own[1], far)
     tile = functools.partial(partner_tile, scalars=scalars, own=own, ids=ids)
-    whole, early, late = (0, ROWS), (0, FIRST), (FIRST, ROWS)
-    summed, loss = tile(
-        0.5, False, partner=paired, cols=whole, summed=summed, loss=loss, labels=paired[0]
-    )
-    unit, inverse = unit_rows(x, w, loss)
-    summed, loss, *passed = tile(
-        0.5,
-        True,
-        partner=[near_first],
-        cols=early,
-        summed=summed,
-        loss=loss,
-        labels=near_first,
-        after=(inverse,),
-    )
-    third_first = [move(piece, pair) for piece in passed]
-    summed, loss = tile(
-        1.0,
-        False,
-        partner=third_first,
-        cols=early,
-        summed=summed,
-        loss=loss,
-        labels=third_first[-1],
-    )
-    summed, loss = tile(
-        None, False, partner=[far_first], cols=early, summed=summed, loss=loss, labels=far_first
-    )
-    summed, loss, *passed = tile(
-        0.5, True, partner=[near_second], cols=late, summed=summed, loss=loss, labels=near_first
-    )
-    third_second = [move(piece, pair) for piece in passed]
-    summed, loss = tile(
-        1.0,
-        False,
-        partner=third_second,
-        cols=late,
-        summed=summed,
-        loss=loss,
-        labels=third_first[-1],
-    )
+    whole, early = (0, ROWS), (0, FIRST)
+    summed, loss = tile(0.5, paired, whole, paired[0], summed, loss)
+    pieces = partner_projection(near_x, w, loss, near_labels)
+    third = [move(piece, pair) for piece in pieces]
+    summed, loss = tile(None, [far_first], early, far_first, summed, loss)
+    summed, loss = tile(0.5, pieces, whole, near_labels, summed, loss)
+    summed, loss = tile(1.0, third, whole, third_labels, summed, loss)
     other_loss = move(loss, pair)
     dproj, kept, sent = last(
         scalars, own, [far_first, far_second], ids, summed, unit, inverse, x

time: 93 us -> 85.8 us (0.923)
  Pallas kernels: 37.7 us -> 31.7 us
  waiting for transfers between devices: 21.8 us -> 25.5 us
  local copies, waits for them, and re-layouts: 4.83 us -> 2.11 us
  starting transfers between devices: 26.1 us -> 24.1 us
    pallas_call x10 -> x8, Pallas kernels: 32.7 us -> 26.7 us  [the longest x4 11.3 us: partner_tile(): pl.pallas_call(functools.partial(partner_tile_kernel, weight, (*cols, tak...]
    ppermute x14 -> x12, waiting for transfers between devices: 5.3 us -> 9 us  [move(): lax.ppermute(value, 'batch', [(i, target(i) % count) for i in range(count)])]
    unnamed x12, local copies, waits for them, and re-layouts: 4.83 us -> 2.11 us
    ppermute x14 -> x12, starting transfers between devices: 18.4 us -> 16.1 us  [move(): lax.ppermute(value, 'batch', [(i, target(i) % count) for i in range(count)])]
  transfers between devices with their start and end apart: 15 -> 13, of which waited for: 7 -> 5; matrix products, arithmetic and copies ran while one was open for 0% -> 0% of each run, Pallas kernels for 27% -> 30%
where the time goes in v3:
time: 85.8 us; the launch traced here: 85.5 us
  Pallas kernels  31.7 us (37%)
  waiting for transfers between devices  25.5 us (30%)
  starting transfers between devices  24.1 us (28%)
  local copies, waits for them, and re-layouts  2.11 us (2%)
  between operations  2.09 us (2%)
    all_to_all x1, waiting for transfers between devices, on_device(): lax.all_to_all(parts, 'batch', 0, 0, tiled=True, axis_index_groups=groups)  16.5 us
    ppermute x12, starting transfers between devices, move(): lax.ppermute(value, 'batch', [(i, target(i) % count) for i in range(count)])  16.1 us
    pallas_call x4, Pallas kernels, partner_tile(): pl.pallas_call(functools.partial(partner_tile_kernel, weight, (*cols, tak...  11.3 us
    ppermute x12, waiting for transfers between devices, move(): lax.ppermute(value, 'batch', [(i, target(i) % count) for i in range(count)])  9 us
    all_to_all x1, starting transfers between devices, on_device(): lax.all_to_all(parts, 'batch', 0, 0, tiled=True, axis_index_groups=groups)  8.04 us
    pallas_call x1, Pallas kernels, project(): pl.pallas_call(project_kernel, in_specs=[HBM] * 3, out_specs=[VMEM] * 4,...  5.72 us
    pallas_call x1, Pallas kernels, last(): pl.pallas_call(last_kernel, in_specs=[VMEM] * 10, out_specs=[VMEM] * 3, o...  4.31 us
    pallas_call x1, Pallas kernels, own_tile(): pl.pallas_call(own_tile_kernel, in_specs=[SCALARS] * 2 + [VMEM] * 2, out_...  3.4 us
  transfers between devices with their start and end apart: 13, of which 5 were waited for; matrix products, arithmetic and copies ran while one was open for 0% of the time, Pallas kernels for 30%

profile of v3, /device:TPU:0, one launch (start us, length us, event | category | flops | bytes accessed | tf_op | source)
XLA Modules:
  0.0 85.5 jit_solution(5707714652427554683)
XLA Ops:
  0.6 8.3 %collective-permute-start.5 = (bf16[768,1024]{1,0:T(8,128)(2,1)}, bf16[768,1024]{1,0:T(8,128)(2,1)S(1)}, u32[]{:S(2)}, u32[]{:S(2)}) collective-permute-start(bf16[768,1024]{1,0:T(8,128)(2,1)} %x_ref.1), channel_id=1, source_target_pairs={{0,127},{1,2},{2,1},{3,4},{4,3},{5,6},{6,5},{7,8},{8,7},{9,10},{10... | collective-permute-start | bytes 4718600 | tf_op jit(solution)/shard_map/ppermute | solution.py:405
  8.9 0.0 copy-start.2
  8.9 0.7 copy-done.2
  9.6 5.7 %shard_map.76 = (bf16[272,1024]{1,0:T(8,128)(2,1)S(1)}, bf16[512,1024]{1,0:T(8,128)(2,1)S(1)}, f32[768,1024]{1,0:T(8,128)}, f32[768,128]{1,0:T(8,128)S(1)}) custom-call(bf16[768,1024]{1,0:T(8,128)(2,1)} %x_ref.1, bf16[1024,1024]{1,0:T(8,128)(2,1)} %w_ref.3, s32[6,128]{1,0:T(8,128)S(1)} %bitcast.3), custom_call_target="tpu_custom_call" | custom-call | flops 1610612736 | bytes 5242880 | tf_op jit(solution)/shard_map/pallas_call | solution.py:109
  15.3 0.1 collective-permute-start.3
  15.4 0.5 collective-permute-start.2
  15.9 0.5 collective-permute-start.4
  17.8 3.4 %shard_map.77 = (f32[8,128]{1,0:T(8,128)S(1)}, f32[768,128]{1,0:T(8,128)S(1)}, f32[768,1024]{1,0:T(8,128)S(1)}, f32[8,128]{1,0:T(8,128)S(1)}, bf16[272,1024]{1,0...) custom-call(f32[1]{0:T(128)S(6)} %copy.8.scale_ref, f32[1]{0:T(128)S(6)} %copy.9.shift_ref, ...), custom_call_target="tpu_custom_call" | custom-call | flops 2415919104 | bytes 5242880 | tf_op jit(solution)/shard_map/pallas_call | solution.py:227
  21.2 1.3 %collective-permute-start = (bf16[272,1024]{1,0:T(8,128)(2,1)S(1)}, bf16[272,1024]{1,0:T(8,128)(2,1)S(1)}, u32[]{:S(2)}, u32[]{:S(2)}) collective-permute-start(bf16[272,1024]{1,0:T(8,128)(2,1)S(1)} %get-tuple-element.32.first_ref), channel_id=1, source_target_pairs={{0,2},{1,127},{2,4},{3,1},{4,6},{5,3},{6,8},{7,5},{8,10},{9,7},{10... | collective-permute-start | bytes 1671176 | tf_op jit(solution)/shard_map/ppermute | solution.py:405
  22.4 0.0 collective-permute-done.2.labels.rest_0_
  22.4 0.1 collective-permute-start.1
  22.5 0.0 collective-permute-done.3.rest_1_
  22.5 3.3 %shard_map.78 = (f32[768,1024]{1,0:T(8,128)S(1)}, f32[8,128]{1,0:T(8,128)S(1)}) custom-call(f32[8,128]{1,0:T(8,128)S(1)} %get-tuple-element.31.scalars, bf16[272,1024]{1,0:T(8,128)(2,1)S(1)} %get-tuple-element.32.first_ref, bf16[512,1024]{1,0:T(8,128)(2,1)S(1)} %get-tuple-element.33.second_ref, f32[768,128]{1,0:T(8,128)S(1)} %get-tuple-element.34.ids, ...), custom_call_target="tpu_custom_call" | custom-call | flops 2415919104 | bytes 10485760 | tf_op jit(solution)/shard_map/pallas_call | solution.py:258
  25.8 1.4 %collective-permute-done.4.also_after.labels = s32[6,128]{1,0:T(8,128)S(1)} collective-permute-done((s32[6,128]{1,0:T(8,128)S(1)}, s32[6,128]{1,0:T(8,128)S(1)}, u32[]{:S(2)}, u32[]{:S(2)}) %collective-permute-start.4) | collective-permute-done | bytes 3104 | tf_op jit(solution)/shard_map/ppermute | solution.py:405
  27.3 0.0 collective-permute-done.5.x_ref
  27.3 0.0 copy-done
  27.3 1.9 %shard_map.80 = (bf16[256,1024]{1,0:T(8,128)(2,1)S(1)}, bf16[256,1024]{1,0:T(8,128)(2,1)S(1)}, bf16[256,1024]{1,0:T(8,128)(2,1)S(1)}) custom-call(bf16[768,1024]{1,0:T(8,128)(2,1)S(1)} %collective-permute-done.5.x_ref, bf16[1024,1024]{1,0:T(8,128)(2,1)S(1)} %copy-done, f32[8,128]{1,0:T(8,128)S(1)} %get-tuple-element.38.loss_in.after, ...), custom_call_target="tpu_custom_call" | custom-call | flops 1610612736 | bytes 5242880 | tf_op jit(solution)/shard_map/pallas_call | solution.py:276
  29.2 4.2 %collective-permute-start.7 = (bf16[256,1024]{1,0:T(8,128)(2,1)S(1)}, bf16[256,1024]{1,0:T(8,128)(2,1)S(1)}, u32[]{:S(2)}, u32[]{:S(2)}) collective-permute-start(bf16[256,1024]{1,0:T(8,128)(2,1)S(1)} %get-tuple-element.41.rest_0_), channel_id=1, source_target_pairs={{0,1},{1,0},{2,3},{3,2},{4,5},{5,4},{6,7},{7,6},{8,9},{9,8},{10,11... | collective-permute-start | bytes 1572872 | tf_op jit(solution)/shard_map/ppermute | solution.py:405
  33.4 0.1 collective-permute-start.8
  33.5 0.4 collective-permute-start.9
  34.0 2.2 %collective-permute-done.labels.rest_0_.far_first = bf16[272,1024]{1,0:T(8,128)(2,1)S(1)} collective-permute-done((bf16[272,1024]{1,0:T(8,128)(2,1)S(1)}, bf16[272,1024]{1,0:T(8,128)(2,1)S(1)}, u32[]{:S(2)}, u32[]{:S(2)}) %collective-permute-start) | collective-permute-done | bytes 557088 | tf_op jit(solution)/shard_map/ppermute | solution.py:405
  36.2 0.0 collective-permute-start.6
  36.2 1.4 %shard_map.79 = (f32[768,1024]{1,0:T(8,128)S(1)}, f32[8,128]{1,0:T(8,128)S(1)}) custom-call(f32[8,128]{1,0:T(8,128)S(1)} %get-tuple-element.31.scalars, bf16[272,1024]{1,0:T(8,128)(2,1)S(1)} %get-tuple-element.32.first_ref, bf16[512,1024]{1,0:T(8,128)(2,1)S(1)} %get-tuple-element.33.second_ref, f32[768,128]{1,0:T(8,128)S(1)} %get-tuple-element.34.ids, ...), custom_call_target="tpu_custom_call" | custom-call | flops 805306368 | bytes 10485760 | tf_op jit(solution)/shard_map/pallas_call | solution.py:258
  37.6 3.3 %shard_map.81 = (f32[768,1024]{1,0:T(8,128)S(1)}, f32[8,128]{1,0:T(8,128)S(1)}) custom-call(f32[8,128]{1,0:T(8,128)S(1)} %get-tuple-element.31.scalars, bf16[272,1024]{1,0:T(8,128)(2,1)S(1)} %get-tuple-element.32.first_ref, bf16[512,1024]{1,0:T(8,128)(2,1)S(1)} %get-tuple-element.33.second_ref, f32[768,128]{1,0:T(8,128)S(1)} %get-tuple-element.34.ids, ...), custom_call_target="tpu_custom_call" | custom-call | flops 2415919104 | bytes 10485760 | tf_op jit(solution)/shard_map/pallas_call | solution.py:258
  40.9 0.0 collective-permute-done.6.labels
  40.9 0.0 collective-permute-done.7.rest_0_
  40.9 0.0 collective-permute-done.8.rest_1_
  40.9 0.0 collective-permute-done.9.rest_2_
  40.9 0.0 copy-start.1
  41.0 0.0 copy-start.3
  41.0 3.3 %shard_map.82 = (f32[768,1024]{1,0:T(8,128)S(1)}, f32[8,128]{1,0:T(8,128)S(1)}) custom-call(f32[8,128]{1,0:T(8,128)S(1)} %get-tuple-element.31.scalars, bf16[272,1024]{1,0:T(8,128)(2,1)S(1)} %get-tuple-element.32.first_ref, bf16[512,1024]{1,0:T(8,128)(2,1)S(1)} %get-tuple-element.33.second_ref, f32[768,128]{1,0:T(8,128)S(1)} %get-tuple-element.34.ids, ...), custom_call_target="tpu_custom_call" | custom-call | flops 2415919104 | bytes 10485760 | tf_op jit(solution)/shard_map/pallas_call | solution.py:258
  44.3 3.2 %collective-permute-done.1.far_ref = bf16[512,1024]{1,0:T(8,128)(2,1)S(1)} collective-permute-done((bf16[512,1024]{1,0:T(8,128)(2,1)S(1)}, bf16[512,1024]{1,0:T(8,128)(2,1)S(1)}, u32[]{:S(2)}, u32[]{:S(2)}) %collective-permute-start.1) | collective-permute-done | bytes 1048608 | tf_op jit(solution)/shard_map/ppermute | solution.py:405
  47.4 0.0 copy-done.1
  47.4 0.0 copy-done.3
  47.4 4.3 %shard_map.83 = (bf16[768,1024]{1,0:T(8,128)(2,1)S(1)}, f32[512,1024]{1,0:T(8,128)S(1)}, bf16[512,1024]{1,0:T(8,128)(2,1)S(1)}) custom-call(f32[8,128]{1,0:T(8,128)S(1)} %get-tuple-element.31.scalars, bf16[272,1024]{1,0:T(8,128)(2,1)S(1)} %get-tuple-element.32.first_ref, bf16[512,1024]{1,0:T(8,128)(2,1)S(1)} %get-tuple-element.33.second_ref, ...), custom_call_target="tpu_custom_call" | custom-call | flops 3221225472 | bytes 14680064 | tf_op jit(solution)/shard_map/pallas_call | solution.py:324
  51.8 0.0 copy-start.4
  51.8 0.1 collective-permute-start.10
  51.9 0.5 collective-permute-start.11
  52.4 2.2 %collective-permute-done.11.other_loss_ref = f32[8,128]{1,0:T(8,128)S(1)} collective-permute-done((f32[8,128]{1,0:T(8,128)S(1)}, f32[8,128]{1,0:T(8,128)S(1)}, u32[]{:S(2)}, u32[]{:S(2)}) %collective-permute-start.11) | collective-permute-done | bytes 4128 | tf_op jit(solution)/shard_map/ppermute | solution.py:405
  54.5 0.0 collective-permute-done.10.received_ref
  54.5 1.3 %shard_map.84 = bf16[512,1152]{1,0:T(8,128)(2,1)} custom-call(f32[512,1024]{1,0:T(8,128)S(1)} %get-tuple-element.49.kept_ref, bf16[512,1024]{1,0:T(8,128)(2,1)S(1)} %collective-permute-done.10.received_ref, f32[8,128]{1,0:T(8,128)S(1)} %get-tuple-element.51.loss_ref, f32[8,128]{1,0:T(8,128)S(1)} %collective-permute-done.11.other_loss_ref), custom_call_target="tpu_custom_call" | custom-call | flops 1048576 | bytes 5242880 | tf_op jit(solution)/shard_map/pallas_call | solution.py:372
  55.8 0.0 copy-done.4
  55.8 8.0 %all-to-all-start = ((bf16[64,8,1152]{2,1,0:T(8,128)(2,1)}), bf16[64,8,1152]{2,1,0:T(8,128)(2,1)S(1)}, u32[]{:S(2)}, u32[]{:S(2)}) async-start(bf16[64,8,1152]{2,1,0:T(8,128)(2,1)} %bitcast.1), calls=%async_computation | async-start | bytes 2359296 | tf_op jit(solution)/shard_map/all_to_all | solution.py:443
  63.8 0.0 copy-start.5
  63.8 1.4 %copy-done.5 = bf16[768,1024]{1,0:T(8,128)(2,1)S(1)} copy-done((bf16[768,1024]{1,0:T(8,128)(2,1)S(1)}, bf16[768,1024]{1,0:T(8,128)(2,1)}, u32[]{:S(2)}) %copy-start.5) | copy-done | bytes 1572888
  65.2 3.0 %shard_map.86 = bf16[768,1024]{1,0:T(8,128)(2,1)} custom-call(bf16[768,1024]{1,0:T(8,128)(2,1)S(1)} %copy-done.5, bf16[1024,1024]{1,0:T(8,128)(2,1)S(1)} %copy-done), custom_call_target="tpu_custom_call" | custom-call | flops 1610612736 | bytes 5242880 | tf_op jit(solution)/shard_map/pallas_call | solution.py:347
  68.2 16.5 %all-to-all-done.parts_ref = bf16[64,8,1152]{2,1,0:T(8,128)(2,1)S(1)} async-done(((bf16[64,8,1152]{2,1,0:T(8,128)(2,1)}), bf16[64,8,1152]{2,1,0:T(8,128)(2,1)S(1)}, u32[]{:S(2)}, u32[]{:S(2)}) %all-to-all-start) | async-done | bytes 1179680 | tf_op jit(solution)/shard_map/all_to_all | solution.py:443
  84.7 0.8 shard_map.85
  (1 shorter events, 0.0 us)
Async XLA Ops:
  0.6 26.6 %collective-permute-start.5 = (bf16[768,1024]{1,0:T(8,128)(2,1)}, bf16[768,1024]{1,0:T(8,128)(2,1)S(1)}, u32[]{:S(2)}, u32[]{:S(2)}) collective-permute-start(bf16[768,1024]{1,0:T(8,128)(2,1)} %x_ref.1), channel_id=1, source_target_pairs={{0,127},{1,2},{2,1},{3,4},{4,3},{5,6},{6,5},{7,8},{8,7},{9,10},{10... | collective-permute-start | bytes 4718600 | tf_op jit(solution)/shard_map/ppermute | solution.py:405
  8.9 0.7 copy-start.2
  15.3 7.2 %collective-permute-start.3 = (bf16[512,1024]{1,0:T(8,128)(2,1)S(1)}, bf16[512,1024]{1,0:T(8,128)(2,1)S(1)}, u32[]{:S(2)}, u32[]{:S(2)}) collective-permute-start(bf16[512,1024]{1,0:T(8,128)(2,1)S(1)} %get-tuple-element.30.second_ref), channel_id=1, source_target_pairs={{0,1},{1,0},{2,3},{3,2},{4,5},{5,4},{6,7},{7,6},{8,9},{9,8},{10,11... | collective-permute-start | bytes 3145736 | tf_op jit(solution)/shard_map/ppermute | solution.py:405
  15.4 7.0 %collective-permute-start.2 = (bf16[272,1024]{1,0:T(8,128)(2,1)S(1)}, bf16[272,1024]{1,0:T(8,128)(2,1)S(1)}, u32[]{:S(2)}, u32[]{:S(2)}) collective-permute-start(bf16[272,1024]{1,0:T(8,128)(2,1)S(1)} %get-tuple-element.29.first_ref), channel_id=1, source_target_pairs={{0,1},{1,0},{2,3},{3,2},{4,5},{5,4},{6,7},{7,6},{8,9},{9,8},{10,11... | collective-permute-start | bytes 1671176 | tf_op jit(solution)/shard_map/ppermute | solution.py:405
  15.9 11.3 %collective-permute-start.4 = (s32[6,128]{1,0:T(8,128)S(1)}, s32[6,128]{1,0:T(8,128)S(1)}, u32[]{:S(2)}, u32[]{:S(2)}) collective-permute-start(s32[6,128]{1,0:T(8,128)S(1)} %bitcast.4), channel_id=1, source_target_pairs={{0,127},{1,2},{2,1},{3,4},{4,3},{5,6},{6,5},{7,8},{8,7},{9,10},{10... | collective-permute-start | bytes 9224 | tf_op jit(solution)/shard_map/ppermute | solution.py:405
  21.2 15.0 %collective-permute-start = (bf16[272,1024]{1,0:T(8,128)(2,1)S(1)}, bf16[272,1024]{1,0:T(8,128)(2,1)S(1)}, u32[]{:S(2)}, u32[]{:S(2)}) collective-permute-start(bf16[272,1024]{1,0:T(8,128)(2,1)S(1)} %get-tuple-element.32.first_ref), channel_id=1, source_target_pairs={{0,2},{1,127},{2,4},{3,1},{4,6},{5,3},{6,8},{7,5},{8,10},{9,7},{10... | collective-permute-start | bytes 1671176 | tf_op jit(solution)/shard_map/ppermute | solution.py:405
  22.4 25.0 %collective-permute-start.1 = (bf16[512,1024]{1,0:T(8,128)(2,1)S(1)}, bf16[512,1024]{1,0:T(8,128)(2,1)S(1)}, u32[]{:S(2)}, u32[]{:S(2)}) collective-permute-start(bf16[512,1024]{1,0:T(8,128)(2,1)S(1)} %get-tuple-element.33.second_ref), channel_id=1, source_target_pairs={{0,2},{1,127},{2,4},{3,1},{4,6},{5,3},{6,8},{7,5},{8,10},{9,7},{10... | collective-permute-start | bytes 3145736 | tf_op jit(solution)/shard_map/ppermute | solution.py:405
  22.5 4.7 %copy-start = (bf16[1024,1024]{1,0:T(8,128)(2,1)S(1)}, bf16[1024,1024]{1,0:T(8,128)(2,1)}, u32[]{:S(2)}) copy-start(bf16[1024,1024]{1,0:T(8,128)(2,1)} %w_ref.3) | copy-start | bytes 6291460
  29.2 11.7 %collective-permute-start.7 = (bf16[256,1024]{1,0:T(8,128)(2,1)S(1)}, bf16[256,1024]{1,0:T(8,128)(2,1)S(1)}, u32[]{:S(2)}, u32[]{:S(2)}) collective-permute-start(bf16[256,1024]{1,0:T(8,128)(2,1)S(1)} %get-tuple-element.41.rest_0_), channel_id=1, source_target_pairs={{0,1},{1,0},{2,3},{3,2},{4,5},{5,4},{6,7},{7,6},{8,9},{9,8},{10,11... | collective-permute-start | bytes 1572872 | tf_op jit(solution)/shard_map/ppermute | solution.py:405
  33.4 7.5 %collective-permute-start.8 = (bf16[256,1024]{1,0:T(8,128)(2,1)S(1)}, bf16[256,1024]{1,0:T(8,128)(2,1)S(1)}, u32[]{:S(2)}, u32[]{:S(2)}) collective-permute-start(bf16[256,1024]{1,0:T(8,128)(2,1)S(1)} %get-tuple-element.42.rest_1_), channel_id=1, source_target_pairs={{0,1},{1,0},{2,3},{3,2},{4,5},{5,4},{6,7},{7,6},{8,9},{9,8},{10,11... | collective-permute-start | bytes 1572872 | tf_op jit(solution)/shard_map/ppermute | solution.py:405
  33.5 7.4 %collective-permute-start.9 = (bf16[256,1024]{1,0:T(8,128)(2,1)S(1)}, bf16[256,1024]{1,0:T(8,128)(2,1)S(1)}, u32[]{:S(2)}, u32[]{:S(2)}) collective-permute-start(bf16[256,1024]{1,0:T(8,128)(2,1)S(1)} %get-tuple-element.43.rest_2_), channel_id=1, source_target_pairs={{0,1},{1,0},{2,3},{3,2},{4,5},{5,4},{6,7},{7,6},{8,9},{9,8},{10,11... | collective-permute-start | bytes 1572872 | tf_op jit(solution)/shard_map/ppermute | solution.py:405
  36.2 4.7 %collective-permute-start.6 = (s32[6,128]{1,0:T(8,128)S(1)}, s32[6,128]{1,0:T(8,128)S(1)}, u32[]{:S(2)}, u32[]{:S(2)}) collective-permute-start(s32[6,128]{1,0:T(8,128)S(1)} %collective-permute-done.4.also_after.labels), channel_id=1, source_target_pairs={{0,1},{1,0},{2,3},{3,2},{4,5},{5,4},{6,7},{7,6},{8,9},{9,8},{10,11... | collective-permute-start | bytes 9224 | tf_op jit(solution)/shard_map/ppermute | solution.py:405
  40.9 6.5 %copy-start.1 = (bf16[768,1024]{1,0:T(8,128)(2,1)S(1)}, bf16[768,1024]{1,0:T(8,128)(2,1)}, u32[]{:S(2)}) copy-start(bf16[768,1024]{1,0:T(8,128)(2,1)} %x_ref.1) | copy-start | bytes 4718596
  41.0 6.5 %copy-start.3 = (f32[768,1024]{1,0:T(8,128)S(1)}, f32[768,1024]{1,0:T(8,128)}, u32[]{:S(2)}) copy-start(f32[768,1024]{1,0:T(8,128)} %get-tuple-element.47.unit_ref) | copy-start | bytes 9437188
  51.8 4.0 %copy-start.4 = (bf16[768,1024]{1,0:T(8,128)(2,1)}, bf16[768,1024]{1,0:T(8,128)(2,1)S(1)}, u32[]{:S(2)}) copy-start(bf16[768,1024]{1,0:T(8,128)(2,1)S(1)} %get-tuple-element.53.dproj_ref) | copy-start | bytes 4718596
  51.8 2.7 %collective-permute-start.10 = (bf16[512,1024]{1,0:T(8,128)(2,1)S(1)}, bf16[512,1024]{1,0:T(8,128)(2,1)S(1)}, u32[]{:S(2)}, u32[]{:S(2)}) collective-permute-start(bf16[512,1024]{1,0:T(8,128)(2,1)S(1)} %get-tuple-element.50), channel_id=1, source_target_pairs={{0,1},{1,0},{2,3},{3,2},{4,5},{5,4},{6,7},{7,6},{8,9},{9,8},{10,11... | collective-permute-start | bytes 3145736 | tf_op jit(solution)/shard_map/ppermute | solution.py:405
  51.9 2.7 %collective-permute-start.11 = (f32[8,128]{1,0:T(8,128)S(1)}, f32[8,128]{1,0:T(8,128)S(1)}, u32[]{:S(2)}, u32[]{:S(2)}) collective-permute-start(f32[8,128]{1,0:T(8,128)S(1)} %get-tuple-element.51.loss_ref), channel_id=1, source_target_pairs={{0,1},{1,0},{2,3},{3,2},{4,5},{5,4},{6,7},{7,6},{8,9},{9,8},{10,11... | collective-permute-start | bytes 12296 | tf_op jit(solution)/shard_map/ppermute | solution.py:405
  55.8 28.9 %all-to-all-start = ((bf16[64,8,1152]{2,1,0:T(8,128)(2,1)}), bf16[64,8,1152]{2,1,0:T(8,128)(2,1)S(1)}, u32[]{:S(2)}, u32[]{:S(2)}) async-start(bf16[64,8,1152]{2,1,0:T(8,128)(2,1)} %bitcast.1), calls=%async_computation | async-start | bytes 2359296 | tf_op jit(solution)/shard_map/all_to_all | solution.py:443
  63.8 1.4 %copy-start.5 = (bf16[768,1024]{1,0:T(8,128)(2,1)S(1)}, bf16[768,1024]{1,0:T(8,128)(2,1)}, u32[]{:S(2)}) copy-start(bf16[768,1024]{1,0:T(8,128)(2,1)} %copy-done.4) | copy-start | bytes 4718596

commit v4 on v3

--- a/solution.py
+++ b/solution.py
@@ -52,26 +52,27 @@
     return jnp.concatenate([label_ref[i : i + 1, :] for i in range(ROWS // LANES)], axis=1)
 
 
-def label_rows(label_ref):
-    ids = id_row(label_ref)
-    ids = jnp.concatenate([ids, jnp.zeros((1, DIM - ROWS), jnp.int32)], axis=1)
-    high = (ids >> 8).astype(jnp.float32)
-    low = (ids & 255).astype(jnp.float32)
-    place = lax.broadcasted_iota(jnp.int32, (LABELS, DIM), 0)
-    return jnp.where(place == 0, high, jnp.where(place == 1, low, 0.0)).astype(jnp.bfloat16)
-
-
-def ids_of(first_ref):
-    if first_ref.dtype == jnp.int32:
-        return id_row(first_ref).astype(jnp.float32)
-    rows = first_ref[first_ref.shape[0] - LABELS :, :ROWS].astype(jnp.float32)
-    return 256.0 * rows[:1] + rows[1:2]
+def label_rows(label_ref, other_ref):
+    rows = []
+    for ref in (label_ref, other_ref):
+        ids = jnp.concatenate([id_row(ref), jnp.zeros((1, DIM - ROWS), jnp.int32)], axis=1)
+        rows += [(ids >> 8).astype(jnp.float32), (ids & 255).astype(jnp.float32)]
+    place = lax.broadcasted_iota(jnp.int32, (LABELS, DIM), 0) % 4
+    own = jnp.where(place == 0, rows[0], rows[1])
+    other = jnp.where(place == 2, rows[2], rows[3])
+    return jnp.where(place < 2, own, other).astype(jnp.bfloat16)
+
+
+def ids_of(ref, other=0):
+    rows = ref[ref.shape[0] - LABELS :, :ROWS].astype(jnp.float32)
+    return 256.0 * rows[2 * other : 2 * other + 1] + rows[2 * other + 1 : 2 * other + 2]
 
 
 def project_kernel(
     x_hbm,
     w_hbm,
     label_hbm,
+    other_hbm,
     first_ref,
     second_ref,
     unit_ref,
@@ -79,6 +80,7 @@
     x_ref,
     w_ref,
     label_ref,
+    other_ref,
     sems,
 ):
     copies = []
@@ -93,10 +95,10 @@
         fetch(x_hbm.at[pl.ds(start, GROUP)], x_ref.at[pl.ds(start, GROUP)])
         for start in range(0, ROWS, GROUP)
     ]
-    needed.append(fetch(label_hbm, label_ref))
+    needed += [fetch(label_hbm, label_ref), fetch(other_hbm, other_ref)]
     for copy in needed + groups:
         copy.wait()
-    first_ref[FIRST:, :] = label_rows(label_ref)
+    first_ref[FIRST:, :] = label_rows(label_ref, other_ref)
     for start in range(0, ROWS, GROUP):
         unit, inverse = normalised(x_ref[start : start + GROUP, :], w_ref[...])
         unit_ref[start : start + GROUP, :] = unit
@@ -105,21 +107,22 @@
         ref[at : at + GROUP, :] = unit.astype(jnp.bfloat16)
 
 
-def project(x, w, label):
+def project(x, w, label, other):
     return pl.pallas_call(
         project_kernel,
-        in_specs=[HBM] * 3,
+        in_specs=[HBM] * 4,
         out_specs=[VMEM] * 4,
         out_shape=BLOCK_SHAPE + [shape(ROWS, DIM), shape(ROWS, LANES)],
         scratch_shapes=[
             pltpu.VMEM((ROWS, DIM), jnp.bfloat16),
             pltpu.VMEM((DIM, DIM), jnp.bfloat16),
             pltpu.VMEM((ROWS // LANES, LANES), jnp.int32),
-            pltpu.SemaphoreType.DMA((2 + ROWS // GROUP,)),
+            pltpu.VMEM((ROWS // LANES, LANES), jnp.int32),
+            pltpu.SemaphoreType.DMA((3 + ROWS // GROUP,)),
         ],
         compiler_params=params(52),
         cost_estimate=cost(2 * ROWS * DIM * DIM, 5 * MIB),
-    )(x, w, label)
+    )(x, w, label, other)
 
 
 def scale_of(scalars):
@@ -235,11 +238,13 @@
 
 
 def partner_tile_kernel(
-    weight, cols, scalars, first_ref, second_ref, ids, sum_in, loss_in, labels, *rest
+    weight, other, cols, scalars, first_ref, second_ref, ids, sum_in, loss_in, labels, *rest
 ):
     first, last, takes = cols
-    sum_ref, loss_ref = rest[-2:]
-    col_ids = ids_of(labels)[:, first:last]
+    sum_ref, loss_ref, passed = (*rest[len(takes) :], None)[:3]
+    if passed is not None:
+        passed[...] = labels[FIRST:, :]
+    col_ids = ids_of(labels, other)[:, first:last]
     partner = [part[:take, :] for part, take in zip(rest, takes)]
     if len(partner) > 1:
         partner = [jnp.concatenate(partner, axis=0)]
@@ -253,34 +258,62 @@
     loss_ref[...] = total
 
 
-def partner_tile(weight, partner, cols, labels, summed, loss, scalars, own, ids):
+def partner_tile(
+    weight, partner, cols, labels, summed, loss, scalars, own, ids, other=0, passes=False
+):
+    passed = [shape(LABELS, DIM, jnp.bfloat16)] if passes else []
     takes = tuple(part.shape[0] // PIECE * PIECE for part in partner)
     return pl.pallas_call(
-        functools.partial(partner_tile_kernel, weight, (*cols, takes)),
+        functools.partial(partner_tile_kernel, weight, other, (*cols, takes)),
         in_specs=[VMEM] * (7 + len(partner)),
-        out_specs=[VMEM] * 2,
-        out_shape=[shape(ROWS, DIM), shape(8, LANES)],
+        out_specs=[VMEM] * (2 + len(passed)),
+        out_shape=[shape(ROWS, DIM), shape(8, LANES)] + passed,
         compiler_params=params(12),
         cost_estimate=cost(4 * ROWS * (cols[1] - cols[0]) * DIM, 10 * MIB),
     )(scalars, *own, ids, summed, loss, labels, *partner)
 
 
-def partner_projection_kernel(x_ref, w_ref, after, also_after, *pieces):
+def partner_projection_kernel(x_ref, w_ref, after, *pieces):
     for start in range(0, ROWS, STEP):
         unit, _ = normalised(x_ref[start : start + STEP, :], w_ref[...])
         for at in range(0, STEP, PIECE):
             pieces[(start + at) // PIECE][...] = unit[at : at + PIECE, :].astype(jnp.bfloat16)
 
 
-def partner_projection(x, w, after, also_after):
+def partner_projection(x, w, after):
     return pl.pallas_call(
         partner_projection_kernel,
-        in_specs=[VMEM] * 2 + [ANY] * 2,
+        in_specs=[VMEM] * 2 + [ANY],
         out_specs=[VMEM] * (ROWS // PIECE),
         out_shape=[shape(PIECE, DIM, jnp.bfloat16)] * (ROWS // PIECE),
         compiler_params=params(12),
         cost_estimate=cost(2 * ROWS * DIM * DIM, 5 * MIB),
-    )(x, w, after, also_after)
+    )(x, w, after)
+
+
+def sorted_columns_kernel(x_ref, after, out_ref):
+    place = lax.broadcasted_iota(jnp.int32, (DIM, DIM), 1)
+    half, chip, row = place // (DIM // 2), place % (DIM // 2) // 8, place % 8
+    core = lax.axis_index("batch") % 2
+    wanted = 16 * chip + 8 * jnp.where(half == 0, 1 - core, core) + row
+    chosen = jnp.where(lax.broadcasted_iota(jnp.int32, (DIM, DIM), 0) == wanted, 1.0, 0.0)
+    chosen = chosen.astype(jnp.bfloat16)
+    for start in range(0, ROWS, STEP):
+        rows = pl.ds(start, STEP)
+        out_ref[rows, :] = jnp.dot(
+            x_ref[rows, :], chosen, preferred_element_type=jnp.float32
+        ).astype(jnp.bfloat16)
+
+
+def sorted_columns(x, after):
+    return pl.pallas_call(
+        sorted_columns_kernel,
+        in_specs=[VMEM, ANY],
+        out_specs=VMEM,
+        out_shape=shape(ROWS, DIM, jnp.bfloat16),
+        compiler_params=params(12),
+        cost_estimate=cost(2 * ROWS * DIM * DIM, 4 * MIB),
+    )(x, after)
 
 
 def last_kernel(
@@ -295,7 +328,6 @@
     inverse_ref,
     x_ref,
     dproj_ref,
-    kept_ref,
     sent_ref,
 ):
     col_ids = ids_of(far_first)[:, FIRST:]
@@ -307,29 +339,39 @@
         radial = jnp.sum(dunit * unit, axis=1, keepdims=True)
         inverse = inverse_ref[rows, :][:, :1]
         dproj_ref[rows, :] = ((dunit - unit * radial) * inverse).astype(jnp.bfloat16)
-    first = lax.axis_index("batch") % 2 == 0
-    for start in range(0, DIM, STEP):
-        product = lax.dot_general(
+    for start in range(0, DIM // 2, STEP):
+        sent_ref[start : start + STEP, :] = lax.dot_general(
             x_ref[:, start : start + STEP], dproj_ref[...], TN, preferred_element_type=jnp.float32
-        ).reshape(STEP // 16, 2, 8, DIM)
-        even, odd = product[:, 0], product[:, 1]
-        rows = pl.ds(start // 2, STEP // 2)
-        kept_ref[rows, :] = jnp.where(first, even, odd).reshape(STEP // 2, DIM)
-        sent_ref[rows, :] = (
-            jnp.where(first, odd, even).reshape(STEP // 2, DIM).astype(jnp.bfloat16)
+        ).astype(jnp.bfloat16)
+
+
+def kept_kernel(dproj_ref, x_ref, out_ref):
+    for start in range(0, DIM // 2, STEP):
+        out_ref[start : start + STEP, :] = lax.dot_general(
+            x_ref[:, DIM // 2 + start : DIM // 2 + start + STEP],
+            dproj_ref[...],
+            TN,
+            preferred_element_type=jnp.float32,
         )
+
+
+def kept_rows(dproj, x):
+    return pl.pallas_call(
+        kept_kernel,
+        in_specs=[VMEM] * 2,
+        out_specs=VMEM,
+        out_shape=shape(DIM // 2, DIM),
+        compiler_params=params(12),
+        cost_estimate=cost(ROWS * DIM * DIM, 5 * MIB),
+    )(dproj, x)
 
 
 def last(scalars, own, far, ids, summed, unit, inverse, x):
     return pl.pallas_call(
         last_kernel,
         in_specs=[VMEM] * 10,
-        out_specs=[VMEM] * 3,
-        out_shape=[
-            shape(ROWS, DIM, jnp.bfloat16),
-            shape(DIM // 2, DIM),
-            shape(DIM // 2, DIM, jnp.bfloat16),
-        ],
+        out_specs=[VMEM] * 2,
+        out_shape=[shape(ROWS, DIM, jnp.bfloat16), shape(DIM // 2, DIM, jnp.bfloat16)],
         compiler_params=params(12),
         cost_estimate=cost(4 * ROWS * SECOND * DIM + 2 * ROWS * DIM * DIM, 14 * MIB),
     )(scalars, *own, *far, ids, summed, unit, inverse, x)
@@ -415,10 +457,8 @@
 
     labels = label.reshape(ROWS // LANES, LANES)
     near_x = move(x, near)
-    near_labels = move(labels, near)
-    third_labels = move(near_labels, pair)
-
-    *own, unit, inverse = project(x, w, labels)
+
+    *own, unit, inverse = project(x, w, labels, move(labels, pair))
     paired = [move(part, pair) for part in own]
     scalars, ids, summed, loss, *own = own_tile(score_scale, score_shift, own)
     far_first = move(own[0], far)
@@ -426,16 +466,19 @@
     tile = functools.partial(partner_tile, scalars=scalars, own=own, ids=ids)
     whole, early = (0, ROWS), (0, FIRST)
     summed, loss = tile(0.5, paired, whole, paired[0], summed, loss)
-    pieces = partner_projection(near_x, w, loss, near_labels)
+    x_sorted = sorted_columns(x, loss)
+    pieces = partner_projection(near_x, w, x_sorted)
     third = [move(piece, pair) for piece in pieces]
-    summed, loss = tile(None, [far_first], early, far_first, summed, loss)
-    summed, loss = tile(0.5, pieces, whole, near_labels, summed, loss)
-    summed, loss = tile(1.0, third, whole, third_labels, summed, loss)
+    summed, loss, passed = tile(None, [far_first], early, far_first, summed, loss, passes=True)
+    third_labels = move(passed, pair)
+    summed, loss = tile(0.5, pieces, whole, far_first, summed, loss, other=1)
+    summed, loss = tile(1.0, third, whole, third_labels, summed, loss, other=1)
     other_loss = move(loss, pair)
-    dproj, kept, sent = last(
-        scalars, own, [far_first, far_second], ids, summed, unit, inverse, x
+    dproj, sent = last(
+        scalars, own, [far_first, far_second], ids, summed, unit, inverse, x_sorted
     )
     received = move(sent, pair)
+    kept = kept_rows(dproj, x_sorted)
     grad_rows = grad_rows_of(dproj, w)
     chips = count // 2
     groups = [[2 * chip + core for chip in range(chips)] for core in range(2)]

time: 85.8 us -> 84.1 us (0.980)
  starting transfers between devices: 24.1 us -> 18.4 us
  Pallas kernels: 31.7 us -> 33.6 us
  waiting for transfers between devices: 25.5 us -> 27.3 us
    ppermute x12, starting transfers between devices: 16.1 us -> 11.4 us  [move(): lax.ppermute(value, 'batch', [(i, target(i) % count) for i in range(count)])]
    ppermute x12, waiting for transfers between devices: 9 us -> 10.9 us  [move(): lax.ppermute(value, 'batch', [(i, target(i) % count) for i in range(count)])]
    pallas_call x7 -> x9, Pallas kernels: 23.3 us -> 25.2 us  [the longest x4 11.1 us: partner_tile(): pl.pallas_call(functools.partial(partner_tile_kernel, weight, other, (*co...]
    all_to_all x1, starting transfers between devices: 8.04 us -> 7.01 us  [on_device(): lax.all_to_all(parts, 'batch', 0, 0, tiled=True, axis_index_groups=groups)]
    unnamed x12 -> x10, local copies, waits for them, and re-layouts: 2.11 us -> 2.29 us
  transfers between devices with their start and end apart: 13 -> 13, of which waited for: 5 -> 5; matrix products, arithmetic and copies ran while one was open for 0% -> 0% of each run, Pallas kernels for 30% -> 34%
where the time goes in v4:
time: 84.1 us; the launch traced here: 83.8 us
  Pallas kernels  33.6 us (40%)
  waiting for transfers between devices  27.3 us (32%)
  starting transfers between devices  18.4 us (22%)
  local copies, waits for them, and re-layouts  2.29 us (3%)
  between operations  2.16 us (3%)
    all_to_all x1, waiting for transfers between devices, on_device(): lax.all_to_all(parts, 'batch', 0, 0, tiled=True, axis_index_groups=groups)  16.3 us
    ppermute x12, starting transfers between devices, move(): lax.ppermute(value, 'batch', [(i, target(i) % count) for i in range(count)])  11.4 us
    pallas_call x4, Pallas kernels, partner_tile(): pl.pallas_call(functools.partial(partner_tile_kernel, weight, other, (*co...  11.1 us
    ppermute x12, waiting for transfers between devices, move(): lax.ppermute(value, 'batch', [(i, target(i) % count) for i in range(count)])  10.9 us
    all_to_all x1, starting transfers between devices, on_device(): lax.all_to_all(parts, 'batch', 0, 0, tiled=True, axis_index_groups=groups)  7.01 us
    pallas_call x1, Pallas kernels, project(): pl.pallas_call(project_kernel, in_specs=[HBM] * 4, out_specs=[VMEM] * 4,...  5.75 us
    pallas_call x1, Pallas kernels, last(): pl.pallas_call(last_kernel, in_specs=[VMEM] * 10, out_specs=[VMEM] * 2, o...  3.43 us
    pallas_call x1, Pallas kernels, own_tile(): pl.pallas_call(own_tile_kernel, in_specs=[SCALARS] * 2 + [VMEM] * 2, out_...  3.41 us
  transfers between devices with their start and end apart: 13, of which 5 were waited for; matrix products, arithmetic and copies ran while one was open for 0% of the time, Pallas kernels for 34%

profile of v4, /device:TPU:0, one launch (start us, length us, event | category | flops | bytes accessed | tf_op | source)
XLA Modules:
  0.0 83.8 jit_solution(11361218937146853637)
XLA Ops:
  0.6 0.1 collective-permute-start
  0.7 8.9 %collective-permute-start.5 = (bf16[768,1024]{1,0:T(8,128)(2,1)}, bf16[768,1024]{1,0:T(8,128)(2,1)S(1)}, u32[]{:S(2)}, u32[]{:S(2)}) collective-permute-start(bf16[768,1024]{1,0:T(8,128)(2,1)} %x_ref.1), channel_id=1, source_target_pairs={{0,127},{1,2},{2,1},{3,4},{4,3},{5,6},{6,5},{7,8},{8,7},{9,10},{10... | collective-permute-start | bytes 4718600 | tf_op jit(solution)/shard_map/ppermute | solution.py:447
  9.6 0.0 collective-permute-done.other_hbm
  9.6 0.7 copy-done.3
  10.3 5.7 %shard_map.76 = (bf16[272,1024]{1,0:T(8,128)(2,1)S(1)}, bf16[512,1024]{1,0:T(8,128)(2,1)S(1)}, f32[768,1024]{1,0:T(8,128)}, f32[768,128]{1,0:T(8,128)S(1)}) custom-call(bf16[768,1024]{1,0:T(8,128)(2,1)} %x_ref.1, bf16[1024,1024]{1,0:T(8,128)(2,1)} %w_ref.3, s32[6,128]{1,0:T(8,128)S(1)} %bitcast.4, s32[6,128]{1,0:T(8,128)S(1)} %collective-permute-done.other_hbm), custom_call_target="tpu_custom_call" | custom-call | flops 1610612736 | bytes 5242880 | tf_op jit(solution)/shard_map/pallas_call | solution.py:111
  16.0 0.1 collective-permute-start.4
  16.1 0.5 collective-permute-start.3
  17.9 3.4 %shard_map.77 = (f32[8,128]{1,0:T(8,128)S(1)}, f32[768,128]{1,0:T(8,128)S(1)}, f32[768,1024]{1,0:T(8,128)S(1)}, f32[8,128]{1,0:T(8,128)S(1)}, bf16[272,1024]{1,0...) custom-call(f32[1]{0:T(128)S(6)} %copy.8.scale_ref, f32[1]{0:T(128)S(6)} %copy.9.shift_ref, ...), custom_call_target="tpu_custom_call" | custom-call | flops 2415919104 | bytes 5242880 | tf_op jit(solution)/shard_map/pallas_call | solution.py:230
  21.3 0.1 collective-permute-start.1
  21.4 0.3 collective-permute-start.2
  21.7 0.0 collective-permute-done.3.labels.rest_0_
  21.7 0.0 collective-permute-done.4.rest_1_
  21.7 0.0 copy-start.2
  21.7 3.2 %shard_map.78 = (f32[768,1024]{1,0:T(8,128)S(1)}, f32[8,128]{1,0:T(8,128)S(1)}) custom-call(f32[8,128]{1,0:T(8,128)S(1)} %get-tuple-element.31.scalars, bf16[272,1024]{1,0:T(8,128)(2,1)S(1)} %get-tuple-element.32.first_ref, bf16[512,1024]{1,0:T(8,128)(2,1)S(1)} %get-tuple-element.33.second_ref, f32[768,128]{1,0:T(8,128)S(1)} %get-tuple-element.34.ids, ...), custom_call_target="tpu_custom_call" | custom-call | flops 2415919104 | bytes 10485760 | tf_op jit(solution)/shard_map/pallas_call | solution.py:266
  25.0 0.0 copy-done.2
  25.0 0.0 copy-start
  25.0 1.9 %shard_map.80.after.x_ref = bf16[768,1024]{1,0:T(8,128)(2,1)S(1)} custom-call(bf16[768,1024]{1,0:T(8,128)(2,1)S(1)} %copy-done.2, f32[8,128]{1,0:T(8,128)S(1)} %get-tuple-element.38.loss_in.after), custom_call_target="tpu_custom_call" | custom-call | flops 1610612736 | bytes 4194304 | tf_op jit(solution)/shard_map/pallas_call | solution.py:309
  26.9 5.7 %collective-permute-done.5.x_ref = bf16[768,1024]{1,0:T(8,128)(2,1)S(1)} collective-permute-done((bf16[768,1024]{1,0:T(8,128)(2,1)}, bf16[768,1024]{1,0:T(8,128)(2,1)S(1)}, u32[]{:S(2)}, u32[]{:S(2)}) %collective-permute-start.5) | collective-permute-done | bytes 1572896 | tf_op jit(solution)/shard_map/ppermute | solution.py:447
  32.6 0.0 copy-done
  32.6 1.9 %shard_map.81 = (bf16[256,1024]{1,0:T(8,128)(2,1)S(1)}, bf16[256,1024]{1,0:T(8,128)(2,1)S(1)}, bf16[256,1024]{1,0:T(8,128)(2,1)S(1)}) custom-call(bf16[768,1024]{1,0:T(8,128)(2,1)S(1)} %collective-permute-done.5.x_ref, bf16[1024,1024]{1,0:T(8,128)(2,1)S(1)} %copy-done, bf16[768,1024]{1,0:T(8,128)(2,1)S(1)} %shard_map.80.after.x_ref), custom_call_target="tpu_custom_call" | custom-call | flops 1610612736 | bytes 5242880 | tf_op jit(solution)/shard_map/pallas_call | solution.py:284
  34.5 0.1 collective-permute-start.7
  34.6 0.5 collective-permute-start.8
  35.1 0.1 collective-permute-start.9
  35.2 1.2 %collective-permute-done.1.labels.rest_0_.far_first = bf16[272,1024]{1,0:T(8,128)(2,1)S(1)} collective-permute-done((bf16[272,1024]{1,0:T(8,128)(2,1)S(1)}, bf16[272,1024]{1,0:T(8,128)(2,1)S(1)}, u32[]{:S(2)}, u32[]{:S(2)}) %collective-permute-start.1) | collective-permute-done | bytes 557088 | tf_op jit(solution)/shard_map/ppermute | solution.py:447
  36.4 1.4 %shard_map.79 = (f32[768,1024]{1,0:T(8,128)S(1)}, f32[8,128]{1,0:T(8,128)S(1)}, bf16[16,1024]{1,0:T(8,128)(2,1)S(1)}) custom-call(f32[8,128]{1,0:T(8,128)S(1)} %get-tuple-element.31.scalars, bf16[272,1024]{1,0:T(8,128)(2,1)S(1)} %get-tuple-element.32.first_ref, bf16[512,1024]{1,0:T(8,128)(2,1)S(1)} %get-tuple-element.33.second_ref, ...), custom_call_target="tpu_custom_call" | custom-call | flops 805306368 | bytes 10485760 | tf_op jit(solution)/shard_map/pallas_call | solution.py:266
  37.8 0.3 collective-permute-start.6
  38.1 3.2 %shard_map.82 = (f32[768,1024]{1,0:T(8,128)S(1)}, f32[8,128]{1,0:T(8,128)S(1)}) custom-call(f32[8,128]{1,0:T(8,128)S(1)} %get-tuple-element.31.scalars, bf16[272,1024]{1,0:T(8,128)(2,1)S(1)} %get-tuple-element.32.first_ref, bf16[512,1024]{1,0:T(8,128)(2,1)S(1)} %get-tuple-element.33.second_ref, f32[768,128]{1,0:T(8,128)S(1)} %get-tuple-element.34.ids, ...), custom_call_target="tpu_custom_call" | custom-call | flops 2415919104 | bytes 10485760 | tf_op jit(solution)/shard_map/pallas_call | solution.py:266
  41.3 0.0 collective-permute-done.6.labels
  41.3 0.0 collective-permute-done.7.rest_0_
  41.3 0.0 collective-permute-done.8.rest_1_
  41.3 0.0 collective-permute-done.9.rest_2_
  41.4 0.0 copy-start.4
  41.4 3.3 %shard_map.83 = (f32[768,1024]{1,0:T(8,128)S(1)}, f32[8,128]{1,0:T(8,128)S(1)}) custom-call(f32[8,128]{1,0:T(8,128)S(1)} %get-tuple-element.31.scalars, bf16[272,1024]{1,0:T(8,128)(2,1)S(1)} %get-tuple-element.32.first_ref, bf16[512,1024]{1,0:T(8,128)(2,1)S(1)} %get-tuple-element.33.second_ref, f32[768,128]{1,0:T(8,128)S(1)} %get-tuple-element.34.ids, ...), custom_call_target="tpu_custom_call" | custom-call | flops 2415919104 | bytes 10485760 | tf_op jit(solution)/shard_map/pallas_call | solution.py:266
  44.7 2.9 %collective-permute-done.2.far_ref = bf16[512,1024]{1,0:T(8,128)(2,1)S(1)} collective-permute-done((bf16[512,1024]{1,0:T(8,128)(2,1)S(1)}, bf16[512,1024]{1,0:T(8,128)(2,1)S(1)}, u32[]{:S(2)}, u32[]{:S(2)}) %collective-permute-start.2) | collective-permute-done | bytes 1048608 | tf_op jit(solution)/shard_map/ppermute | solution.py:447
  47.6 0.0 copy-done.4
  47.6 3.4 %shard_map.84 = (bf16[768,1024]{1,0:T(8,128)(2,1)S(1)}, bf16[512,1024]{1,0:T(8,128)(2,1)S(1)}) custom-call(f32[8,128]{1,0:T(8,128)S(1)} %get-tuple-element.31.scalars, bf16[272,1024]{1,0:T(8,128)(2,1)S(1)} %get-tuple-element.32.first_ref, bf16[512,1024]{1,0:T(8,128)(2,1)S(1)} %get-tuple-element.33.second_ref, ...), custom_call_target="tpu_custom_call" | custom-call | flops 3221225472 | bytes 14680064 | tf_op jit(solution)/shard_map/pallas_call | solution.py:370
  51.0 0.1 collective-permute-start.10
  51.1 0.5 collective-permute-start.11
  51.6 1.0 %shard_map.85.kept_ref = f32[512,1024]{1,0:T(8,128)S(1)} custom-call(bf16[768,1024]{1,0:T(8,128)(2,1)S(1)} %get-tuple-element.50.dproj_ref, bf16[768,1024]{1,0:T(8,128)(2,1)S(1)} %shard_map.80.after.x_ref), custom_call_target="tpu_custom_call" | custom-call | flops 805306368 | bytes 5242880 | tf_op jit(solution)/shard_map/pallas_call | solution.py:359
  52.7 1.1 %collective-permute-done.11.other_loss_ref = f32[8,128]{1,0:T(8,128)S(1)} collective-permute-done((f32[8,128]{1,0:T(8,128)S(1)}, f32[8,128]{1,0:T(8,128)S(1)}, u32[]{:S(2)}, u32[]{:S(2)}) %collective-permute-start.11) | collective-permute-done | bytes 4128 | tf_op jit(solution)/shard_map/ppermute | solution.py:447
  53.8 0.0 collective-permute-done.10.received_ref
  53.8 1.3 %shard_map.86 = bf16[512,1152]{1,0:T(8,128)(2,1)} custom-call(f32[512,1024]{1,0:T(8,128)S(1)} %shard_map.85.kept_ref, bf16[512,1024]{1,0:T(8,128)(2,1)S(1)} %collective-permute-done.10.received_ref, f32[8,128]{1,0:T(8,128)S(1)} %get-tuple-element.52.loss_ref, f32[8,128]{1,0:T(8,128)S(1)} %collective-permute-done.11.other_loss_ref), custom_call_target="tpu_custom_call" | custom-call | flops 1048576 | bytes 5242880 | tf_op jit(solution)/shard_map/pallas_call | solution.py:414
  55.1 7.0 %all-to-all-start = ((bf16[64,8,1152]{2,1,0:T(8,128)(2,1)}), bf16[64,8,1152]{2,1,0:T(8,128)(2,1)S(1)}, u32[]{:S(2)}, u32[]{:S(2)}) async-start(bf16[64,8,1152]{2,1,0:T(8,128)(2,1)} %bitcast.1), calls=%async_computation | async-start | bytes 2359296 | tf_op jit(solution)/shard_map/all_to_all | solution.py:486
  62.1 0.0 copy-start.1
  62.1 1.6 %copy-done.1 = bf16[1024,1024]{1,0:T(8,128)(2,1)S(1)} copy-done((bf16[1024,1024]{1,0:T(8,128)(2,1)S(1)}, bf16[1024,1024]{1,0:T(8,128)(2,1)}, u32[]{:S(2)}) %copy-start.1) | copy-done | bytes 2097176
  63.7 3.0 %shard_map.88 = bf16[768,1024]{1,0:T(8,128)(2,1)} custom-call(bf16[768,1024]{1,0:T(8,128)(2,1)S(1)} %get-tuple-element.50.dproj_ref, bf16[1024,1024]{1,0:T(8,128)(2,1)S(1)} %copy-done.1), custom_call_target="tpu_custom_call" | custom-call | flops 1610612736 | bytes 5242880 | tf_op jit(solution)/shard_map/pallas_call | solution.py:389
  66.7 16.3 %all-to-all-done.parts_ref = bf16[64,8,1152]{2,1,0:T(8,128)(2,1)S(1)} async-done(((bf16[64,8,1152]{2,1,0:T(8,128)(2,1)}), bf16[64,8,1152]{2,1,0:T(8,128)(2,1)S(1)}, u32[]{:S(2)}, u32[]{:S(2)}) %all-to-all-start) | async-done | bytes 1179680 | tf_op jit(solution)/shard_map/all_to_all | solution.py:486
  83.0 0.8 shard_map.87
  (1 shorter events, 0.0 us)
Async XLA Ops:
  0.6 9.0 %collective-permute-start = (s32[6,128]{1,0:T(8,128)}, s32[6,128]{1,0:T(8,128)S(1)}, u32[]{:S(2)}, u32[]{:S(2)}) collective-permute-start(s32[6,128]{1,0:T(8,128)} %bitcast.3), channel_id=1, source_target_pairs={{0,1},{1,0},{2,3},{3,2},{4,5},{5,4},{6,7},{7,6},{8,9},{9,8},{10,11... | collective-permute-start | bytes 9224 | tf_op jit(solution)/shard_map/ppermute | solution.py:447
  0.7 31.8 %collective-permute-start.5 = (bf16[768,1024]{1,0:T(8,128)(2,1)}, bf16[768,1024]{1,0:T(8,128)(2,1)S(1)}, u32[]{:S(2)}, u32[]{:S(2)}) collective-permute-start(bf16[768,1024]{1,0:T(8,128)(2,1)} %x_ref.1), channel_id=1, source_target_pairs={{0,127},{1,2},{2,1},{3,4},{4,3},{5,6},{6,5},{7,8},{8,7},{9,10},{10... | collective-permute-start | bytes 4718600 | tf_op jit(solution)/shard_map/ppermute | solution.py:447
  9.6 0.7 copy-start.3
  16.0 5.7 %collective-permute-start.4 = (bf16[512,1024]{1,0:T(8,128)(2,1)S(1)}, bf16[512,1024]{1,0:T(8,128)(2,1)S(1)}, u32[]{:S(2)}, u32[]{:S(2)}) collective-permute-start(bf16[512,1024]{1,0:T(8,128)(2,1)S(1)} %get-tuple-element.30.second_ref), channel_id=1, source_target_pairs={{0,1},{1,0},{2,3},{3,2},{4,5},{5,4},{6,7},{7,6},{8,9},{9,8},{10,11... | collective-permute-start | bytes 3145736 | tf_op jit(solution)/shard_map/ppermute | solution.py:447
  16.1 5.6 %collective-permute-start.3 = (bf16[272,1024]{1,0:T(8,128)(2,1)S(1)}, bf16[272,1024]{1,0:T(8,128)(2,1)S(1)}, u32[]{:S(2)}, u32[]{:S(2)}) collective-permute-start(bf16[272,1024]{1,0:T(8,128)(2,1)S(1)} %get-tuple-element.29.first_ref), channel_id=1, source_target_pairs={{0,1},{1,0},{2,3},{3,2},{4,5},{5,4},{6,7},{7,6},{8,9},{9,8},{10,11... | collective-permute-start | bytes 1671176 | tf_op jit(solution)/shard_map/ppermute | solution.py:447
  21.3 15.0 %collective-permute-start.1 = (bf16[272,1024]{1,0:T(8,128)(2,1)S(1)}, bf16[272,1024]{1,0:T(8,128)(2,1)S(1)}, u32[]{:S(2)}, u32[]{:S(2)}) collective-permute-start(bf16[272,1024]{1,0:T(8,128)(2,1)S(1)} %get-tuple-element.32.first_ref), channel_id=1, source_target_pairs={{0,2},{1,127},{2,4},{3,1},{4,6},{5,3},{6,8},{7,5},{8,10},{9,7},{10... | collective-permute-start | bytes 1671176 | tf_op jit(solution)/shard_map/ppermute | solution.py:447
  21.4 26.2 %collective-permute-start.2 = (bf16[512,1024]{1,0:T(8,128)(2,1)S(1)}, bf16[512,1024]{1,0:T(8,128)(2,1)S(1)}, u32[]{:S(2)}, u32[]{:S(2)}) collective-permute-start(bf16[512,1024]{1,0:T(8,128)(2,1)S(1)} %get-tuple-element.33.second_ref), channel_id=1, source_target_pairs={{0,2},{1,127},{2,4},{3,1},{4,6},{5,3},{6,8},{7,5},{8,10},{9,7},{10... | collective-permute-start | bytes 3145736 | tf_op jit(solution)/shard_map/ppermute | solution.py:447
  21.7 3.3 %copy-start.2 = (bf16[768,1024]{1,0:T(8,128)(2,1)S(1)}, bf16[768,1024]{1,0:T(8,128)(2,1)}, u32[]{:S(2)}) copy-start(bf16[768,1024]{1,0:T(8,128)(2,1)} %x_ref.1) | copy-start | bytes 4718596
  25.0 7.6 %copy-start = (bf16[1024,1024]{1,0:T(8,128)(2,1)S(1)}, bf16[1024,1024]{1,0:T(8,128)(2,1)}, u32[]{:S(2)}) copy-start(bf16[1024,1024]{1,0:T(8,128)(2,1)} %w_ref.3) | copy-start | bytes 6291460
  34.5 6.8 %collective-permute-start.7 = (bf16[256,1024]{1,0:T(8,128)(2,1)S(1)}, bf16[256,1024]{1,0:T(8,128)(2,1)S(1)}, u32[]{:S(2)}, u32[]{:S(2)}) collective-permute-start(bf16[256,1024]{1,0:T(8,128)(2,1)S(1)} %get-tuple-element.41.rest_0_), channel_id=1, source_target_pairs={{0,1},{1,0},{2,3},{3,2},{4,5},{5,4},{6,7},{7,6},{8,9},{9,8},{10,11... | collective-permute-start | bytes 1572872 | tf_op jit(solution)/shard_map/ppermute | solution.py:447
  34.6 6.7 %collective-permute-start.8 = (bf16[256,1024]{1,0:T(8,128)(2,1)S(1)}, bf16[256,1024]{1,0:T(8,128)(2,1)S(1)}, u32[]{:S(2)}, u32[]{:S(2)}) collective-permute-start(bf16[256,1024]{1,0:T(8,128)(2,1)S(1)} %get-tuple-element.42.rest_1_), channel_id=1, source_target_pairs={{0,1},{1,0},{2,3},{3,2},{4,5},{5,4},{6,7},{7,6},{8,9},{9,8},{10,11... | collective-permute-start | bytes 1572872 | tf_op jit(solution)/shard_map/ppermute | solution.py:447
  35.1 6.3 %collective-permute-start.9 = (bf16[256,1024]{1,0:T(8,128)(2,1)S(1)}, bf16[256,1024]{1,0:T(8,128)(2,1)S(1)}, u32[]{:S(2)}, u32[]{:S(2)}) collective-permute-start(bf16[256,1024]{1,0:T(8,128)(2,1)S(1)} %get-tuple-element.43.rest_2_), channel_id=1, source_target_pairs={{0,1},{1,0},{2,3},{3,2},{4,5},{5,4},{6,7},{7,6},{8,9},{9,8},{10,11... | collective-permute-start | bytes 1572872 | tf_op jit(solution)/shard_map/ppermute | solution.py:447
  37.8 3.6 %collective-permute-start.6 = (bf16[16,1024]{1,0:T(8,128)(2,1)S(1)}, bf16[16,1024]{1,0:T(8,128)(2,1)S(1)}, u32[]{:S(2)}, u32[]{:S(2)}) collective-permute-start(bf16[16,1024]{1,0:T(8,128)(2,1)S(1)} %get-tuple-element.46), channel_id=1, source_target_pairs={{0,1},{1,0},{2,3},{3,2},{4,5},{5,4},{6,7},{7,6},{8,9},{9,8},{10,11... | collective-permute-start | bytes 98312 | tf_op jit(solution)/shard_map/ppermute | solution.py:447
  41.4 6.3 %copy-start.4 = (f32[768,1024]{1,0:T(8,128)S(1)}, f32[768,1024]{1,0:T(8,128)}, u32[]{:S(2)}) copy-start(f32[768,1024]{1,0:T(8,128)} %get-tuple-element.48.unit_ref) | copy-start | bytes 9437188
  51.0 2.7 %collective-permute-start.10 = (bf16[512,1024]{1,0:T(8,128)(2,1)S(1)}, bf16[512,1024]{1,0:T(8,128)(2,1)S(1)}, u32[]{:S(2)}, u32[]{:S(2)}) collective-permute-start(bf16[512,1024]{1,0:T(8,128)(2,1)S(1)} %get-tuple-element.51), channel_id=1, source_target_pairs={{0,1},{1,0},{2,3},{3,2},{4,5},{5,4},{6,7},{7,6},{8,9},{9,8},{10,11... | collective-permute-start | bytes 3145736 | tf_op jit(solution)/shard_map/ppermute | solution.py:447
  51.1 2.7 %collective-permute-start.11 = (f32[8,128]{1,0:T(8,128)S(1)}, f32[8,128]{1,0:T(8,128)S(1)}, u32[]{:S(2)}, u32[]{:S(2)}) collective-permute-start(f32[8,128]{1,0:T(8,128)S(1)} %get-tuple-element.52.loss_ref), channel_id=1, source_target_pairs={{0,1},{1,0},{2,3},{3,2},{4,5},{5,4},{6,7},{7,6},{8,9},{9,8},{10,11... | collective-permute-start | bytes 12296 | tf_op jit(solution)/shard_map/ppermute | solution.py:447
  55.1 27.9 %all-to-all-start = ((bf16[64,8,1152]{2,1,0:T(8,128)(2,1)}), bf16[64,8,1152]{2,1,0:T(8,128)(2,1)S(1)}, u32[]{:S(2)}, u32[]{:S(2)}) async-start(bf16[64,8,1152]{2,1,0:T(8,128)(2,1)} %bitcast.1), calls=%async_computation | async-start | bytes 2359296 | tf_op jit(solution)/shard_map/all_to_all | solution.py:486
  62.1 1.6 %copy-start.1 = (bf16[1024,1024]{1,0:T(8,128)(2,1)S(1)}, bf16[1024,1024]{1,0:T(8,128)(2,1)}, u32[]{:S(2)}) copy-start(bf16[1024,1024]{1,0:T(8,128)(2,1)} %w_ref.3) | copy-start | bytes 6291460

commit v5 on v4

--- a/solution.py
+++ b/solution.py
@@ -238,10 +238,10 @@
 
 
 def partner_tile_kernel(
-    weight, other, cols, scalars, first_ref, second_ref, ids, sum_in, loss_in, labels, *rest
+    weight, other, waits, cols, scalars, first_ref, second_ref, ids, sum_in, loss_in, labels, *rest
 ):
     first, last, takes = cols
-    sum_ref, loss_ref, passed = (*rest[len(takes) :], None)[:3]
+    sum_ref, loss_ref, passed = (*rest[len(takes) + waits :], None)[:3]
     if passed is not None:
         passed[...] = labels[FIRST:, :]
     col_ids = ids_of(labels, other)[:, first:last]
@@ -259,18 +259,18 @@
 
 
 def partner_tile(
-    weight, partner, cols, labels, summed, loss, scalars, own, ids, other=0, passes=False
+    weight, partner, cols, labels, summed, loss, scalars, own, ids, other=0, passes=False, after=()
 ):
     passed = [shape(LABELS, DIM, jnp.bfloat16)] if passes else []
     takes = tuple(part.shape[0] // PIECE * PIECE for part in partner)
     return pl.pallas_call(
-        functools.partial(partner_tile_kernel, weight, other, (*cols, takes)),
-        in_specs=[VMEM] * (7 + len(partner)),
+        functools.partial(partner_tile_kernel, weight, other, len(after), (*cols, takes)),
+        in_specs=[VMEM] * (7 + len(partner)) + [ANY] * len(after),
         out_specs=[VMEM] * (2 + len(passed)),
         out_shape=[shape(ROWS, DIM), shape(8, LANES)] + passed,
         compiler_params=params(12),
         cost_estimate=cost(4 * ROWS * (cols[1] - cols[0]) * DIM, 10 * MIB),
-    )(scalars, *own, ids, summed, loss, labels, *partner)
+    )(scalars, *own, ids, summed, loss, labels, *partner, *after)
 
 
 def partner_projection_kernel(x_ref, w_ref, after, *pieces):
@@ -465,9 +465,9 @@
     far_second = move(own[1], far)
     tile = functools.partial(partner_tile, scalars=scalars, own=own, ids=ids)
     whole, early = (0, ROWS), (0, FIRST)
-    summed, loss = tile(0.5, paired, whole, paired[0], summed, loss)
     x_sorted = sorted_columns(x, loss)
-    pieces = partner_projection(near_x, w, x_sorted)
+    summed, loss = tile(0.5, paired, whole, paired[0], summed, loss, after=(x_sorted,))
+    pieces = partner_projection(near_x, w, loss)
     third = [move(piece, pair) for piece in pieces]
     summed, loss, passed = tile(None, [far_first], early, far_first, summed, loss, passes=True)
     third_labels = move(passed, pair)

time: 84.1 us -> 83.4 us (level)
  starting transfers between devices: 18.4 us -> 16.4 us
  waiting for transfers between devices: 27.3 us -> 28.6 us
    all_to_all x1, starting transfers between devices: 7.01 us -> 5.61 us  [on_device(): lax.all_to_all(parts, 'batch', 0, 0, tiled=True, axis_index_groups=groups)]
    ppermute x12, waiting for transfers between devices: 10.9 us -> 12.2 us  [move(): lax.ppermute(value, 'batch', [(i, target(i) % count) for i in range(count)])]
  transfers between devices with their start and end apart: 13 -> 13, of which waited for: 5 -> 6; matrix products, arithmetic and copies ran while one was open for 0% -> 0% of each run, Pallas kernels for 34% -> 34%
where the time goes in v5:
time: 83.4 us; the launch traced here: 83.1 us
  Pallas kernels  33.7 us (40%)
  waiting for transfers between devices  28.6 us (34%)
  starting transfers between devices  16.4 us (20%)
  local copies, waits for them, and re-layouts  2.29 us (3%)
  between operations  2.15 us (3%)
    all_to_all x1, waiting for transfers between devices, on_device(): lax.all_to_all(parts, 'batch', 0, 0, tiled=True, axis_index_groups=groups)  16.3 us
    ppermute x12, waiting for transfers between devices, move(): lax.ppermute(value, 'batch', [(i, target(i) % count) for i in range(count)])  12.2 us
    pallas_call x4, Pallas kernels, partner_tile(): pl.pallas_call(functools.partial(partner_tile_kernel, weight, other, len(...  11.2 us
    ppermute x12, starting transfers between devices, move(): lax.ppermute(value, 'batch', [(i, target(i) % count) for i in range(count)])  10.8 us
    pallas_call x1, Pallas kernels, project(): pl.pallas_call(project_kernel, in_specs=[HBM] * 4, out_specs=[VMEM] * 4,...  5.75 us
    all_to_all x1, starting transfers between devices, on_device(): lax.all_to_all(parts, 'batch', 0, 0, tiled=True, axis_index_groups=groups)  5.61 us
    pallas_call x1, Pallas kernels, last(): pl.pallas_call(last_kernel, in_specs=[VMEM] * 10, out_specs=[VMEM] * 2, o...  3.46 us
    pallas_call x1, Pallas kernels, own_tile(): pl.pallas_call(own_tile_kernel, in_specs=[SCALARS] * 2 + [VMEM] * 2, out_...  3.41 us
  transfers between devices with their start and end apart: 13, of which 6 were waited for; matrix products, arithmetic and copies ran while one was open for 0% of the time, Pallas kernels for 34%

profile of v5, /device:TPU:0, one launch (start us, length us, event | category | flops | bytes accessed | tf_op | source)
XLA Modules:
  0.0 83.1 jit_solution(7451887414811146635)
XLA Ops:
  0.6 8.3 %collective-permute-start.5 = (bf16[768,1024]{1,0:T(8,128)(2,1)}, bf16[768,1024]{1,0:T(8,128)(2,1)S(1)}, u32[]{:S(2)}, u32[]{:S(2)}) collective-permute-start(bf16[768,1024]{1,0:T(8,128)(2,1)} %x_ref.1), channel_id=1, source_target_pairs={{0,127},{1,2},{2,1},{3,4},{4,3},{5,6},{6,5},{7,8},{8,7},{9,10},{10... | collective-permute-start | bytes 4718600 | tf_op jit(solution)/shard_map/ppermute | solution.py:447
  8.9 0.0 collective-permute-start
  8.9 1.4 %collective-permute-done.other_hbm = s32[6,128]{1,0:T(8,128)S(1)} collective-permute-done((s32[6,128]{1,0:T(8,128)}, s32[6,128]{1,0:T(8,128)S(1)}, u32[]{:S(2)}, u32[]{:S(2)}) %collective-permute-start) | collective-permute-done | bytes 3104 | tf_op jit(solution)/shard_map/ppermute | solution.py:447
  10.3 0.7 copy-done.3
  11.0 5.7 %shard_map.76 = (bf16[272,1024]{1,0:T(8,128)(2,1)S(1)}, bf16[512,1024]{1,0:T(8,128)(2,1)S(1)}, f32[768,1024]{1,0:T(8,128)}, f32[768,128]{1,0:T(8,128)S(1)}) custom-call(bf16[768,1024]{1,0:T(8,128)(2,1)} %x_ref.1, bf16[1024,1024]{1,0:T(8,128)(2,1)} %w_ref.3, s32[6,128]{1,0:T(8,128)S(1)} %bitcast.4, s32[6,128]{1,0:T(8,128)S(1)} %collective-permute-done.other_hbm), custom_call_target="tpu_custom_call" | custom-call | flops 1610612736 | bytes 5242880 | tf_op jit(solution)/shard_map/pallas_call | solution.py:111
  16.7 0.3 collective-permute-start.4
  17.0 0.3 collective-permute-start.3
  18.6 0.0 copy-start.2
  18.6 3.4 %shard_map.77 = (f32[8,128]{1,0:T(8,128)S(1)}, f32[768,128]{1,0:T(8,128)S(1)}, f32[768,1024]{1,0:T(8,128)S(1)}, f32[8,128]{1,0:T(8,128)S(1)}, bf16[272,1024]{1,0...) custom-call(f32[1]{0:T(128)S(6)} %copy.8.scale_ref, f32[1]{0:T(128)S(6)} %copy.9.shift_ref, ...), custom_call_target="tpu_custom_call" | custom-call | flops 2415919104 | bytes 5242880 | tf_op jit(solution)/shard_map/pallas_call | solution.py:230
  22.1 0.1 collective-permute-start.1
  22.1 0.3 collective-permute-start.2
  22.4 0.0 copy-done.2
  22.4 1.9 %shard_map.78.rest_2_.x_ref = bf16[768,1024]{1,0:T(8,128)(2,1)S(1)} custom-call(bf16[768,1024]{1,0:T(8,128)(2,1)S(1)} %copy-done.2, f32[8,128]{1,0:T(8,128)S(1)} %get-tuple-element.36.after.loss_in), custom_call_target="tpu_custom_call" | custom-call | flops 1610612736 | bytes 4194304 | tf_op jit(solution)/shard_map/pallas_call | solution.py:309
  24.3 0.0 collective-permute-done.3.labels.rest_0_
  24.3 0.0 collective-permute-done.4.rest_1_
  24.3 0.0 copy-start
  24.3 3.2 %shard_map.79 = (f32[768,1024]{1,0:T(8,128)S(1)}, f32[8,128]{1,0:T(8,128)S(1)}) custom-call(f32[8,128]{1,0:T(8,128)S(1)} %get-tuple-element.31.scalars, bf16[272,1024]{1,0:T(8,128)(2,1)S(1)} %get-tuple-element.32.first_ref, bf16[512,1024]{1,0:T(8,128)(2,1)S(1)} %get-tuple-element.33.second_ref, f32[768,128]{1,0:T(8,128)S(1)} %get-tuple-element.34.ids, ...), custom_call_target="tpu_custom_call" | custom-call | flops 2415919104 | bytes 10485760 | tf_op jit(solution)/shard_map/pallas_call | solution.py:266
  27.6 3.3 %collective-permute-done.5.x_ref = bf16[768,1024]{1,0:T(8,128)(2,1)S(1)} collective-permute-done((bf16[768,1024]{1,0:T(8,128)(2,1)}, bf16[768,1024]{1,0:T(8,128)(2,1)S(1)}, u32[]{:S(2)}, u32[]{:S(2)}) %collective-permute-start.5) | collective-permute-done | bytes 1572896 | tf_op jit(solution)/shard_map/ppermute | solution.py:447
  30.9 0.0 copy-done
  30.9 1.9 %shard_map.81 = (bf16[256,1024]{1,0:T(8,128)(2,1)S(1)}, bf16[256,1024]{1,0:T(8,128)(2,1)S(1)}, bf16[256,1024]{1,0:T(8,128)(2,1)S(1)}) custom-call(bf16[768,1024]{1,0:T(8,128)(2,1)S(1)} %collective-permute-done.5.x_ref, bf16[1024,1024]{1,0:T(8,128)(2,1)S(1)} %copy-done, f32[8,128]{1,0:T(8,128)S(1)} %get-tuple-element.38.loss_in.after), custom_call_target="tpu_custom_call" | custom-call | flops 1610612736 | bytes 5242880 | tf_op jit(solution)/shard_map/pallas_call | solution.py:284
  32.9 0.1 collective-permute-start.7
  33.0 0.5 collective-permute-start.8
  33.5 0.1 collective-permute-start.9
  33.5 3.5 %collective-permute-done.1.labels.rest_0_.far_first = bf16[272,1024]{1,0:T(8,128)(2,1)S(1)} collective-permute-done((bf16[272,1024]{1,0:T(8,128)(2,1)S(1)}, bf16[272,1024]{1,0:T(8,128)(2,1)S(1)}, u32[]{:S(2)}, u32[]{:S(2)}) %collective-permute-start.1) | collective-permute-done | bytes 557088 | tf_op jit(solution)/shard_map/ppermute | solution.py:447
  37.1 1.4 %shard_map.80 = (f32[768,1024]{1,0:T(8,128)S(1)}, f32[8,128]{1,0:T(8,128)S(1)}, bf16[16,1024]{1,0:T(8,128)(2,1)S(1)}) custom-call(f32[8,128]{1,0:T(8,128)S(1)} %get-tuple-element.31.scalars, bf16[272,1024]{1,0:T(8,128)(2,1)S(1)} %get-tuple-element.32.first_ref, bf16[512,1024]{1,0:T(8,128)(2,1)S(1)} %get-tuple-element.33.second_ref, ...), custom_call_target="tpu_custom_call" | custom-call | flops 805306368 | bytes 10485760 | tf_op jit(solution)/shard_map/pallas_call | solution.py:266
  38.5 0.3 collective-permute-start.6
  38.8 3.3 %shard_map.82 = (f32[768,1024]{1,0:T(8,128)S(1)}, f32[8,128]{1,0:T(8,128)S(1)}) custom-call(f32[8,128]{1,0:T(8,128)S(1)} %get-tuple-element.31.scalars, bf16[272,1024]{1,0:T(8,128)(2,1)S(1)} %get-tuple-element.32.first_ref, bf16[512,1024]{1,0:T(8,128)(2,1)S(1)} %get-tuple-element.33.second_ref, f32[768,128]{1,0:T(8,128)S(1)} %get-tuple-element.34.ids, ...), custom_call_target="tpu_custom_call" | custom-call | flops 2415919104 | bytes 10485760 | tf_op jit(solution)/shard_map/pallas_call | solution.py:266
  42.1 0.0 collective-permute-done.6.labels
  42.1 0.0 collective-permute-done.7.rest_0_
  42.1 0.0 collective-permute-done.8.rest_1_
  42.1 0.0 collective-permute-done.9.rest_2_
  42.1 0.0 copy-start.4
  42.1 3.3 %shard_map.83 = (f32[768,1024]{1,0:T(8,128)S(1)}, f32[8,128]{1,0:T(8,128)S(1)}) custom-call(f32[8,128]{1,0:T(8,128)S(1)} %get-tuple-element.31.scalars, bf16[272,1024]{1,0:T(8,128)(2,1)S(1)} %get-tuple-element.32.first_ref, bf16[512,1024]{1,0:T(8,128)(2,1)S(1)} %get-tuple-element.33.second_ref, f32[768,128]{1,0:T(8,128)S(1)} %get-tuple-element.34.ids, ...), custom_call_target="tpu_custom_call" | custom-call | flops 2415919104 | bytes 10485760 | tf_op jit(solution)/shard_map/pallas_call | solution.py:266
  45.4 2.9 %collective-permute-done.2.far_ref = bf16[512,1024]{1,0:T(8,128)(2,1)S(1)} collective-permute-done((bf16[512,1024]{1,0:T(8,128)(2,1)S(1)}, bf16[512,1024]{1,0:T(8,128)(2,1)S(1)}, u32[]{:S(2)}, u32[]{:S(2)}) %collective-permute-start.2) | collective-permute-done | bytes 1048608 | tf_op jit(solution)/shard_map/ppermute | solution.py:447
  48.3 0.0 copy-done.4
  48.3 3.5 %shard_map.84 = (bf16[768,1024]{1,0:T(8,128)(2,1)S(1)}, bf16[512,1024]{1,0:T(8,128)(2,1)S(1)}) custom-call(f32[8,128]{1,0:T(8,128)S(1)} %get-tuple-element.31.scalars, bf16[272,1024]{1,0:T(8,128)(2,1)S(1)} %get-tuple-element.32.first_ref, bf16[512,1024]{1,0:T(8,128)(2,1)S(1)} %get-tuple-element.33.second_ref, ...), custom_call_target="tpu_custom_call" | custom-call | flops 3221225472 | bytes 14680064 | tf_op jit(solution)/shard_map/pallas_call | solution.py:370
  51.8 0.1 collective-permute-start.10
  51.9 0.5 collective-permute-start.11
  52.4 1.0 %shard_map.85.kept_ref = f32[512,1024]{1,0:T(8,128)S(1)} custom-call(bf16[768,1024]{1,0:T(8,128)(2,1)S(1)} %get-tuple-element.50.dproj_ref, bf16[768,1024]{1,0:T(8,128)(2,1)S(1)} %shard_map.78.rest_2_.x_ref), custom_call_target="tpu_custom_call" | custom-call | flops 805306368 | bytes 5242880 | tf_op jit(solution)/shard_map/pallas_call | solution.py:359
  53.4 1.1 %collective-permute-done.11.other_loss_ref = f32[8,128]{1,0:T(8,128)S(1)} collective-permute-done((f32[8,128]{1,0:T(8,128)S(1)}, f32[8,128]{1,0:T(8,128)S(1)}, u32[]{:S(2)}, u32[]{:S(2)}) %collective-permute-start.11) | collective-permute-done | bytes 4128 | tf_op jit(solution)/shard_map/ppermute | solution.py:447
  54.5 0.0 collective-permute-done.10.received_ref
  54.5 1.3 %shard_map.86 = bf16[512,1152]{1,0:T(8,128)(2,1)} custom-call(f32[512,1024]{1,0:T(8,128)S(1)} %shard_map.85.kept_ref, bf16[512,1024]{1,0:T(8,128)(2,1)S(1)} %collective-permute-done.10.received_ref, f32[8,128]{1,0:T(8,128)S(1)} %get-tuple-element.52.loss_ref, f32[8,128]{1,0:T(8,128)S(1)} %collective-permute-done.11.other_loss_ref), custom_call_target="tpu_custom_call" | custom-call | flops 1048576 | bytes 5242880 | tf_op jit(solution)/shard_map/pallas_call | solution.py:414
  55.8 5.6 %all-to-all-start = ((bf16[64,8,1152]{2,1,0:T(8,128)(2,1)}), bf16[64,8,1152]{2,1,0:T(8,128)(2,1)S(1)}, u32[]{:S(2)}, u32[]{:S(2)}) async-start(bf16[64,8,1152]{2,1,0:T(8,128)(2,1)} %bitcast.1), calls=%async_computation | async-start | bytes 2359296 | tf_op jit(solution)/shard_map/all_to_all | solution.py:486
  61.5 0.0 copy-start.1
  61.5 1.6 %copy-done.1 = bf16[1024,1024]{1,0:T(8,128)(2,1)S(1)} copy-done((bf16[1024,1024]{1,0:T(8,128)(2,1)S(1)}, bf16[1024,1024]{1,0:T(8,128)(2,1)}, u32[]{:S(2)}) %copy-start.1) | copy-done | bytes 2097176
  63.0 3.0 %shard_map.88 = bf16[768,1024]{1,0:T(8,128)(2,1)} custom-call(bf16[768,1024]{1,0:T(8,128)(2,1)S(1)} %get-tuple-element.50.dproj_ref, bf16[1024,1024]{1,0:T(8,128)(2,1)S(1)} %copy-done.1), custom_call_target="tpu_custom_call" | custom-call | flops 1610612736 | bytes 5242880 | tf_op jit(solution)/shard_map/pallas_call | solution.py:389
  66.0 16.3 %all-to-all-done.parts_ref = bf16[64,8,1152]{2,1,0:T(8,128)(2,1)S(1)} async-done(((bf16[64,8,1152]{2,1,0:T(8,128)(2,1)}), bf16[64,8,1152]{2,1,0:T(8,128)(2,1)S(1)}, u32[]{:S(2)}, u32[]{:S(2)}) %all-to-all-start) | async-done | bytes 1179680 | tf_op jit(solution)/shard_map/all_to_all | solution.py:486
  82.3 0.8 shard_map.87
  (1 shorter events, 0.0 us)
Async XLA Ops:
  0.6 30.3 %collective-permute-start.5 = (bf16[768,1024]{1,0:T(8,128)(2,1)}, bf16[768,1024]{1,0:T(8,128)(2,1)S(1)}, u32[]{:S(2)}, u32[]{:S(2)}) collective-permute-start(bf16[768,1024]{1,0:T(8,128)(2,1)} %x_ref.1), channel_id=1, source_target_pairs={{0,127},{1,2},{2,1},{3,4},{4,3},{5,6},{6,5},{7,8},{8,7},{9,10},{10... | collective-permute-start | bytes 4718600 | tf_op jit(solution)/shard_map/ppermute | solution.py:447
  8.9 1.4 %collective-permute-start = (s32[6,128]{1,0:T(8,128)}, s32[6,128]{1,0:T(8,128)S(1)}, u32[]{:S(2)}, u32[]{:S(2)}) collective-permute-start(s32[6,128]{1,0:T(8,128)} %bitcast.3), channel_id=1, source_target_pairs={{0,1},{1,0},{2,3},{3,2},{4,5},{5,4},{6,7},{7,6},{8,9},{9,8},{10,11... | collective-permute-start | bytes 9224 | tf_op jit(solution)/shard_map/ppermute | solution.py:447
  10.3 0.7 copy-start.3
  16.7 7.6 %collective-permute-start.4 = (bf16[512,1024]{1,0:T(8,128)(2,1)S(1)}, bf16[512,1024]{1,0:T(8,128)(2,1)S(1)}, u32[]{:S(2)}, u32[]{:S(2)}) collective-permute-start(bf16[512,1024]{1,0:T(8,128)(2,1)S(1)} %get-tuple-element.30.second_ref), channel_id=1, source_target_pairs={{0,1},{1,0},{2,3},{3,2},{4,5},{5,4},{6,7},{7,6},{8,9},{9,8},{10,11... | collective-permute-start | bytes 3145736 | tf_op jit(solution)/shard_map/ppermute | solution.py:447
  17.0 7.3 %collective-permute-start.3 = (bf16[272,1024]{1,0:T(8,128)(2,1)S(1)}, bf16[272,1024]{1,0:T(8,128)(2,1)S(1)}, u32[]{:S(2)}, u32[]{:S(2)}) collective-permute-start(bf16[272,1024]{1,0:T(8,128)(2,1)S(1)} %get-tuple-element.29.first_ref), channel_id=1, source_target_pairs={{0,1},{1,0},{2,3},{3,2},{4,5},{5,4},{6,7},{7,6},{8,9},{9,8},{10,11... | collective-permute-start | bytes 1671176 | tf_op jit(solution)/shard_map/ppermute | solution.py:447
  18.6 3.8 %copy-start.2 = (bf16[768,1024]{1,0:T(8,128)(2,1)S(1)}, bf16[768,1024]{1,0:T(8,128)(2,1)}, u32[]{:S(2)}) copy-start(bf16[768,1024]{1,0:T(8,128)(2,1)} %x_ref.1) | copy-start | bytes 4718596
  22.1 15.0 %collective-permute-start.1 = (bf16[272,1024]{1,0:T(8,128)(2,1)S(1)}, bf16[272,1024]{1,0:T(8,128)(2,1)S(1)}, u32[]{:S(2)}, u32[]{:S(2)}) collective-permute-start(bf16[272,1024]{1,0:T(8,128)(2,1)S(1)} %get-tuple-element.32.first_ref), channel_id=1, source_target_pairs={{0,2},{1,127},{2,4},{3,1},{4,6},{5,3},{6,8},{7,5},{8,10},{9,7},{10... | collective-permute-start | bytes 1671176 | tf_op jit(solution)/shard_map/ppermute | solution.py:447
  22.1 26.2 %collective-permute-start.2 = (bf16[512,1024]{1,0:T(8,128)(2,1)S(1)}, bf16[512,1024]{1,0:T(8,128)(2,1)S(1)}, u32[]{:S(2)}, u32[]{:S(2)}) collective-permute-start(bf16[512,1024]{1,0:T(8,128)(2,1)S(1)} %get-tuple-element.33.second_ref), channel_id=1, source_target_pairs={{0,2},{1,127},{2,4},{3,1},{4,6},{5,3},{6,8},{7,5},{8,10},{9,7},{10... | collective-permute-start | bytes 3145736 | tf_op jit(solution)/shard_map/ppermute | solution.py:447
  24.3 6.6 %copy-start = (bf16[1024,1024]{1,0:T(8,128)(2,1)S(1)}, bf16[1024,1024]{1,0:T(8,128)(2,1)}, u32[]{:S(2)}) copy-start(bf16[1024,1024]{1,0:T(8,128)(2,1)} %w_ref.3) | copy-start | bytes 6291460
  32.9 9.2 %collective-permute-start.7 = (bf16[256,1024]{1,0:T(8,128)(2,1)S(1)}, bf16[256,1024]{1,0:T(8,128)(2,1)S(1)}, u32[]{:S(2)}, u32[]{:S(2)}) collective-permute-start(bf16[256,1024]{1,0:T(8,128)(2,1)S(1)} %get-tuple-element.41.rest_0_), channel_id=1, source_target_pairs={{0,1},{1,0},{2,3},{3,2},{4,5},{5,4},{6,7},{7,6},{8,9},{9,8},{10,11... | collective-permute-start | bytes 1572872 | tf_op jit(solution)/shard_map/ppermute | solution.py:447
  33.0 9.1 %collective-permute-start.8 = (bf16[256,1024]{1,0:T(8,128)(2,1)S(1)}, bf16[256,1024]{1,0:T(8,128)(2,1)S(1)}, u32[]{:S(2)}, u32[]{:S(2)}) collective-permute-start(bf16[256,1024]{1,0:T(8,128)(2,1)S(1)} %get-tuple-element.42.rest_1_), channel_id=1, source_target_pairs={{0,1},{1,0},{2,3},{3,2},{4,5},{5,4},{6,7},{7,6},{8,9},{9,8},{10,11... | collective-permute-start | bytes 1572872 | tf_op jit(solution)/shard_map/ppermute | solution.py:447
  33.5 8.6 %collective-permute-start.9 = (bf16[256,1024]{1,0:T(8,128)(2,1)S(1)}, bf16[256,1024]{1,0:T(8,128)(2,1)S(1)}, u32[]{:S(2)}, u32[]{:S(2)}) collective-permute-start(bf16[256,1024]{1,0:T(8,128)(2,1)S(1)} %get-tuple-element.43.rest_2_), channel_id=1, source_target_pairs={{0,1},{1,0},{2,3},{3,2},{4,5},{5,4},{6,7},{7,6},{8,9},{9,8},{10,11... | collective-permute-start | bytes 1572872 | tf_op jit(solution)/shard_map/ppermute | solution.py:447
  38.5 3.6 %collective-permute-start.6 = (bf16[16,1024]{1,0:T(8,128)(2,1)S(1)}, bf16[16,1024]{1,0:T(8,128)(2,1)S(1)}, u32[]{:S(2)}, u32[]{:S(2)}) collective-permute-start(bf16[16,1024]{1,0:T(8,128)(2,1)S(1)} %get-tuple-element.46), channel_id=1, source_target_pairs={{0,1},{1,0},{2,3},{3,2},{4,5},{5,4},{6,7},{7,6},{8,9},{9,8},{10,11... | collective-permute-start | bytes 98312 | tf_op jit(solution)/shard_map/ppermute | solution.py:447
  42.1 6.2 %copy-start.4 = (f32[768,1024]{1,0:T(8,128)S(1)}, f32[768,1024]{1,0:T(8,128)}, u32[]{:S(2)}) copy-start(f32[768,1024]{1,0:T(8,128)} %get-tuple-element.48.unit_ref) | copy-start | bytes 9437188
  51.8 2.7 %collective-permute-start.10 = (bf16[512,1024]{1,0:T(8,128)(2,1)S(1)}, bf16[512,1024]{1,0:T(8,128)(2,1)S(1)}, u32[]{:S(2)}, u32[]{:S(2)}) collective-permute-start(bf16[512,1024]{1,0:T(8,128)(2,1)S(1)} %get-tuple-element.51), channel_id=1, source_target_pairs={{0,1},{1,0},{2,3},{3,2},{4,5},{5,4},{6,7},{7,6},{8,9},{9,8},{10,11... | collective-permute-start | bytes 3145736 | tf_op jit(solution)/shard_map/ppermute | solution.py:447
  51.9 2.7 %collective-permute-start.11 = (f32[8,128]{1,0:T(8,128)S(1)}, f32[8,128]{1,0:T(8,128)S(1)}, u32[]{:S(2)}, u32[]{:S(2)}) collective-permute-start(f32[8,128]{1,0:T(8,128)S(1)} %get-tuple-element.52.loss_ref), channel_id=1, source_target_pairs={{0,1},{1,0},{2,3},{3,2},{4,5},{5,4},{6,7},{7,6},{8,9},{9,8},{10,11... | collective-permute-start | bytes 12296 | tf_op jit(solution)/shard_map/ppermute | solution.py:447
  55.8 26.5 %all-to-all-start = ((bf16[64,8,1152]{2,1,0:T(8,128)(2,1)}), bf16[64,8,1152]{2,1,0:T(8,128)(2,1)S(1)}, u32[]{:S(2)}, u32[]{:S(2)}) async-start(bf16[64,8,1152]{2,1,0:T(8,128)(2,1)} %bitcast.1), calls=%async_computation | async-start | bytes 2359296 | tf_op jit(solution)/shard_map/all_to_all | solution.py:486
  61.5 1.6 %copy-start.1 = (bf16[1024,1024]{1,0:T(8,128)(2,1)S(1)}, bf16[1024,1024]{1,0:T(8,128)(2,1)}, u32[]{:S(2)}) copy-start(bf16[1024,1024]{1,0:T(8,128)(2,1)} %w_ref.3) | copy-start | bytes 6291460

commit v6 on v5

--- a/solution.py
+++ b/solution.py
@@ -396,8 +396,7 @@
     )(dproj, w)
 
 
-def packed_kernel(kept_ref, received_ref, loss_ref, other_loss_ref, out_ref):
-    out_ref[:, :DIM] = (kept_ref[...] + received_ref[...].astype(jnp.float32)).astype(jnp.bfloat16)
+def packed_kernel(kept_ref, received_ref, loss_ref, other_loss_ref, out_hbm, held, sems):
     lanes = jnp.sum(loss_ref[...] + other_loss_ref[...], axis=0, keepdims=True)
     high = lanes.astype(jnp.bfloat16).astype(jnp.float32)
     middle = (lanes - high).astype(jnp.bfloat16).astype(jnp.float32)
@@ -406,16 +405,31 @@
     tile = jnp.where(
         place == 0, high, jnp.where(place == 1, middle, jnp.where(place == 2, low, 0.0))
     ).astype(jnp.bfloat16)
-    for start in range(0, out_ref.shape[0], 16):
-        out_ref[start : start + 16, DIM:] = tile
+    copies = []
+    for number, start in enumerate(range(0, DIM // 2, LANES)):
+        rows = pl.ds(start, LANES)
+        summed = kept_ref[rows, :] + received_ref[rows, :].astype(jnp.float32)
+        held[rows, :DIM] = summed.astype(jnp.bfloat16)
+        for at in range(start, start + LANES, 16):
+            held[at : at + 16, DIM:] = tile
+        copies.append(
+            pltpu.make_async_copy(held.at[rows], out_hbm.at[rows], sems.at[number])
+        )
+        copies[-1].start()
+    for copy in copies:
+        copy.wait()
 
 
 def packed(kept, received, loss, other_loss):
     return pl.pallas_call(
         packed_kernel,
         in_specs=[VMEM] * 4,
-        out_specs=VMEM,
+        out_specs=HBM,
         out_shape=shape(DIM // 2, DIM + LANES, jnp.bfloat16),
+        scratch_shapes=[
+            pltpu.VMEM((DIM // 2, DIM + LANES), jnp.bfloat16),
+            pltpu.SemaphoreType.DMA((DIM // 2 // LANES,)),
+        ],
         compiler_params=params(12),
         cost_estimate=cost(DIM * DIM, 5 * MIB),
     )(kept, received, loss, other_loss)

time: 83.4 us -> 83.3 us (level)
  no operation moved by 1% of the time
where the time goes in v6:
time: 83.3 us; the launch traced here: 83 us
  Pallas kernels  33.6 us (40%)
  waiting for transfers between devices  28.6 us (34%)
  starting transfers between devices  16.4 us (20%)
  local copies, waits for them, and re-layouts  2.29 us (3%)
  between operations  2.16 us (3%)
    all_to_all x1, waiting for transfers between devices, on_device(): lax.all_to_all(parts, 'batch', 0, 0, tiled=True, axis_index_groups=groups)  16.3 us
    ppermute x12, waiting for transfers between devices, move(): lax.ppermute(value, 'batch', [(i, target(i) % count) for i in range(count)])  12.2 us
    pallas_call x4, Pallas kernels, partner_tile(): pl.pallas_call(functools.partial(partner_tile_kernel, weight, other, len(...  11.2 us
    ppermute x12, starting transfers between devices, move(): lax.ppermute(value, 'batch', [(i, target(i) % count) for i in range(count)])  10.8 us
    pallas_call x1, Pallas kernels, project(): pl.pallas_call(project_kernel, in_specs=[HBM] * 4, out_specs=[VMEM] * 4,...  5.75 us
    all_to_all x1, starting transfers between devices, on_device(): lax.all_to_all(parts, 'batch', 0, 0, tiled=True, axis_index_groups=groups)  5.62 us
    pallas_call x1, Pallas kernels, last(): pl.pallas_call(last_kernel, in_specs=[VMEM] * 10, out_specs=[VMEM] * 2, o...  3.46 us
    pallas_call x1, Pallas kernels, own_tile(): pl.pallas_call(own_tile_kernel, in_specs=[SCALARS] * 2 + [VMEM] * 2, out_...  3.41 us
  transfers between devices with their start and end apart: 13, of which 6 were waited for; matrix products, arithmetic and copies ran while one was open for 0% of the time, Pallas kernels for 34%

profile of v6, /device:TPU:0, one launch (start us, length us, event | category | flops | bytes accessed | tf_op | source)
XLA Modules:
  0.0 83.0 jit_solution(5349233055483626358)
XLA Ops:
  0.6 8.3 %collective-permute-start.5 = (bf16[768,1024]{1,0:T(8,128)(2,1)}, bf16[768,1024]{1,0:T(8,128)(2,1)S(1)}, u32[]{:S(2)}, u32[]{:S(2)}) collective-permute-start(bf16[768,1024]{1,0:T(8,128)(2,1)} %x_ref.1), channel_id=1, source_target_pairs={{0,127},{1,2},{2,1},{3,4},{4,3},{5,6},{6,5},{7,8},{8,7},{9,10},{10... | collective-permute-start | bytes 4718600 | tf_op jit(solution)/shard_map/ppermute | solution.py:461
  8.9 0.0 collective-permute-start
  8.9 1.4 %collective-permute-done.other_hbm = s32[6,128]{1,0:T(8,128)S(1)} collective-permute-done((s32[6,128]{1,0:T(8,128)}, s32[6,128]{1,0:T(8,128)S(1)}, u32[]{:S(2)}, u32[]{:S(2)}) %collective-permute-start) | collective-permute-done | bytes 3104 | tf_op jit(solution)/shard_map/ppermute | solution.py:461
  10.3 0.7 copy-done.3
  11.0 5.7 %shard_map.76 = (bf16[272,1024]{1,0:T(8,128)(2,1)S(1)}, bf16[512,1024]{1,0:T(8,128)(2,1)S(1)}, f32[768,1024]{1,0:T(8,128)}, f32[768,128]{1,0:T(8,128)S(1)}) custom-call(bf16[768,1024]{1,0:T(8,128)(2,1)} %x_ref.1, bf16[1024,1024]{1,0:T(8,128)(2,1)} %w_ref.3, s32[6,128]{1,0:T(8,128)S(1)} %bitcast.4, s32[6,128]{1,0:T(8,128)S(1)} %collective-permute-done.other_hbm), custom_call_target="tpu_custom_call" | custom-call | flops 1610612736 | bytes 5242880 | tf_op jit(solution)/shard_map/pallas_call | solution.py:111
  16.7 0.3 collective-permute-start.4
  17.0 0.3 collective-permute-start.3
  18.6 0.0 copy-start.2
  18.6 3.4 %shard_map.77 = (f32[8,128]{1,0:T(8,128)S(1)}, f32[768,128]{1,0:T(8,128)S(1)}, f32[768,1024]{1,0:T(8,128)S(1)}, f32[8,128]{1,0:T(8,128)S(1)}, bf16[272,1024]{1,0...) custom-call(f32[1]{0:T(128)S(6)} %copy.8.scale_ref, f32[1]{0:T(128)S(6)} %copy.9.shift_ref, ...), custom_call_target="tpu_custom_call" | custom-call | flops 2415919104 | bytes 5242880 | tf_op jit(solution)/shard_map/pallas_call | solution.py:230
  22.1 0.1 collective-permute-start.1
  22.1 0.3 collective-permute-start.2
  22.4 0.0 copy-done.2
  22.4 1.9 %shard_map.78.rest_2_.x_ref = bf16[768,1024]{1,0:T(8,128)(2,1)S(1)} custom-call(bf16[768,1024]{1,0:T(8,128)(2,1)S(1)} %copy-done.2, f32[8,128]{1,0:T(8,128)S(1)} %get-tuple-element.36.after.loss_in), custom_call_target="tpu_custom_call" | custom-call | flops 1610612736 | bytes 4194304 | tf_op jit(solution)/shard_map/pallas_call | solution.py:309
  24.3 0.0 collective-permute-done.3.labels.rest_0_
  24.3 0.0 collective-permute-done.4.rest_1_
  24.3 0.0 copy-start
  24.3 3.2 %shard_map.79 = (f32[768,1024]{1,0:T(8,128)S(1)}, f32[8,128]{1,0:T(8,128)S(1)}) custom-call(f32[8,128]{1,0:T(8,128)S(1)} %get-tuple-element.31.scalars, bf16[272,1024]{1,0:T(8,128)(2,1)S(1)} %get-tuple-element.32.first_ref, bf16[512,1024]{1,0:T(8,128)(2,1)S(1)} %get-tuple-element.33.second_ref, f32[768,128]{1,0:T(8,128)S(1)} %get-tuple-element.34.ids, ...), custom_call_target="tpu_custom_call" | custom-call | flops 2415919104 | bytes 10485760 | tf_op jit(solution)/shard_map/pallas_call | solution.py:266
  27.6 3.3 %collective-permute-done.5.x_ref = bf16[768,1024]{1,0:T(8,128)(2,1)S(1)} collective-permute-done((bf16[768,1024]{1,0:T(8,128)(2,1)}, bf16[768,1024]{1,0:T(8,128)(2,1)S(1)}, u32[]{:S(2)}, u32[]{:S(2)}) %collective-permute-start.5) | collective-permute-done | bytes 1572896 | tf_op jit(solution)/shard_map/ppermute | solution.py:461
  30.9 0.0 copy-done
  30.9 1.9 %shard_map.81 = (bf16[256,1024]{1,0:T(8,128)(2,1)S(1)}, bf16[256,1024]{1,0:T(8,128)(2,1)S(1)}, bf16[256,1024]{1,0:T(8,128)(2,1)S(1)}) custom-call(bf16[768,1024]{1,0:T(8,128)(2,1)S(1)} %collective-permute-done.5.x_ref, bf16[1024,1024]{1,0:T(8,128)(2,1)S(1)} %copy-done, f32[8,128]{1,0:T(8,128)S(1)} %get-tuple-element.38.loss_in.after), custom_call_target="tpu_custom_call" | custom-call | flops 1610612736 | bytes 5242880 | tf_op jit(solution)/shard_map/pallas_call | solution.py:284
  32.9 0.1 collective-permute-start.7
  33.0 0.5 collective-permute-start.8
  33.5 0.1 collective-permute-start.9
  33.5 3.5 %collective-permute-done.1.labels.rest_0_.far_first = bf16[272,1024]{1,0:T(8,128)(2,1)S(1)} collective-permute-done((bf16[272,1024]{1,0:T(8,128)(2,1)S(1)}, bf16[272,1024]{1,0:T(8,128)(2,1)S(1)}, u32[]{:S(2)}, u32[]{:S(2)}) %collective-permute-start.1) | collective-permute-done | bytes 557088 | tf_op jit(solution)/shard_map/ppermute | solution.py:461
  37.1 1.4 %shard_map.80 = (f32[768,1024]{1,0:T(8,128)S(1)}, f32[8,128]{1,0:T(8,128)S(1)}, bf16[16,1024]{1,0:T(8,128)(2,1)S(1)}) custom-call(f32[8,128]{1,0:T(8,128)S(1)} %get-tuple-element.31.scalars, bf16[272,1024]{1,0:T(8,128)(2,1)S(1)} %get-tuple-element.32.first_ref, bf16[512,1024]{1,0:T(8,128)(2,1)S(1)} %get-tuple-element.33.second_ref, ...), custom_call_target="tpu_custom_call" | custom-call | flops 805306368 | bytes 10485760 | tf_op jit(solution)/shard_map/pallas_call | solution.py:266
  38.5 0.3 collective-permute-start.6
  38.8 3.3 %shard_map.82 = (f32[768,1024]{1,0:T(8,128)S(1)}, f32[8,128]{1,0:T(8,128)S(1)}) custom-call(f32[8,128]{1,0:T(8,128)S(1)} %get-tuple-element.31.scalars, bf16[272,1024]{1,0:T(8,128)(2,1)S(1)} %get-tuple-element.32.first_ref, bf16[512,1024]{1,0:T(8,128)(2,1)S(1)} %get-tuple-element.33.second_ref, f32[768,128]{1,0:T(8,128)S(1)} %get-tuple-element.34.ids, ...), custom_call_target="tpu_custom_call" | custom-call | flops 2415919104 | bytes 10485760 | tf_op jit(solution)/shard_map/pallas_call | solution.py:266
  42.1 0.0 collective-permute-done.6.labels
  42.1 0.0 collective-permute-done.7.rest_0_
  42.1 0.0 collective-permute-done.8.rest_1_
  42.1 0.0 collective-permute-done.9.rest_2_
  42.1 0.0 copy-start.4
  42.1 3.3 %shard_map.83 = (f32[768,1024]{1,0:T(8,128)S(1)}, f32[8,128]{1,0:T(8,128)S(1)}) custom-call(f32[8,128]{1,0:T(8,128)S(1)} %get-tuple-element.31.scalars, bf16[272,1024]{1,0:T(8,128)(2,1)S(1)} %get-tuple-element.32.first_ref, bf16[512,1024]{1,0:T(8,128)(2,1)S(1)} %get-tuple-element.33.second_ref, f32[768,128]{1,0:T(8,128)S(1)} %get-tuple-element.34.ids, ...), custom_call_target="tpu_custom_call" | custom-call | flops 2415919104 | bytes 10485760 | tf_op jit(solution)/shard_map/pallas_call | solution.py:266
  45.4 2.9 %collective-permute-done.2.far_ref = bf16[512,1024]{1,0:T(8,128)(2,1)S(1)} collective-permute-done((bf16[512,1024]{1,0:T(8,128)(2,1)S(1)}, bf16[512,1024]{1,0:T(8,128)(2,1)S(1)}, u32[]{:S(2)}, u32[]{:S(2)}) %collective-permute-start.2) | collective-permute-done | bytes 1048608 | tf_op jit(solution)/shard_map/ppermute | solution.py:461
  48.3 0.0 copy-done.4
  48.3 3.5 %shard_map.84 = (bf16[768,1024]{1,0:T(8,128)(2,1)S(1)}, bf16[512,1024]{1,0:T(8,128)(2,1)S(1)}) custom-call(f32[8,128]{1,0:T(8,128)S(1)} %get-tuple-element.31.scalars, bf16[272,1024]{1,0:T(8,128)(2,1)S(1)} %get-tuple-element.32.first_ref, bf16[512,1024]{1,0:T(8,128)(2,1)S(1)} %get-tuple-element.33.second_ref, ...), custom_call_target="tpu_custom_call" | custom-call | flops 3221225472 | bytes 14680064 | tf_op jit(solution)/shard_map/pallas_call | solution.py:370
  51.8 0.1 collective-permute-start.10
  51.9 0.5 collective-permute-start.11
  52.4 1.0 %shard_map.85.kept_ref = f32[512,1024]{1,0:T(8,128)S(1)} custom-call(bf16[768,1024]{1,0:T(8,128)(2,1)S(1)} %get-tuple-element.50.dproj_ref, bf16[768,1024]{1,0:T(8,128)(2,1)S(1)} %shard_map.78.rest_2_.x_ref), custom_call_target="tpu_custom_call" | custom-call | flops 805306368 | bytes 5242880 | tf_op jit(solution)/shard_map/pallas_call | solution.py:359
  53.4 1.1 %collective-permute-done.11.other_loss_ref = f32[8,128]{1,0:T(8,128)S(1)} collective-permute-done((f32[8,128]{1,0:T(8,128)S(1)}, f32[8,128]{1,0:T(8,128)S(1)}, u32[]{:S(2)}, u32[]{:S(2)}) %collective-permute-start.11) | collective-permute-done | bytes 4128 | tf_op jit(solution)/shard_map/ppermute | solution.py:461
  54.5 0.0 collective-permute-done.10.received_ref
  54.5 1.2 %shard_map.86 = bf16[512,1152]{1,0:T(8,128)(2,1)} custom-call(f32[512,1024]{1,0:T(8,128)S(1)} %shard_map.85.kept_ref, bf16[512,1024]{1,0:T(8,128)(2,1)S(1)} %collective-permute-done.10.received_ref, f32[8,128]{1,0:T(8,128)S(1)} %get-tuple-element.52.loss_ref, f32[8,128]{1,0:T(8,128)S(1)} %collective-permute-done.11.other_loss_ref), custom_call_target="tpu_custom_call" | custom-call | flops 1048576 | bytes 5242880 | tf_op jit(solution)/shard_map/pallas_call | solution.py:424
  55.7 5.6 %all-to-all-start = ((bf16[64,8,1152]{2,1,0:T(8,128)(2,1)}), bf16[64,8,1152]{2,1,0:T(8,128)(2,1)S(1)}, u32[]{:S(2)}, u32[]{:S(2)}) async-start(bf16[64,8,1152]{2,1,0:T(8,128)(2,1)} %bitcast.1), calls=%async_computation | async-start | bytes 2359296 | tf_op jit(solution)/shard_map/all_to_all | solution.py:500
  61.3 0.0 copy-start.1
  61.4 1.6 %copy-done.1 = bf16[1024,1024]{1,0:T(8,128)(2,1)S(1)} copy-done((bf16[1024,1024]{1,0:T(8,128)(2,1)S(1)}, bf16[1024,1024]{1,0:T(8,128)(2,1)}, u32[]{:S(2)}) %copy-start.1) | copy-done | bytes 2097176
  62.9 3.0 %shard_map.88 = bf16[768,1024]{1,0:T(8,128)(2,1)} custom-call(bf16[768,1024]{1,0:T(8,128)(2,1)S(1)} %get-tuple-element.50.dproj_ref, bf16[1024,1024]{1,0:T(8,128)(2,1)S(1)} %copy-done.1), custom_call_target="tpu_custom_call" | custom-call | flops 1610612736 | bytes 5242880 | tf_op jit(solution)/shard_map/pallas_call | solution.py:389
  65.9 16.3 %all-to-all-done.parts_ref = bf16[64,8,1152]{2,1,0:T(8,128)(2,1)S(1)} async-done(((bf16[64,8,1152]{2,1,0:T(8,128)(2,1)}), bf16[64,8,1152]{2,1,0:T(8,128)(2,1)S(1)}, u32[]{:S(2)}, u32[]{:S(2)}) %all-to-all-start) | async-done | bytes 1179680 | tf_op jit(solution)/shard_map/all_to_all | solution.py:500
  82.2 0.8 shard_map.87
  (1 shorter events, 0.0 us)
Async XLA Ops:
  0.6 30.3 %collective-permute-start.5 = (bf16[768,1024]{1,0:T(8,128)(2,1)}, bf16[768,1024]{1,0:T(8,128)(2,1)S(1)}, u32[]{:S(2)}, u32[]{:S(2)}) collective-permute-start(bf16[768,1024]{1,0:T(8,128)(2,1)} %x_ref.1), channel_id=1, source_target_pairs={{0,127},{1,2},{2,1},{3,4},{4,3},{5,6},{6,5},{7,8},{8,7},{9,10},{10... | collective-permute-start | bytes 4718600 | tf_op jit(solution)/shard_map/ppermute | solution.py:461
  8.9 1.4 %collective-permute-start = (s32[6,128]{1,0:T(8,128)}, s32[6,128]{1,0:T(8,128)S(1)}, u32[]{:S(2)}, u32[]{:S(2)}) collective-permute-start(s32[6,128]{1,0:T(8,128)} %bitcast.3), channel_id=1, source_target_pairs={{0,1},{1,0},{2,3},{3,2},{4,5},{5,4},{6,7},{7,6},{8,9},{9,8},{10,11... | collective-permute-start | bytes 9224 | tf_op jit(solution)/shard_map/ppermute | solution.py:461
  10.3 0.7 copy-start.3
  16.7 7.6 %collective-permute-start.4 = (bf16[512,1024]{1,0:T(8,128)(2,1)S(1)}, bf16[512,1024]{1,0:T(8,128)(2,1)S(1)}, u32[]{:S(2)}, u32[]{:S(2)}) collective-permute-start(bf16[512,1024]{1,0:T(8,128)(2,1)S(1)} %get-tuple-element.30.second_ref), channel_id=1, source_target_pairs={{0,1},{1,0},{2,3},{3,2},{4,5},{5,4},{6,7},{7,6},{8,9},{9,8},{10,11... | collective-permute-start | bytes 3145736 | tf_op jit(solution)/shard_map/ppermute | solution.py:461
  17.0 7.3 %collective-permute-start.3 = (bf16[272,1024]{1,0:T(8,128)(2,1)S(1)}, bf16[272,1024]{1,0:T(8,128)(2,1)S(1)}, u32[]{:S(2)}, u32[]{:S(2)}) collective-permute-start(bf16[272,1024]{1,0:T(8,128)(2,1)S(1)} %get-tuple-element.29.first_ref), channel_id=1, source_target_pairs={{0,1},{1,0},{2,3},{3,2},{4,5},{5,4},{6,7},{7,6},{8,9},{9,8},{10,11... | collective-permute-start | bytes 1671176 | tf_op jit(solution)/shard_map/ppermute | solution.py:461
  18.6 3.8 %copy-start.2 = (bf16[768,1024]{1,0:T(8,128)(2,1)S(1)}, bf16[768,1024]{1,0:T(8,128)(2,1)}, u32[]{:S(2)}) copy-start(bf16[768,1024]{1,0:T(8,128)(2,1)} %x_ref.1) | copy-start | bytes 4718596
  22.1 15.0 %collective-permute-start.1 = (bf16[272,1024]{1,0:T(8,128)(2,1)S(1)}, bf16[272,1024]{1,0:T(8,128)(2,1)S(1)}, u32[]{:S(2)}, u32[]{:S(2)}) collective-permute-start(bf16[272,1024]{1,0:T(8,128)(2,1)S(1)} %get-tuple-element.32.first_ref), channel_id=1, source_target_pairs={{0,2},{1,127},{2,4},{3,1},{4,6},{5,3},{6,8},{7,5},{8,10},{9,7},{10... | collective-permute-start | bytes 1671176 | tf_op jit(solution)/shard_map/ppermute | solution.py:461
  22.1 26.2 %collective-permute-start.2 = (bf16[512,1024]{1,0:T(8,128)(2,1)S(1)}, bf16[512,1024]{1,0:T(8,128)(2,1)S(1)}, u32[]{:S(2)}, u32[]{:S(2)}) collective-permute-start(bf16[512,1024]{1,0:T(8,128)(2,1)S(1)} %get-tuple-element.33.second_ref), channel_id=1, source_target_pairs={{0,2},{1,127},{2,4},{3,1},{4,6},{5,3},{6,8},{7,5},{8,10},{9,7},{10... | collective-permute-start | bytes 3145736 | tf_op jit(solution)/shard_map/ppermute | solution.py:461
  24.3 6.6 %copy-start = (bf16[1024,1024]{1,0:T(8,128)(2,1)S(1)}, bf16[1024,1024]{1,0:T(8,128)(2,1)}, u32[]{:S(2)}) copy-start(bf16[1024,1024]{1,0:T(8,128)(2,1)} %w_ref.3) | copy-start | bytes 6291460
  32.9 9.2 %collective-permute-start.7 = (bf16[256,1024]{1,0:T(8,128)(2,1)S(1)}, bf16[256,1024]{1,0:T(8,128)(2,1)S(1)}, u32[]{:S(2)}, u32[]{:S(2)}) collective-permute-start(bf16[256,1024]{1,0:T(8,128)(2,1)S(1)} %get-tuple-element.41.rest_0_), channel_id=1, source_target_pairs={{0,1},{1,0},{2,3},{3,2},{4,5},{5,4},{6,7},{7,6},{8,9},{9,8},{10,11... | collective-permute-start | bytes 1572872 | tf_op jit(solution)/shard_map/ppermute | solution.py:461
  33.0 9.1 %collective-permute-start.8 = (bf16[256,1024]{1,0:T(8,128)(2,1)S(1)}, bf16[256,1024]{1,0:T(8,128)(2,1)S(1)}, u32[]{:S(2)}, u32[]{:S(2)}) collective-permute-start(bf16[256,1024]{1,0:T(8,128)(2,1)S(1)} %get-tuple-element.42.rest_1_), channel_id=1, source_target_pairs={{0,1},{1,0},{2,3},{3,2},{4,5},{5,4},{6,7},{7,6},{8,9},{9,8},{10,11... | collective-permute-start | bytes 1572872 | tf_op jit(solution)/shard_map/ppermute | solution.py:461
  33.5 8.6 %collective-permute-start.9 = (bf16[256,1024]{1,0:T(8,128)(2,1)S(1)}, bf16[256,1024]{1,0:T(8,128)(2,1)S(1)}, u32[]{:S(2)}, u32[]{:S(2)}) collective-permute-start(bf16[256,1024]{1,0:T(8,128)(2,1)S(1)} %get-tuple-element.43.rest_2_), channel_id=1, source_target_pairs={{0,1},{1,0},{2,3},{3,2},{4,5},{5,4},{6,7},{7,6},{8,9},{9,8},{10,11... | collective-permute-start | bytes 1572872 | tf_op jit(solution)/shard_map/ppermute | solution.py:461
  38.5 3.6 %collective-permute-start.6 = (bf16[16,1024]{1,0:T(8,128)(2,1)S(1)}, bf16[16,1024]{1,0:T(8,128)(2,1)S(1)}, u32[]{:S(2)}, u32[]{:S(2)}) collective-permute-start(bf16[16,1024]{1,0:T(8,128)(2,1)S(1)} %get-tuple-element.46), channel_id=1, source_target_pairs={{0,1},{1,0},{2,3},{3,2},{4,5},{5,4},{6,7},{7,6},{8,9},{9,8},{10,11... | collective-permute-start | bytes 98312 | tf_op jit(solution)/shard_map/ppermute | solution.py:461
  42.1 6.2 %copy-start.4 = (f32[768,1024]{1,0:T(8,128)S(1)}, f32[768,1024]{1,0:T(8,128)}, u32[]{:S(2)}) copy-start(f32[768,1024]{1,0:T(8,128)} %get-tuple-element.48.unit_ref) | copy-start | bytes 9437188
  51.8 2.7 %collective-permute-start.10 = (bf16[512,1024]{1,0:T(8,128)(2,1)S(1)}, bf16[512,1024]{1,0:T(8,128)(2,1)S(1)}, u32[]{:S(2)}, u32[]{:S(2)}) collective-permute-start(bf16[512,1024]{1,0:T(8,128)(2,1)S(1)} %get-tuple-element.51), channel_id=1, source_target_pairs={{0,1},{1,0},{2,3},{3,2},{4,5},{5,4},{6,7},{7,6},{8,9},{9,8},{10,11... | collective-permute-start | bytes 3145736 | tf_op jit(solution)/shard_map/ppermute | solution.py:461
  51.9 2.7 %collective-permute-start.11 = (f32[8,128]{1,0:T(8,128)S(1)}, f32[8,128]{1,0:T(8,128)S(1)}, u32[]{:S(2)}, u32[]{:S(2)}) collective-permute-start(f32[8,128]{1,0:T(8,128)S(1)} %get-tuple-element.52.loss_ref), channel_id=1, source_target_pairs={{0,1},{1,0},{2,3},{3,2},{4,5},{5,4},{6,7},{7,6},{8,9},{9,8},{10,11... | collective-permute-start | bytes 12296 | tf_op jit(solution)/shard_map/ppermute | solution.py:461
  55.7 26.5 %all-to-all-start = ((bf16[64,8,1152]{2,1,0:T(8,128)(2,1)}), bf16[64,8,1152]{2,1,0:T(8,128)(2,1)S(1)}, u32[]{:S(2)}, u32[]{:S(2)}) async-start(bf16[64,8,1152]{2,1,0:T(8,128)(2,1)} %bitcast.1), calls=%async_computation | async-start | bytes 2359296 | tf_op jit(solution)/shard_map/all_to_all | solution.py:500
  61.3 1.6 %copy-start.1 = (bf16[1024,1024]{1,0:T(8,128)(2,1)S(1)}, bf16[1024,1024]{1,0:T(8,128)(2,1)}, u32[]{:S(2)}) copy-start(bf16[1024,1024]{1,0:T(8,128)(2,1)} %w_ref.3) | copy-start | bytes 6291460

commit v7 on v5

--- a/solution.py
+++ b/solution.py
@@ -75,8 +75,6 @@
     other_hbm,
     first_ref,
     second_ref,
-    unit_ref,
-    inverse_ref,
     x_ref,
     w_ref,
     label_ref,
@@ -100,9 +98,7 @@
         copy.wait()
     first_ref[FIRST:, :] = label_rows(label_ref, other_ref)
     for start in range(0, ROWS, GROUP):
-        unit, inverse = normalised(x_ref[start : start + GROUP, :], w_ref[...])
-        unit_ref[start : start + GROUP, :] = unit
-        inverse_ref[start : start + GROUP, :] = jnp.broadcast_to(inverse, (GROUP, LANES))
+        unit, _ = normalised(x_ref[start : start + GROUP, :], w_ref[...])
         ref, at = (first_ref, start) if start < FIRST else (second_ref, start - FIRST)
         ref[at : at + GROUP, :] = unit.astype(jnp.bfloat16)
 
@@ -111,8 +107,8 @@
     return pl.pallas_call(
         project_kernel,
         in_specs=[HBM] * 4,
-        out_specs=[VMEM] * 4,
-        out_shape=BLOCK_SHAPE + [shape(ROWS, DIM), shape(ROWS, LANES)],
+        out_specs=[VMEM] * 2,
+        out_shape=BLOCK_SHAPE,
         scratch_shapes=[
             pltpu.VMEM((ROWS, DIM), jnp.bfloat16),
             pltpu.VMEM((DIM, DIM), jnp.bfloat16),
@@ -291,7 +287,7 @@
     )(x, w, after)
 
 
-def sorted_columns_kernel(x_ref, after, out_ref):
+def prepared_kernel(x_ref, w_ref, after, out_ref, unit_ref, inverse_ref):
     place = lax.broadcasted_iota(jnp.int32, (DIM, DIM), 1)
     half, chip, row = place // (DIM // 2), place % (DIM // 2) // 8, place % 8
     core = lax.axis_index("batch") % 2
@@ -303,17 +299,20 @@
         out_ref[rows, :] = jnp.dot(
             x_ref[rows, :], chosen, preferred_element_type=jnp.float32
         ).astype(jnp.bfloat16)
-
-
-def sorted_columns(x, after):
-    return pl.pallas_call(
-        sorted_columns_kernel,
-        in_specs=[VMEM, ANY],
-        out_specs=VMEM,
-        out_shape=shape(ROWS, DIM, jnp.bfloat16),
-        compiler_params=params(12),
-        cost_estimate=cost(2 * ROWS * DIM * DIM, 4 * MIB),
-    )(x, after)
+        unit, inverse = normalised(x_ref[rows, :], w_ref[...])
+        unit_ref[rows, :] = unit
+        inverse_ref[rows, :] = jnp.broadcast_to(inverse, (STEP, LANES))
+
+
+def prepared(x, w, after):
+    return pl.pallas_call(
+        prepared_kernel,
+        in_specs=[VMEM] * 2 + [ANY],
+        out_specs=[VMEM] * 3,
+        out_shape=[shape(ROWS, DIM, jnp.bfloat16), shape(ROWS, DIM), shape(ROWS, LANES)],
+        compiler_params=params(12),
+        cost_estimate=cost(4 * ROWS * DIM * DIM, 8 * MIB),
+    )(x, w, after)
 
 
 def last_kernel(
@@ -458,14 +457,14 @@
     labels = label.reshape(ROWS // LANES, LANES)
     near_x = move(x, near)
 
-    *own, unit, inverse = project(x, w, labels, move(labels, pair))
+    own = project(x, w, labels, move(labels, pair))
     paired = [move(part, pair) for part in own]
     scalars, ids, summed, loss, *own = own_tile(score_scale, score_shift, own)
     far_first = move(own[0], far)
     far_second = move(own[1], far)
     tile = functools.partial(partner_tile, scalars=scalars, own=own, ids=ids)
     whole, early = (0, ROWS), (0, FIRST)
-    x_sorted = sorted_columns(x, loss)
+    x_sorted, unit, inverse = prepared(x, w, loss)
     summed, loss = tile(0.5, paired, whole, paired[0], summed, loss, after=(x_sorted,))
     pieces = partner_projection(near_x, w, loss)
     third = [move(piece, pair) for piece in pieces]

time: 83.4 us -> 83.5 us (level)
  waiting for transfers between devices: 28.6 us -> 26.4 us
  starting transfers between devices: 16.4 us -> 18.5 us
    ppermute x12, waiting for transfers between devices: 12.2 us -> 10.1 us  [move(): lax.ppermute(value, 'batch', [(i, target(i) % count) for i in range(count)])]
    all_to_all x1, starting transfers between devices: 5.61 us -> 7.36 us  [on_device(): lax.all_to_all(parts, 'batch', 0, 0, tiled=True, axis_index_groups=groups)]
    unnamed x10 -> x8, local copies, waits for them, and re-layouts: 2.29 us -> 2.29 us
  transfers between devices with their start and end apart: 13 -> 13, of which waited for: 6 -> 5; matrix products, arithmetic and copies ran while one was open for 0% -> 0% of each run, Pallas kernels for 34% -> 34%
where the time goes in v7:
time: 83.5 us; the launch traced here: 83.2 us
  Pallas kernels  33.8 us (40%)
  waiting for transfers between devices  26.4 us (32%)
  starting transfers between devices  18.5 us (22%)
  local copies, waits for them, and re-layouts  2.29 us (3%)
  between operations  2.14 us (3%)
    all_to_all x1, waiting for transfers between devices, on_device(): lax.all_to_all(parts, 'batch', 0, 0, tiled=True, axis_index_groups=groups)  16.3 us
    ppermute x12, starting transfers between devices, move(): lax.ppermute(value, 'batch', [(i, target(i) % count) for i in range(count)])  11.2 us
    pallas_call x4, Pallas kernels, partner_tile(): pl.pallas_call(functools.partial(partner_tile_kernel, weight, other, len(...  11.2 us
    ppermute x12, waiting for transfers between devices, move(): lax.ppermute(value, 'batch', [(i, target(i) % count) for i in range(count)])  10.1 us
    all_to_all x1, starting transfers between devices, on_device(): lax.all_to_all(parts, 'batch', 0, 0, tiled=True, axis_index_groups=groups)  7.36 us
    pallas_call x1, Pallas kernels, project(): pl.pallas_call(project_kernel, in_specs=[HBM] * 4, out_specs=[VMEM] * 2,...  3.97 us
    pallas_call x1, Pallas kernels, prepared(): pl.pallas_call(prepared_kernel, in_specs=[VMEM] * 2 + [ANY], out_specs=[V...  3.71 us
    pallas_call x1, Pallas kernels, last(): pl.pallas_call(last_kernel, in_specs=[VMEM] * 10, out_specs=[VMEM] * 2, o...  3.52 us
  transfers between devices with their start and end apart: 13, of which 5 were waited for; matrix products, arithmetic and copies ran while one was open for 0% of the time, Pallas kernels for 34%

profile of v7, /device:TPU:0, one launch (start us, length us, event | category | flops | bytes accessed | tf_op | source)
XLA Modules:
  0.0 83.2 jit_solution(320219251406790899)
XLA Ops:
  0.6 8.3 %collective-permute-start.5 = (bf16[768,1024]{1,0:T(8,128)(2,1)}, bf16[768,1024]{1,0:T(8,128)(2,1)S(1)}, u32[]{:S(2)}, u32[]{:S(2)}) collective-permute-start(bf16[768,1024]{1,0:T(8,128)(2,1)} %x_ref.1), channel_id=1, source_target_pairs={{0,127},{1,2},{2,1},{3,4},{4,3},{5,6},{6,5},{7,8},{8,7},{9,10},{10... | collective-permute-start | bytes 4718600 | tf_op jit(solution)/shard_map/ppermute | solution.py:446
  8.9 0.0 collective-permute-start
  8.9 1.4 %collective-permute-done.other_hbm = s32[6,128]{1,0:T(8,128)S(1)} collective-permute-done((s32[6,128]{1,0:T(8,128)}, s32[6,128]{1,0:T(8,128)S(1)}, u32[]{:S(2)}, u32[]{:S(2)}) %collective-permute-start) | collective-permute-done | bytes 3104 | tf_op jit(solution)/shard_map/ppermute | solution.py:446
  10.3 0.0 copy-start.3
  10.3 0.7 copy-done.3
  11.0 4.0 %shard_map.76 = (bf16[272,1024]{1,0:T(8,128)(2,1)S(1)}, bf16[512,1024]{1,0:T(8,128)(2,1)S(1)}) custom-call(bf16[768,1024]{1,0:T(8,128)(2,1)} %x_ref.1, bf16[1024,1024]{1,0:T(8,128)(2,1)} %w_ref.5, s32[6,128]{1,0:T(8,128)S(1)} %bitcast.4, s32[6,128]{1,0:T(8,128)S(1)} %collective-permute-done.other_hbm), custom_call_target="tpu_custom_call" | custom-call | flops 1610612736 | bytes 5242880 | tf_op jit(solution)/shard_map/pallas_call | solution.py:107
  15.0 0.2 collective-permute-start.4
  15.2 0.3 collective-permute-start.3
  16.9 0.0 copy-start
  16.9 0.0 copy-start.2
  16.9 3.4 %shard_map.77 = (f32[8,128]{1,0:T(8,128)S(1)}, f32[768,128]{1,0:T(8,128)S(1)}, f32[768,1024]{1,0:T(8,128)S(1)}, f32[8,128]{1,0:T(8,128)S(1)}, bf16[272,1024]{1,0...) custom-call(f32[1]{0:T(128)S(6)} %copy.8.scale_ref, f32[1]{0:T(128)S(6)} %copy.9.shift_ref, ...), custom_call_target="tpu_custom_call" | custom-call | flops 2415919104 | bytes 5242880 | tf_op jit(solution)/shard_map/pallas_call | solution.py:226
  20.3 0.1 collective-permute-start.1
  20.4 0.3 collective-permute-start.2
  20.6 0.0 copy-done
  20.6 0.0 copy-done.2
  20.7 3.7 %shard_map.78 = (bf16[768,1024]{1,0:T(8,128)(2,1)S(1)}, f32[768,1024]{1,0:T(8,128)S(1)}, f32[768,128]{1,0:T(8,128)S(1)}) custom-call(bf16[768,1024]{1,0:T(8,128)(2,1)S(1)} %copy-done.2, bf16[1024,1024]{1,0:T(8,128)(2,1)S(1)} %copy-done, f32[8,128]{1,0:T(8,128)S(1)} %get-tuple-element.37.after.loss_in), custom_call_target="tpu_custom_call" | custom-call | flops 3221225472 | bytes 8388608 | tf_op jit(solution)/shard_map/pallas_call | solution.py:308
  24.4 0.0 collective-permute-done.3.labels.rest_0_
  24.4 0.0 collective-permute-done.4.rest_1_
  24.4 3.3 %shard_map.79 = (f32[768,1024]{1,0:T(8,128)S(1)}, f32[8,128]{1,0:T(8,128)S(1)}) custom-call(f32[8,128]{1,0:T(8,128)S(1)} %get-tuple-element.32.scalars, bf16[272,1024]{1,0:T(8,128)(2,1)S(1)} %get-tuple-element.33.first_ref, bf16[512,1024]{1,0:T(8,128)(2,1)S(1)} %get-tuple-element.34.second_ref, f32[768,128]{1,0:T(8,128)S(1)} %get-tuple-element.35.ids, ...), custom_call_target="tpu_custom_call" | custom-call | flops 2415919104 | bytes 10485760 | tf_op jit(solution)/shard_map/pallas_call | solution.py:262
  27.7 5.0 %collective-permute-done.5.x_ref = bf16[768,1024]{1,0:T(8,128)(2,1)S(1)} collective-permute-done((bf16[768,1024]{1,0:T(8,128)(2,1)}, bf16[768,1024]{1,0:T(8,128)(2,1)S(1)}, u32[]{:S(2)}, u32[]{:S(2)}) %collective-permute-start.5) | collective-permute-done | bytes 1572896 | tf_op jit(solution)/shard_map/ppermute | solution.py:446
  32.7 1.9 %shard_map.81 = (bf16[256,1024]{1,0:T(8,128)(2,1)S(1)}, bf16[256,1024]{1,0:T(8,128)(2,1)S(1)}, bf16[256,1024]{1,0:T(8,128)(2,1)S(1)}) custom-call(bf16[768,1024]{1,0:T(8,128)(2,1)S(1)} %collective-permute-done.5.x_ref, bf16[1024,1024]{1,0:T(8,128)(2,1)S(1)} %copy-done, f32[8,128]{1,0:T(8,128)S(1)} %get-tuple-element.40.loss_in.after), custom_call_target="tpu_custom_call" | custom-call | flops 1610612736 | bytes 5242880 | tf_op jit(solution)/shard_map/pallas_call | solution.py:280
  34.6 0.1 collective-permute-start.7
  34.7 0.5 collective-permute-start.8
  35.2 0.1 collective-permute-start.9
  35.3 0.0 collective-permute-done.1.labels.rest_0_.far_first
  35.3 1.4 %shard_map.80 = (f32[768,1024]{1,0:T(8,128)S(1)}, f32[8,128]{1,0:T(8,128)S(1)}, bf16[16,1024]{1,0:T(8,128)(2,1)S(1)}) custom-call(f32[8,128]{1,0:T(8,128)S(1)} %get-tuple-element.32.scalars, bf16[272,1024]{1,0:T(8,128)(2,1)S(1)} %get-tuple-element.33.first_ref, bf16[512,1024]{1,0:T(8,128)(2,1)S(1)} %get-tuple-element.34.second_ref, ...), custom_call_target="tpu_custom_call" | custom-call | flops 805306368 | bytes 10485760 | tf_op jit(solution)/shard_map/pallas_call | solution.py:262
  36.7 0.7 collective-permute-start.6
  37.4 3.3 %shard_map.82 = (f32[768,1024]{1,0:T(8,128)S(1)}, f32[8,128]{1,0:T(8,128)S(1)}) custom-call(f32[8,128]{1,0:T(8,128)S(1)} %get-tuple-element.32.scalars, bf16[272,1024]{1,0:T(8,128)(2,1)S(1)} %get-tuple-element.33.first_ref, bf16[512,1024]{1,0:T(8,128)(2,1)S(1)} %get-tuple-element.34.second_ref, f32[768,128]{1,0:T(8,128)S(1)} %get-tuple-element.35.ids, ...), custom_call_target="tpu_custom_call" | custom-call | flops 2415919104 | bytes 10485760 | tf_op jit(solution)/shard_map/pallas_call | solution.py:262
  40.7 0.0 collective-permute-done.6.labels
  40.7 0.0 collective-permute-done.7.rest_0_
  40.7 0.0 collective-permute-done.8.rest_1_
  40.7 0.0 collective-permute-done.9.rest_2_
  40.8 3.2 %shard_map.83 = (f32[768,1024]{1,0:T(8,128)S(1)}, f32[8,128]{1,0:T(8,128)S(1)}) custom-call(f32[8,128]{1,0:T(8,128)S(1)} %get-tuple-element.32.scalars, bf16[272,1024]{1,0:T(8,128)(2,1)S(1)} %get-tuple-element.33.first_ref, bf16[512,1024]{1,0:T(8,128)(2,1)S(1)} %get-tuple-element.34.second_ref, f32[768,128]{1,0:T(8,128)S(1)} %get-tuple-element.35.ids, ...), custom_call_target="tpu_custom_call" | custom-call | flops 2415919104 | bytes 10485760 | tf_op jit(solution)/shard_map/pallas_call | solution.py:262
  44.0 2.6 %collective-permute-done.2.far_ref = bf16[512,1024]{1,0:T(8,128)(2,1)S(1)} collective-permute-done((bf16[512,1024]{1,0:T(8,128)(2,1)S(1)}, bf16[512,1024]{1,0:T(8,128)(2,1)S(1)}, u32[]{:S(2)}, u32[]{:S(2)}) %collective-permute-start.2) | collective-permute-done | bytes 1048608 | tf_op jit(solution)/shard_map/ppermute | solution.py:446
  46.6 3.5 %shard_map.84 = (bf16[768,1024]{1,0:T(8,128)(2,1)S(1)}, bf16[512,1024]{1,0:T(8,128)(2,1)S(1)}) custom-call(f32[8,128]{1,0:T(8,128)S(1)} %get-tuple-element.32.scalars, bf16[272,1024]{1,0:T(8,128)(2,1)S(1)} %get-tuple-element.33.first_ref, bf16[512,1024]{1,0:T(8,128)(2,1)S(1)} %get-tuple-element.34.second_ref, ...), custom_call_target="tpu_custom_call" | custom-call | flops 3221225472 | bytes 14680064 | tf_op jit(solution)/shard_map/pallas_call | solution.py:369
  50.1 0.1 collective-permute-start.10
  50.2 0.5 collective-permute-start.11
  50.7 1.0 %shard_map.85.kept_ref = f32[512,1024]{1,0:T(8,128)S(1)} custom-call(bf16[768,1024]{1,0:T(8,128)(2,1)S(1)} %get-tuple-element.52.dproj_ref, bf16[768,1024]{1,0:T(8,128)(2,1)S(1)} %get-tuple-element.38.rest_2_.x_ref), custom_call_target="tpu_custom_call" | custom-call | flops 805306368 | bytes 5242880 | tf_op jit(solution)/shard_map/pallas_call | solution.py:358
  51.7 1.1 %collective-permute-done.11.other_loss_ref = f32[8,128]{1,0:T(8,128)S(1)} collective-permute-done((f32[8,128]{1,0:T(8,128)S(1)}, f32[8,128]{1,0:T(8,128)S(1)}, u32[]{:S(2)}, u32[]{:S(2)}) %collective-permute-start.11) | collective-permute-done | bytes 4128 | tf_op jit(solution)/shard_map/ppermute | solution.py:446
  52.8 0.0 collective-permute-done.10.received_ref
  52.8 1.3 %shard_map.86 = bf16[512,1152]{1,0:T(8,128)(2,1)} custom-call(f32[512,1024]{1,0:T(8,128)S(1)} %shard_map.85.kept_ref, bf16[512,1024]{1,0:T(8,128)(2,1)S(1)} %collective-permute-done.10.received_ref, f32[8,128]{1,0:T(8,128)S(1)} %get-tuple-element.54.loss_ref, f32[8,128]{1,0:T(8,128)S(1)} %collective-permute-done.11.other_loss_ref), custom_call_target="tpu_custom_call" | custom-call | flops 1048576 | bytes 5242880 | tf_op jit(solution)/shard_map/pallas_call | solution.py:413
  54.1 7.4 %all-to-all-start = ((bf16[64,8,1152]{2,1,0:T(8,128)(2,1)}), bf16[64,8,1152]{2,1,0:T(8,128)(2,1)S(1)}, u32[]{:S(2)}, u32[]{:S(2)}) async-start(bf16[64,8,1152]{2,1,0:T(8,128)(2,1)} %bitcast.1), calls=%async_computation | async-start | bytes 2359296 | tf_op jit(solution)/shard_map/all_to_all | solution.py:485
  61.5 0.0 copy-start.1
  61.5 1.6 %copy-done.1 = bf16[1024,1024]{1,0:T(8,128)(2,1)S(1)} copy-done((bf16[1024,1024]{1,0:T(8,128)(2,1)S(1)}, bf16[1024,1024]{1,0:T(8,128)(2,1)}, u32[]{:S(2)}) %copy-start.1) | copy-done | bytes 2097176
  63.1 3.0 %shard_map.88 = bf16[768,1024]{1,0:T(8,128)(2,1)} custom-call(bf16[768,1024]{1,0:T(8,128)(2,1)S(1)} %get-tuple-element.52.dproj_ref, bf16[1024,1024]{1,0:T(8,128)(2,1)S(1)} %copy-done.1), custom_call_target="tpu_custom_call" | custom-call | flops 1610612736 | bytes 5242880 | tf_op jit(solution)/shard_map/pallas_call | solution.py:388
  66.1 16.3 %all-to-all-done.parts_ref = bf16[64,8,1152]{2,1,0:T(8,128)(2,1)S(1)} async-done(((bf16[64,8,1152]{2,1,0:T(8,128)(2,1)}), bf16[64,8,1152]{2,1,0:T(8,128)(2,1)S(1)}, u32[]{:S(2)}, u32[]{:S(2)}) %all-to-all-start) | async-done | bytes 1179680 | tf_op jit(solution)/shard_map/all_to_all | solution.py:485
  82.4 0.8 shard_map.87
Async XLA Ops:
  0.6 32.1 %collective-permute-start.5 = (bf16[768,1024]{1,0:T(8,128)(2,1)}, bf16[768,1024]{1,0:T(8,128)(2,1)S(1)}, u32[]{:S(2)}, u32[]{:S(2)}) collective-permute-start(bf16[768,1024]{1,0:T(8,128)(2,1)} %x_ref.1), channel_id=1, source_target_pairs={{0,127},{1,2},{2,1},{3,4},{4,3},{5,6},{6,5},{7,8},{8,7},{9,10},{10... | collective-permute-start | bytes 4718600 | tf_op jit(solution)/shard_map/ppermute | solution.py:446
  8.9 1.4 %collective-permute-start = (s32[6,128]{1,0:T(8,128)}, s32[6,128]{1,0:T(8,128)S(1)}, u32[]{:S(2)}, u32[]{:S(2)}) collective-permute-start(s32[6,128]{1,0:T(8,128)} %bitcast.3), channel_id=1, source_target_pairs={{0,1},{1,0},{2,3},{3,2},{4,5},{5,4},{6,7},{7,6},{8,9},{9,8},{10,11... | collective-permute-start | bytes 9224 | tf_op jit(solution)/shard_map/ppermute | solution.py:446
  10.3 0.7 copy-start.3
  15.0 9.4 %collective-permute-start.4 = (bf16[512,1024]{1,0:T(8,128)(2,1)S(1)}, bf16[512,1024]{1,0:T(8,128)(2,1)S(1)}, u32[]{:S(2)}, u32[]{:S(2)}) collective-permute-start(bf16[512,1024]{1,0:T(8,128)(2,1)S(1)} %get-tuple-element.31.second_ref), channel_id=1, source_target_pairs={{0,1},{1,0},{2,3},{3,2},{4,5},{5,4},{6,7},{7,6},{8,9},{9,8},{10,11... | collective-permute-start | bytes 3145736 | tf_op jit(solution)/shard_map/ppermute | solution.py:446
  15.2 9.2 %collective-permute-start.3 = (bf16[272,1024]{1,0:T(8,128)(2,1)S(1)}, bf16[272,1024]{1,0:T(8,128)(2,1)S(1)}, u32[]{:S(2)}, u32[]{:S(2)}) collective-permute-start(bf16[272,1024]{1,0:T(8,128)(2,1)S(1)} %get-tuple-element.30.first_ref), channel_id=1, source_target_pairs={{0,1},{1,0},{2,3},{3,2},{4,5},{5,4},{6,7},{7,6},{8,9},{9,8},{10,11... | collective-permute-start | bytes 1671176 | tf_op jit(solution)/shard_map/ppermute | solution.py:446
  16.9 3.8 %copy-start = (bf16[1024,1024]{1,0:T(8,128)(2,1)S(1)}, bf16[1024,1024]{1,0:T(8,128)(2,1)}, u32[]{:S(2)}) copy-start(bf16[1024,1024]{1,0:T(8,128)(2,1)} %w_ref.5) | copy-start | bytes 6291460
  16.9 3.8 %copy-start.2 = (bf16[768,1024]{1,0:T(8,128)(2,1)S(1)}, bf16[768,1024]{1,0:T(8,128)(2,1)}, u32[]{:S(2)}) copy-start(bf16[768,1024]{1,0:T(8,128)(2,1)} %x_ref.1) | copy-start | bytes 4718596
  20.3 15.0 %collective-permute-start.1 = (bf16[272,1024]{1,0:T(8,128)(2,1)S(1)}, bf16[272,1024]{1,0:T(8,128)(2,1)S(1)}, u32[]{:S(2)}, u32[]{:S(2)}) collective-permute-start(bf16[272,1024]{1,0:T(8,128)(2,1)S(1)} %get-tuple-element.33.first_ref), channel_id=1, source_target_pairs={{0,2},{1,127},{2,4},{3,1},{4,6},{5,3},{6,8},{7,5},{8,10},{9,7},{10... | collective-permute-start | bytes 1671176 | tf_op jit(solution)/shard_map/ppermute | solution.py:446
  20.4 26.2 %collective-permute-start.2 = (bf16[512,1024]{1,0:T(8,128)(2,1)S(1)}, bf16[512,1024]{1,0:T(8,128)(2,1)S(1)}, u32[]{:S(2)}, u32[]{:S(2)}) collective-permute-start(bf16[512,1024]{1,0:T(8,128)(2,1)S(1)} %get-tuple-element.34.second_ref), channel_id=1, source_target_pairs={{0,2},{1,127},{2,4},{3,1},{4,6},{5,3},{6,8},{7,5},{8,10},{9,7},{10... | collective-permute-start | bytes 3145736 | tf_op jit(solution)/shard_map/ppermute | solution.py:446
  34.6 6.1 %collective-permute-start.7 = (bf16[256,1024]{1,0:T(8,128)(2,1)S(1)}, bf16[256,1024]{1,0:T(8,128)(2,1)S(1)}, u32[]{:S(2)}, u32[]{:S(2)}) collective-permute-start(bf16[256,1024]{1,0:T(8,128)(2,1)S(1)} %get-tuple-element.43.rest_0_), channel_id=1, source_target_pairs={{0,1},{1,0},{2,3},{3,2},{4,5},{5,4},{6,7},{7,6},{8,9},{9,8},{10,11... | collective-permute-start | bytes 1572872 | tf_op jit(solution)/shard_map/ppermute | solution.py:446
  34.7 6.0 %collective-permute-start.8 = (bf16[256,1024]{1,0:T(8,128)(2,1)S(1)}, bf16[256,1024]{1,0:T(8,128)(2,1)S(1)}, u32[]{:S(2)}, u32[]{:S(2)}) collective-permute-start(bf16[256,1024]{1,0:T(8,128)(2,1)S(1)} %get-tuple-element.44.rest_1_), channel_id=1, source_target_pairs={{0,1},{1,0},{2,3},{3,2},{4,5},{5,4},{6,7},{7,6},{8,9},{9,8},{10,11... | collective-permute-start | bytes 1572872 | tf_op jit(solution)/shard_map/ppermute | solution.py:446
  35.2 5.5 %collective-permute-start.9 = (bf16[256,1024]{1,0:T(8,128)(2,1)S(1)}, bf16[256,1024]{1,0:T(8,128)(2,1)S(1)}, u32[]{:S(2)}, u32[]{:S(2)}) collective-permute-start(bf16[256,1024]{1,0:T(8,128)(2,1)S(1)} %get-tuple-element.45.rest_2_), channel_id=1, source_target_pairs={{0,1},{1,0},{2,3},{3,2},{4,5},{5,4},{6,7},{7,6},{8,9},{9,8},{10,11... | collective-permute-start | bytes 1572872 | tf_op jit(solution)/shard_map/ppermute | solution.py:446
  36.7 4.0 %collective-permute-start.6 = (bf16[16,1024]{1,0:T(8,128)(2,1)S(1)}, bf16[16,1024]{1,0:T(8,128)(2,1)S(1)}, u32[]{:S(2)}, u32[]{:S(2)}) collective-permute-start(bf16[16,1024]{1,0:T(8,128)(2,1)S(1)} %get-tuple-element.48), channel_id=1, source_target_pairs={{0,1},{1,0},{2,3},{3,2},{4,5},{5,4},{6,7},{7,6},{8,9},{9,8},{10,11... | collective-permute-start | bytes 98312 | tf_op jit(solution)/shard_map/ppermute | solution.py:446
  50.1 2.7 %collective-permute-start.10 = (bf16[512,1024]{1,0:T(8,128)(2,1)S(1)}, bf16[512,1024]{1,0:T(8,128)(2,1)S(1)}, u32[]{:S(2)}, u32[]{:S(2)}) collective-permute-start(bf16[512,1024]{1,0:T(8,128)(2,1)S(1)} %get-tuple-element.53), channel_id=1, source_target_pairs={{0,1},{1,0},{2,3},{3,2},{4,5},{5,4},{6,7},{7,6},{8,9},{9,8},{10,11... | collective-permute-start | bytes 3145736 | tf_op jit(solution)/shard_map/ppermute | solution.py:446
  50.2 2.7 %collective-permute-start.11 = (f32[8,128]{1,0:T(8,128)S(1)}, f32[8,128]{1,0:T(8,128)S(1)}, u32[]{:S(2)}, u32[]{:S(2)}) collective-permute-start(f32[8,128]{1,0:T(8,128)S(1)} %get-tuple-element.54.loss_ref), channel_id=1, source_target_pairs={{0,1},{1,0},{2,3},{3,2},{4,5},{5,4},{6,7},{7,6},{8,9},{9,8},{10,11... | collective-permute-start | bytes 12296 | tf_op jit(solution)/shard_map/ppermute | solution.py:446
  54.1 28.3 %all-to-all-start = ((bf16[64,8,1152]{2,1,0:T(8,128)(2,1)}), bf16[64,8,1152]{2,1,0:T(8,128)(2,1)S(1)}, u32[]{:S(2)}, u32[]{:S(2)}) async-start(bf16[64,8,1152]{2,1,0:T(8,128)(2,1)} %bitcast.1), calls=%async_computation | async-start | bytes 2359296 | tf_op jit(solution)/shard_map/all_to_all | solution.py:485
  61.5 1.6 %copy-start.1 = (bf16[1024,1024]{1,0:T(8,128)(2,1)S(1)}, bf16[1024,1024]{1,0:T(8,128)(2,1)}, u32[]{:S(2)}) copy-start(bf16[1024,1024]{1,0:T(8,128)(2,1)} %w_ref.5) | copy-start | bytes 6291460
